TPU v7x, 256 devices: a whole 4x4x8 slice. The times are simulated.
256 devices in a mesh: ab: 64 (over z, y_hi, x), cd: 4 (over y_lo, core).
Axes of the slice: x: 4, y: 4 (y_hi: 2, y_lo: 2; y = y_hi * 2 + y_lo), z: 8, core: 2. Of those that a mesh axis runs over, the one named last changes fastest.
Arguments:
- amplitudes: bfloat16 [6144, 8192], P(('cd', 'ab')), may hold values from -6 to 6
- integrals: bfloat16 [8192, 8192], P('ab', 'cd'), may hold values from -0.1875 to 0.1875
- ab_symmetry: int32 [8192], P('ab'), may hold values from 0 to 7, as said below
- cd_symmetry: int32 [8192], replicated, may hold values from 0 to 7, as said below
- ij_symmetry: int32 [6144], P('cd'), may hold values from 0 to 7, as said below
Outputs:
- ladder: bfloat16 [6144, 8192], P('cd', 'ab')
Inputs may be any that keep to these rules, and one draw needn't show every extreme that they name: `ab_symmetry`: irrep labels of the eight irreps of D2h. `cd_symmetry`: irrep labels of the eight irreps of D2h. `ij_symmetry`: irrep labels of the eight irreps of D2h.
All inputs are finite; a program needn't handle non-finite values.
Results may differ from a plain program's by a relative error of at most 0.001.
Values may be sent and summed in bfloat16 or wider, within the bound.
No kernel may reach another device: no remote copies, remote signals or barrier semaphores. Data moves between devices by JAX's collectives and lax.ppermute only.
A program may use at most 128 MiB of HBM per device.

v0:
```python
import jax
import jax.numpy as jnp
from jax import lax
from jax.sharding import PartitionSpec as P


def local(amplitudes, integrals, ab_symmetry, cd_symmetry, ij_symmetry):
    width = integrals.shape[1]
    own_labels = lax.dynamic_slice_in_dim(cd_symmetry, lax.axis_index("cd") * width, width)
    allowed = ab_symmetry[:, None] == own_labels[None, :]
    masked = jnp.where(allowed, integrals, jnp.zeros_like(integrals))
    blocks = lax.all_to_all(amplitudes[None], "cd", split_axis=2, concat_axis=0, tiled=True)
    partial_rows = jnp.einsum(
        "gkc,ac->gka",
        lax.all_gather(blocks, "ab", axis=1, tiled=True),
        masked,
        preferred_element_type=jnp.float32,
    )
    summed = lax.psum_scatter(partial_rows, "cd", scatter_dimension=0, tiled=True)[0]
    keep = ij_symmetry[:, None] == ab_symmetry[None, :]
    return jnp.where(keep, summed, jnp.zeros_like(summed)).astype(jnp.bfloat16)


def solution(mesh):
    placed = (P(("cd", "ab"), None), P("ab", "cd"), P("ab"), P(), P("cd"))
    return jax.shard_map(
        local, mesh=mesh, in_specs=placed, out_specs=P("cd", "ab"), check_vma=False
    )
```

profile of v0, /device:TPU:24, one launch (start us, length us, event | category | flops | bytes accessed | tf_op | source)
XLA Modules:
  0.0 410.9 jit_solution(7265064380437399833)
XLA Ops:
  6.5 0.0 all-gather.3.cloned.1.call-start
  6.5 8.5 %copy.13 = bf16[1,24,8192]{1,0,2:T(2,128)(2,1)} copy(bf16[1,24,8192]{2,1,0:T(8,128)(2,1)} %bitcast.28) | data formatting | bytes 786432 | tf_op jit(solution)/shard_map/broadcast_in_dim | solution.py:12
  15.0 0.5 broadcast.4
  15.5 45.2 %reduce = bf16[8192,24]{1,0:T(8,128)(2,1)S(1)} reduce(bf16[8192,1,24]{2,1,0:T(2,128)(2,1)} %bitcast.24, bf16[]{:T(256)} %broadcast.4), dimensions={1}, to_apply=%bitcast.20.reduce_sub_computation | reduce | bytes 786434
  60.7 2.8 reshape.6
  63.5 8.9 %all_to_all.18 = bf16[4,2,24576]{2,1,0:T(2,128)(2,1)S(1)} all-to-all(bf16[4,2,24576]{2,1,0:T(2,128)(2,1)S(1)} %reshape.6), channel_id=1, replica_groups=mesh['ab'=64,'cd'=4] {'cd'}, dimensions={0} | all-to-all | bytes 786432 | tf_op jit(solution)/shard_map/all_to_all | solution.py:12
  72.4 0.0 copy-start
  72.4 0.0 copy-start.2
  72.4 6.5 %reshape.7 = bf16[8192,1,24]{2,1,0:T(2,128)(2,1)} reshape(bf16[4,2,24576]{2,1,0:T(2,128)(2,1)S(1)} %all_to_all.18) | data formatting | bytes 786432
  79.0 8.0 %copy.14 = bf16[1,24,8192]{2,1,0:T(8,128)(2,1)S(1)} copy(bf16[1,24,8192]{1,0,2:T(2,128)(2,1)} %bitcast.25) | data formatting | bytes 786432 | tf_op jit(solution)/shard_map/all_to_all | solution.py:12
  87.0 0.8 copy.19
  87.7 0.0 all-gather.3.cloned.1.call-update
  87.8 0.2 reduce-scatter.2.cloned.1.call-start
  88.0 0.7 dynamic_slice.3
  88.7 0.0 copy-start.1
  88.7 261.0 %all-gather.3.cloned.1.call-done = bf16[4,1,1536,2048]{3,2,0,1:T(8,128)(2,1)} async-done(((bf16[4,1,24,2048]{3,2,0,1:T(8,128)(2,1)}), bf16[4,1,1536,2048]{3,2,0,1:T(8,128)(2,1)}) %all-gather.3.cloned.1.call-update) | async-done | bytes 25165840 | tf_op jit(solution)/shard_map/all_gather | solution.py:15
  349.7 0.0 copy-done
  349.7 0.0 copy-done.2
  349.7 14.9 %fusion.2 = f32[4,1536,128]{1,2,0:T(8,128)} fusion(bf16[4,1,1536,2048]{3,2,0,1:T(8,128)(2,1)} %all-gather.3.cloned.1.call-done, bf16[128,2048]{1,0:T(8,128)(2,1)S(1)} %copy-done, s32[2048]{0:T(1024)S(1)} %dynamic_slice.3, s32[128]{0:T(128)S(1)} %copy-done.2), kind=kOutput, calls=%fused_computation.2 | convolution fusion | flops 3221749760 | bytes 28844544 | tf_op jit(solution)/shard_map/gkc,ac->gka/dot_general | solution.py:13
  364.6 0.0 reduce-scatter.2.cloned.1.call-update
  364.6 37.3 %reduce-scatter.2.cloned.1.call-done = f32[1,1536,128]{1,2,0:T(8,128)} async-done(((f32[4,1536,128]{1,2,0:T(8,128)}), f32[1,1536,128]{1,2,0:T(8,128)}) %reduce-scatter.2.cloned.1.call-update) | async-done | bytes 786448 | tf_op jit(solution)/shard_map/reduce_scatter | solution.py:19
  401.9 0.0 copy-done.1
  401.9 1.3 fusion.5
  403.2 0.9 copy.16
Async XLA Ops:
  6.5 343.1 %all-gather.3.cloned.1.call-start = ((), (), s32[]{:S(2)}) async-start(), calls=%async_computation.3 | async-start | bytes 25559040 | tf_op jit(solution)/shard_map/all_gather | solution.py:15
  72.4 277.2 %copy-start = (bf16[128,2048]{1,0:T(8,128)(2,1)S(1)}, bf16[128,2048]{1,0:T(8,128)(2,1)}, u32[]{:S(2)}) copy-start(bf16[128,2048]{1,0:T(8,128)(2,1)} %param.6) | copy-start | bytes 1572868
  72.4 277.2 %copy-start.2 = (s32[128]{0:T(128)S(1)}, s32[128]{0:T(128)}, u32[]{:S(2)}) copy-start(s32[128]{0:T(128)} %param.7) | copy-start | bytes 1540
  87.8 314.1 %reduce-scatter.2.cloned.1.call-start = ((), (), s32[]{:S(2)}) async-start(), calls=%async_computation.2 | async-start | bytes 3932160 | tf_op jit(solution)/shard_map/reduce_scatter | solution.py:19
  88.7 313.2 %copy-start.1 = (s32[1536]{0:T(1024)S(1)}, s32[1536]{0:T(1024)}, u32[]{:S(2)}) copy-start(s32[1536]{0:T(1024)} %param.9) | copy-start | bytes 18436
Sparse Core Ops, SparseCore 0:
  87.9 261.7 all-gather.2
  364.8 37.0 reduce-scatter.1
where the time goes:
time: 414 us; the launch traced here: 411 us
  waiting for transfers between devices  298 us (72%)
  other arithmetic  46.5 us (11%)
  local copies, waits for them, and re-layouts  28.7 us (7%)
  matrix products  14.9 us (4%)
  between operations  13.4 us (3%)
  blocking collectives  8.91 us (2%)
    all_gather x1, waiting for transfers between devices, local(): lax.all_gather(blocks, 'ab', axis=1, tiled=True)  261 us
    unnamed x1, other arithmetic  45.2 us
    reduce_scatter x1, waiting for transfers between devices, local(): lax.psum_scatter(partial_rows, 'cd', scatter_dimension=0, tiled=True)[0]  37.3 us
    dot_general x1, matrix products, local(): jnp.einsum('gkc,ac->gka', lax.all_gather(blocks, 'ab', axis=1, tiled=True...  14.9 us
    unnamed x9, local copies, waits for them, and re-layouts  9.84 us
    all_to_all x1, blocking collectives, local(): lax.all_to_all(amplitudes[None], 'cd', split_axis=2, concat_axis=0, tiled...  8.91 us
    all_to_all x2, local copies, waits for them, and re-layouts, local(): lax.all_to_all(amplitudes[None], 'cd', split_axis=2, concat_axis=0, tiled...  8.77 us
    broadcast_in_dim x1, local copies, waits for them, and re-layouts, local(): amplitudes[None]  8.46 us
  transfers between devices with their start and end apart: 2, of which 2 were waited for; matrix products, arithmetic and copies ran while one was open for 0% of the time, Pallas kernels for 0%

commit v1 on v0

v1 whole, which is shorter than its diff:
```python
import jax
import jax.numpy as jnp
from jax import lax
from jax.sharding import Mesh, PartitionSpec as P

AXES = ("z", "h", "x", "l", "k")
SIZES = (8, 2, 4, 2, 2)


def shift(value, axis, step, size):
    return lax.ppermute(value, axis, [(i, (i + step) % size) for i in range(size)])


def ring_of_four(block):
    below = shift(block, "x", 1, 4)
    above = shift(block, "x", 3, 4)
    half = block.shape[0] // 2
    far = jnp.concatenate(
        [shift(below[:half], "x", 1, 4), shift(above[half:], "x", 3, 4)], axis=0
    )
    return [block, below, far, above]


def local(amplitudes, integrals, ab_symmetry, cd_symmetry, ij_symmetry):
    rows, cols = amplitudes.shape
    width = integrals.shape[1]
    z, h, x = lax.axis_index("z"), lax.axis_index("h"), lax.axis_index("x")
    mine = (z * 2 + h) * 4 + x
    slab_labels = lax.dynamic_slice_in_dim(ij_symmetry, mine * rows, rows)
    allowed = slab_labels[:, None] == cd_symmetry[None, :]
    masked = jnp.where(allowed, amplitudes, jnp.zeros_like(amplitudes))

    other = shift(integrals, "h", 1, 2)
    blocks = ring_of_four(integrals) + ring_of_four(other)
    gathered = jnp.concatenate(blocks, axis=0)

    split = jnp.swapaxes(masked.reshape(rows, 4, width), 0, 1)
    swapped = lax.all_to_all(split, ("l", "k"), split_axis=0, concat_axis=0, tiled=True)
    lines = lax.all_gather(swapped.reshape(4 * rows, width), "z", axis=0, tiled=True)

    partial = lax.dot_general(
        lines, gathered, (((1,), (1,)), ((), ())), preferred_element_type=jnp.float32
    )
    partial = partial.reshape(8, 2, 2, rows, 8 * 128)
    k, l = lax.axis_index("k"), lax.axis_index("l")

    def reduce_over(value, axis, index):
        keep = lax.dynamic_index_in_dim(value, index, 1, keepdims=False)
        give = lax.dynamic_index_in_dim(value, 1 - index, 1, keepdims=False)
        return keep + shift(give, axis, 1, 2)

    summed = reduce_over(partial.swapaxes(1, 2), "k", k)
    summed = reduce_over(summed, "l", l)
    summed = summed.astype(jnp.bfloat16).reshape(8, rows, 2, 4, 128)
    home = []
    for dh in range(2):
        for dx in range(4):
            part = summed[:, :, dh, dx]
            if dh or dx:
                pairs = [
                    (a * 4 + b, ((a + dh) % 2) * 4 + (b - dx) % 4)
                    for a in range(2)
                    for b in range(4)
                ]
                part = lax.ppermute(part, ("h", "x"), pairs)
            home.append(part)
    home = jnp.stack(home).reshape(2, 4, 8, rows, 128)
    home = jnp.roll(home, (h, x), axis=(0, 1))
    out = home.transpose(2, 0, 1, 3, 4).reshape(64 * rows, 128)
    keep = ij_symmetry[:, None] == ab_symmetry[None, :]
    return jnp.where(keep, out, jnp.zeros_like(out))


def solution(mesh):
    fine = Mesh(mesh.devices.reshape(SIZES), AXES)
    ab, cd = ("z", "h", "x"), ("l", "k")
    placed = (P(cd + ab, None), P(ab, cd), P(ab), P(), P(cd))
    return jax.shard_map(
        local, mesh=fine, in_specs=placed, out_specs=P(cd, ab), check_vma=False
    )
```

time: 414 us -> 132 us (0.32)
  waiting for transfers between devices: 298 us -> 53.6 us
  other arithmetic: 46.5 us -> 4.29 us
  starting transfers between devices: 0.22 us -> 30.8 us
  local copies, waits for them, and re-layouts: 28.7 us -> 12.2 us
  matrix products: 14.9 us -> 6.19 us
    all_gather x1, waiting for transfers between devices: 261 us -> 3.68 us  [local(): lax.all_gather(swapped.reshape(4 * rows, width), 'z', axis=0, tiled=True)]
    ppermute x0 -> x18, waiting for transfers between devices: none -> 49.9 us  [the longest x11 43.3 us: shift(): lax.ppermute(value, axis, [(i, (i + step) % size) for i in range(size)])]
    unnamed x1 -> x0, other arithmetic: 45.2 us -> none
    reduce_scatter x1 -> x0, waiting for transfers between devices: 37.3 us -> none  [local(): lax.psum_scatter(partial_rows, 'cd', scatter_dimension=0, tiled=True)[0]]
    ppermute x0 -> x18, starting transfers between devices: none -> 30.8 us  [the longest x11 17.2 us: shift(): lax.ppermute(value, axis, [(i, (i + step) % size) for i in range(size)])]
    all_to_all x2 -> x0, local copies, waits for them, and re-layouts: 8.77 us -> none  [local(): lax.all_to_all(amplitudes[None], 'cd', split_axis=2, concat_axis=0, tiled...]
    dot_general x1, matrix products: 14.9 us -> 6.19 us  [local(): lax.dot_general(lines, gathered, (((1,), (1,)), ((), ())), preferred_elem...]
    broadcast_in_dim x1 -> x0, local copies, waits for them, and re-layouts: 8.46 us -> none  [local(): amplitudes[None]]
  transfers between devices with their start and end apart: 2 -> 19, of which waited for: 2 -> 9; matrix products, arithmetic and copies ran while one was open for 0% -> 6% of each run, Pallas kernels for 0% -> 0%
where the time goes in v1:
time: 132 us; the launch traced here: 130 us
  waiting for transfers between devices  53.6 us (41%)
  starting transfers between devices  30.8 us (23%)
  between operations  13.7 us (10%)
  local copies, waits for them, and re-layouts  12.2 us (9%)
  blocking collectives  9.59 us (7%)
  matrix products  6.19 us (5%)
  other arithmetic  4.29 us (3%)
    ppermute x11, waiting for transfers between devices, shift(): lax.ppermute(value, axis, [(i, (i + step) % size) for i in range(size)])  43.3 us
    ppermute x11, starting transfers between devices, shift(): lax.ppermute(value, axis, [(i, (i + step) % size) for i in range(size)])  17.2 us
    ppermute x7, starting transfers between devices, local(): part = lax.ppermute(part, ('h', 'x'), pairs)  13.6 us
    all_to_all x1, blocking collectives, local(): lax.all_to_all(split, ('l', 'k'), split_axis=0, concat_axis=0, tiled=True)  9.59 us
    unnamed x31, local copies, waits for them, and re-layouts  8.81 us
    ppermute x7, waiting for transfers between devices, local(): part = lax.ppermute(part, ('h', 'x'), pairs)  6.64 us
    dot_general x1, matrix products, local(): lax.dot_general(lines, gathered, (((1,), (1,)), ((), ())), preferred_elem...  6.19 us
    all_gather x1, waiting for transfers between devices, local(): lax.all_gather(swapped.reshape(4 * rows, width), 'z', axis=0, tiled=True)  3.68 us
  transfers between devices with their start and end apart: 19, of which 9 were waited for; matrix products, arithmetic and copies ran while one was open for 6% of the time, Pallas kernels for 0%

profile of v1, /device:TPU:24, one launch (start us, length us, event | category | flops | bytes accessed | tf_op | source)
XLA Modules:
  0.0 130.3 jit_solution(17320679174780102949)
XLA Ops:
  7.4 1.2 compare_select_fusion
  9.0 9.6 %all_to_all.5 = bf16[4,24,2048]{2,1,0:T(8,128)(2,1)} all-to-all(bf16[4,24,2048]{2,1,0:T(8,128)(2,1)S(1)} %copy.74), channel_id=1, replica_groups=mesh['z'=8,'h'=2,'x'=4,'l'=2,'k'=2] {'l','k'}, dimensions={0} | all-to-all | bytes 786432 | tf_op jit(solution)/shard_map/all_to_all | solution.py:38
  18.7 1.6 %collective-permute-start = (bf16[128,2048]{1,0:T(8,128)(2,1)}, bf16[128,2048]{1,0:T(8,128)(2,1)S(1)}, u32[]{:S(2)}, u32[]{:S(2)}) collective-permute-start(bf16[128,2048]{1,0:T(8,128)(2,1)} %param.6), channel_id=1, source_target_pairs={{0,4},{4,8},{8,12},{12,0},{1,5},{5,9},{9,13},{13,1},{2,6},{6,10},{... | collective-permute-start | bytes 1572872 | tf_op jit(solution)/shard_map/ppermute | solution.py:11
  20.2 1.7 %collective-permute-start.2 = (bf16[128,2048]{1,0:T(8,128)(2,1)}, bf16[128,2048]{1,0:T(8,128)(2,1)S(1)}, u32[]{:S(2)}, u32[]{:S(2)}) collective-permute-start(bf16[128,2048]{1,0:T(8,128)(2,1)} %param.6), channel_id=1, source_target_pairs={{0,12},{4,0},{8,4},{12,8},{1,13},{5,1},{9,5},{13,9},{2,14},{6,2},{... | collective-permute-start | bytes 1572872 | tf_op jit(solution)/shard_map/ppermute | solution.py:11
  22.0 2.7 %collective-permute-start.4 = (bf16[128,2048]{1,0:T(8,128)(2,1)}, bf16[128,2048]{1,0:T(8,128)(2,1)S(1)}, u32[]{:S(2)}, u32[]{:S(2)}) collective-permute-start(bf16[128,2048]{1,0:T(8,128)(2,1)} %param.6), channel_id=1, source_target_pairs={{0,16},{16,0},{1,17},{17,1},{2,18},{18,2},{3,19},{19,3},{4,20},{20... | collective-permute-start | bytes 1572872 | tf_op jit(solution)/shard_map/ppermute | solution.py:11
  24.6 9.2 %collective-permute-done = bf16[128,2048]{1,0:T(8,128)(2,1)S(1)} collective-permute-done((bf16[128,2048]{1,0:T(8,128)(2,1)}, bf16[128,2048]{1,0:T(8,128)(2,1)S(1)}, u32[]{:S(2)}, u32[]{:S(2)}) %collective-permute-start) | collective-permute-done | bytes 524320 | tf_op jit(solution)/shard_map/ppermute | solution.py:11
  35.1 3.0 %collective-permute-start.3 = (bf16[64,2048]{1,0:T(8,128)(2,1)S(1)}, bf16[64,2048]{1,0:T(8,128)(2,1)S(1)}, u32[]{:S(2)}, u32[]{:S(2)}) collective-permute-start(bf16[64,2048]{1,0:T(8,128)(2,1)S(1)} %slice.49), channel_id=1, source_target_pairs={{0,12},{4,0},{8,4},{12,8},{1,13},{5,1},{9,5},{13,9},{2,14},{6,2},{... | collective-permute-start | bytes 786440 | tf_op jit(solution)/shard_map/ppermute | solution.py:11
  38.2 3.2 %collective-permute-start.7 = (bf16[128,2048]{1,0:T(8,128)(2,1)S(1)}, bf16[128,2048]{1,0:T(8,128)(2,1)S(1)}, u32[]{:S(2)}, u32[]{:S(2)}) collective-permute-start(bf16[128,2048]{1,0:T(8,128)(2,1)S(1)} %collective-permute-done.4), channel_id=1, source_target_pairs={{0,12},{4,0},{8,4},{12,8},{1,13},{5,1},{9,5},{13,9},{2,14},{6,2},{... | collective-permute-start | bytes 1572872 | tf_op jit(solution)/shard_map/ppermute | solution.py:11
  42.2 2.1 %collective-permute-done.1 = bf16[64,2048]{1,0:T(8,128)(2,1)S(1)} collective-permute-done((bf16[64,2048]{1,0:T(8,128)(2,1)S(1)}, bf16[64,2048]{1,0:T(8,128)(2,1)S(1)}, u32[]{:S(2)}, u32[]{:S(2)}) %collective-permute-start.1) | collective-permute-done | bytes 262176 | tf_op jit(solution)/shard_map/ppermute | solution.py:11
  46.6 7.1 %collective-permute-done.5 = bf16[128,2048]{1,0:T(8,128)(2,1)S(1)} collective-permute-done((bf16[128,2048]{1,0:T(8,128)(2,1)S(1)}, bf16[128,2048]{1,0:T(8,128)(2,1)S(1)}, u32[]{:S(2)}, u32[]{:S(2)}) %collective-permute-start.5) | collective-permute-done | bytes 524320 | tf_op jit(solution)/shard_map/ppermute | solution.py:11
  54.6 3.3 %collective-permute-start.8 = (bf16[64,2048]{1,0:T(8,128)(2,1)S(1)}, bf16[64,2048]{1,0:T(8,128)(2,1)S(1)}, u32[]{:S(2)}, u32[]{:S(2)}) collective-permute-start(bf16[64,2048]{1,0:T(8,128)(2,1)S(1)} %slice.51), channel_id=1, source_target_pairs={{0,12},{4,0},{8,4},{12,8},{1,13},{5,1},{9,5},{13,9},{2,14},{6,2},{... | collective-permute-start | bytes 786440 | tf_op jit(solution)/shard_map/ppermute | solution.py:11
  58.8 2.7 %collective-permute-done.6 = bf16[64,2048]{1,0:T(8,128)(2,1)S(1)} collective-permute-done((bf16[64,2048]{1,0:T(8,128)(2,1)S(1)}, bf16[64,2048]{1,0:T(8,128)(2,1)S(1)}, u32[]{:S(2)}, u32[]{:S(2)}) %collective-permute-start.6) | collective-permute-done | bytes 262176 | tf_op jit(solution)/shard_map/ppermute | solution.py:11
  63.7 3.7 %all-gather.2.cloned.1.call-done = bf16[768,2048]{1,0:T(8,128)(2,1)} async-done(((bf16[96,2048]{1,0:T(8,128)(2,1)}), bf16[768,2048]{1,0:T(8,128)(2,1)}) %all-gather.2.cloned.1.call-update) | async-done | bytes 3145744 | tf_op jit(solution)/shard_map/all_gather | solution.py:39
  67.4 6.2 %fusion.5 = f32[768,1024]{1,0:T(8,128)S(1)} fusion(bf16[768,2048]{1,0:T(8,128)(2,1)} %all-gather.2.cloned.1.call-done, bf16[1024,2048]{1,0:T(8,128)(2,1)} %constant_dynamic-update-slice_fusion), kind=kOutput, calls=%fused_computation.40 | convolution fusion | flops 3221225472 | bytes 10485760 | tf_op jit(solution)/shard_map/dot_general | solution.py:41
  73.6 1.6 %copy-done = f32[768,1024]{1,0:T(8,128)} copy-done((f32[768,1024]{1,0:T(8,128)}, f32[768,1024]{1,0:T(8,128)S(1)}, u32[]{:S(2)}) %copy-start) | copy-done | bytes 3145752
  75.5 3.4 %collective-permute-done.9 = f32[8,2,24,1024]{3,2,1,0:T(8,128)S(1)} collective-permute-done((f32[8,2,24,1024]{3,2,1,0:T(8,128)S(1)}, f32[8,2,24,1024]{3,2,1,0:T(8,128)S(1)}, u32[]{:S(2)}, u32[]{:S(2)}) %collective-permute-start.9) | collective-permute-done | bytes 1572896 | tf_op jit(solution)/shard_map/ppermute | solution.py:11
  78.9 1.7 %bitcast_add_fusion = f32[8,2,24,1024]{3,2,1,0:T(8,128)S(1)} fusion(f32[8,2,24,1024]{3,2,1,0:T(8,128)S(1)} %collective-permute-done.9, f32[8,2,2,24,1024]{4,3,2,1,0:T(8,128)} %bitcast.62, s32[]{:T(128)S(6)} %select_n.50), kind=kLoop, calls=%fused_computation | loop fusion | flops 393216 | bytes 4718596 | tf_op jit(solution)/shard_map/add | solution.py:50
  81.8 18.7 %collective-permute-done.10 = f32[8,24,1024]{2,1,0:T(8,128)S(1)} collective-permute-done((f32[8,24,1024]{2,1,0:T(8,128)S(1)}, f32[8,24,1024]{2,1,0:T(8,128)S(1)}, u32[]{:S(2)}, u32[]{:S(2)}) %collective-permute-start.10) | collective-permute-done | bytes 786464 | tf_op jit(solution)/shard_map/ppermute | solution.py:11
  101.6 2.8 %collective-permute-start.11 = (bf16[8,24,128]{2,1,0:T(8,128)(2,1)S(1)}, bf16[8,24,128]{2,1,0:T(8,128)(2,1)S(1)}, u32[]{:S(2)}, u32[]{:S(2)}) collective-permute-start(bf16[8,24,128]{2,1,0:T(8,128)(2,1)S(1)} %bitcast.72), channel_id=1, source_target_pairs={{0,12},{4,0},{8,4},{12,8},{16,28},{20,16},{24,20},{28,24},{1,13},{... | collective-permute-start | bytes 147464 | tf_op jit(solution)/shard_map/ppermute | solution.py:65
  106.2 1.5 %collective-permute-start.14 = (bf16[8,24,128]{2,1,0:T(8,128)(2,1)S(1)}, bf16[8,24,128]{2,1,0:T(8,128)(2,1)S(1)}, u32[]{:S(2)}, u32[]{:S(2)}) collective-permute-start(bf16[8,24,128]{2,1,0:T(8,128)(2,1)S(1)} %bitcast.69), channel_id=1, source_target_pairs={{0,16},{4,20},{8,24},{12,28},{16,0},{20,4},{24,8},{28,12},{1,17},{... | collective-permute-start | bytes 147464 | tf_op jit(solution)/shard_map/ppermute | solution.py:65
  107.8 4.0 %collective-permute-start.15 = (bf16[8,24,128]{2,1,0:T(8,128)(2,1)S(1)}, bf16[8,24,128]{2,1,0:T(8,128)(2,1)S(1)}, u32[]{:S(2)}, u32[]{:S(2)}) collective-permute-start(bf16[8,24,128]{2,1,0:T(8,128)(2,1)S(1)} %bitcast.68), channel_id=1, source_target_pairs={{0,28},{4,16},{8,20},{12,24},{16,12},{20,0},{24,4},{28,8},{1,29},{... | collective-permute-start | bytes 147464 | tf_op jit(solution)/shard_map/ppermute | solution.py:65
  111.8 2.4 %collective-permute-start.16 = (bf16[8,24,128]{2,1,0:T(8,128)(2,1)S(1)}, bf16[8,24,128]{2,1,0:T(8,128)(2,1)S(1)}, u32[]{:S(2)}, u32[]{:S(2)}) collective-permute-start(bf16[8,24,128]{2,1,0:T(8,128)(2,1)S(1)} %bitcast.67), channel_id=1, source_target_pairs={{0,24},{4,28},{8,16},{12,20},{16,8},{20,12},{24,0},{28,4},{1,25},{... | collective-permute-start | bytes 147464 | tf_op jit(solution)/shard_map/ppermute | solution.py:65
  115.4 4.5 %collective-permute-done.16 = bf16[8,24,128]{2,1,0:T(8,128)(2,1)S(1)} collective-permute-done((bf16[8,24,128]{2,1,0:T(8,128)(2,1)S(1)}, bf16[8,24,128]{2,1,0:T(8,128)(2,1)S(1)}, u32[]{:S(2)}, u32[]{:S(2)}) %collective-permute-start.16) | collective-permute-done | bytes 49184 | tf_op jit(solution)/shard_map/ppermute | solution.py:65
  119.9 2.1 %collective-permute-done.17 = bf16[8,24,128]{2,1,0:T(8,128)(2,1)S(1)} collective-permute-done((bf16[8,24,128]{2,1,0:T(8,128)(2,1)S(1)}, bf16[8,24,128]{2,1,0:T(8,128)(2,1)S(1)}, u32[]{:S(2)}, u32[]{:S(2)}) %collective-permute-start.17) | collective-permute-done | bytes 49184 | tf_op jit(solution)/shard_map/ppermute | solution.py:65
  (68 shorter events, 16.6 us)
Async XLA Ops:
  6.5 27.7 %copy-start.1 = (bf16[128,2048]{1,0:T(8,128)(2,1)S(1)}, bf16[128,2048]{1,0:T(8,128)(2,1)}, u32[]{:S(2)}) copy-start(bf16[128,2048]{1,0:T(8,128)(2,1)} %param.6) | copy-start | bytes 1572868
  6.5 60.9 %all-gather.2.cloned.1.call-start = ((), (), s32[]{:S(2)}) async-start(), calls=%async_computation.1 | async-start | bytes 3538944 | tf_op jit(solution)/shard_map/all_gather | solution.py:39
  18.7 15.2 %collective-permute-start = (bf16[128,2048]{1,0:T(8,128)(2,1)}, bf16[128,2048]{1,0:T(8,128)(2,1)S(1)}, u32[]{:S(2)}, u32[]{:S(2)}) collective-permute-start(bf16[128,2048]{1,0:T(8,128)(2,1)} %param.6), channel_id=1, source_target_pairs={{0,4},{4,8},{8,12},{12,0},{1,5},{5,9},{9,13},{13,1},{2,6},{6,10},{... | collective-permute-start | bytes 1572872 | tf_op jit(solution)/shard_map/ppermute | solution.py:11
  20.2 14.9 %collective-permute-start.2 = (bf16[128,2048]{1,0:T(8,128)(2,1)}, bf16[128,2048]{1,0:T(8,128)(2,1)S(1)}, u32[]{:S(2)}, u32[]{:S(2)}) collective-permute-start(bf16[128,2048]{1,0:T(8,128)(2,1)} %param.6), channel_id=1, source_target_pairs={{0,12},{4,0},{8,4},{12,8},{1,13},{5,1},{9,5},{13,9},{2,14},{6,2},{... | collective-permute-start | bytes 1572872 | tf_op jit(solution)/shard_map/ppermute | solution.py:11
  22.0 16.2 %collective-permute-start.4 = (bf16[128,2048]{1,0:T(8,128)(2,1)}, bf16[128,2048]{1,0:T(8,128)(2,1)S(1)}, u32[]{:S(2)}, u32[]{:S(2)}) collective-permute-start(bf16[128,2048]{1,0:T(8,128)(2,1)} %param.6), channel_id=1, source_target_pairs={{0,16},{16,0},{1,17},{17,1},{2,18},{18,2},{3,19},{19,3},{4,20},{20... | collective-permute-start | bytes 1572872 | tf_op jit(solution)/shard_map/ppermute | solution.py:11
  33.9 10.5 %collective-permute-start.1 = (bf16[64,2048]{1,0:T(8,128)(2,1)S(1)}, bf16[64,2048]{1,0:T(8,128)(2,1)S(1)}, u32[]{:S(2)}, u32[]{:S(2)}) collective-permute-start(bf16[64,2048]{1,0:T(8,128)(2,1)S(1)} %slice.48), channel_id=1, source_target_pairs={{0,4},{4,8},{8,12},{12,0},{1,5},{5,9},{9,13},{13,1},{2,6},{6,10},{... | collective-permute-start | bytes 786440 | tf_op jit(solution)/shard_map/ppermute | solution.py:11
  35.1 9.9 %collective-permute-start.3 = (bf16[64,2048]{1,0:T(8,128)(2,1)S(1)}, bf16[64,2048]{1,0:T(8,128)(2,1)S(1)}, u32[]{:S(2)}, u32[]{:S(2)}) collective-permute-start(bf16[64,2048]{1,0:T(8,128)(2,1)S(1)} %slice.49), channel_id=1, source_target_pairs={{0,12},{4,0},{8,4},{12,8},{1,13},{5,1},{9,5},{13,9},{2,14},{6,2},{... | collective-permute-start | bytes 786440 | tf_op jit(solution)/shard_map/ppermute | solution.py:11
  38.2 15.5 %collective-permute-start.5 = (bf16[128,2048]{1,0:T(8,128)(2,1)S(1)}, bf16[128,2048]{1,0:T(8,128)(2,1)S(1)}, u32[]{:S(2)}, u32[]{:S(2)}) collective-permute-start(bf16[128,2048]{1,0:T(8,128)(2,1)S(1)} %collective-permute-done.4), channel_id=1, source_target_pairs={{0,4},{4,8},{8,12},{12,0},{1,5},{5,9},{9,13},{13,1},{2,6},{6,10},{... | collective-permute-start | bytes 1572872 | tf_op jit(solution)/shard_map/ppermute | solution.py:11
  38.2 16.4 %collective-permute-start.7 = (bf16[128,2048]{1,0:T(8,128)(2,1)S(1)}, bf16[128,2048]{1,0:T(8,128)(2,1)S(1)}, u32[]{:S(2)}, u32[]{:S(2)}) collective-permute-start(bf16[128,2048]{1,0:T(8,128)(2,1)S(1)} %collective-permute-done.4), channel_id=1, source_target_pairs={{0,12},{4,0},{8,4},{12,8},{1,13},{5,1},{9,5},{13,9},{2,14},{6,2},{... | collective-permute-start | bytes 1572872 | tf_op jit(solution)/shard_map/ppermute | solution.py:11
  53.7 7.8 %collective-permute-start.6 = (bf16[64,2048]{1,0:T(8,128)(2,1)S(1)}, bf16[64,2048]{1,0:T(8,128)(2,1)S(1)}, u32[]{:S(2)}, u32[]{:S(2)}) collective-permute-start(bf16[64,2048]{1,0:T(8,128)(2,1)S(1)} %slice.50), channel_id=1, source_target_pairs={{0,4},{4,8},{8,12},{12,0},{1,5},{5,9},{9,13},{13,1},{2,6},{6,10},{... | collective-permute-start | bytes 786440 | tf_op jit(solution)/shard_map/ppermute | solution.py:11
  54.6 7.6 %collective-permute-start.8 = (bf16[64,2048]{1,0:T(8,128)(2,1)S(1)}, bf16[64,2048]{1,0:T(8,128)(2,1)S(1)}, u32[]{:S(2)}, u32[]{:S(2)}) collective-permute-start(bf16[64,2048]{1,0:T(8,128)(2,1)S(1)} %slice.51), channel_id=1, source_target_pairs={{0,12},{4,0},{8,4},{12,8},{1,13},{5,1},{9,5},{13,9},{2,14},{6,2},{... | collective-permute-start | bytes 786440 | tf_op jit(solution)/shard_map/ppermute | solution.py:11
  73.6 1.6 %copy-start = (f32[768,1024]{1,0:T(8,128)}, f32[768,1024]{1,0:T(8,128)S(1)}, u32[]{:S(2)}) copy-start(f32[768,1024]{1,0:T(8,128)S(1)} %fusion.5) | copy-start | bytes 9437188
  75.4 3.5 %collective-permute-start.9 = (f32[8,2,24,1024]{3,2,1,0:T(8,128)S(1)}, f32[8,2,24,1024]{3,2,1,0:T(8,128)S(1)}, u32[]{:S(2)}, u32[]{:S(2)}) collective-permute-start(f32[8,2,24,1024]{3,2,1,0:T(8,128)S(1)} %dynamic-slice_bitcast_fusion), channel_id=1, source_target_pairs={{0,1},{1,0},{2,3},{3,2},{4,5},{5,4},{6,7},{7,6},{8,9},{9,8},{10,11... | collective-permute-start | bytes 4718600 | tf_op jit(solution)/shard_map/ppermute | solution.py:11
  80.7 19.9 %collective-permute-start.10 = (f32[8,24,1024]{2,1,0:T(8,128)S(1)}, f32[8,24,1024]{2,1,0:T(8,128)S(1)}, u32[]{:S(2)}, u32[]{:S(2)}) collective-permute-start(f32[8,24,1024]{2,1,0:T(8,128)S(1)} %dynamic-slice_bitcast_fusion.1), channel_id=1, source_target_pairs={{0,2},{2,0},{1,3},{3,1},{4,6},{6,4},{5,7},{7,5},{8,10},{10,8},{9,1... | collective-permute-start | bytes 2359304 | tf_op jit(solution)/shard_map/ppermute | solution.py:11
  81.8 40.6 %copy-start.2 = (s32[1536]{0:T(1024)S(1)}, s32[1536]{0:T(1024)}, u32[]{:S(2)}) copy-start(s32[1536]{0:T(1024)} %param.9) | copy-start | bytes 18436
  81.8 40.6 %copy-start.3 = (s32[128]{0:T(128)S(1)}, s32[128]{0:T(128)}, u32[]{:S(2)}) copy-start(s32[128]{0:T(128)} %param.7) | copy-start | bytes 1540
  101.6 10.2 %collective-permute-start.11 = (bf16[8,24,128]{2,1,0:T(8,128)(2,1)S(1)}, bf16[8,24,128]{2,1,0:T(8,128)(2,1)S(1)}, u32[]{:S(2)}, u32[]{:S(2)}) collective-permute-start(bf16[8,24,128]{2,1,0:T(8,128)(2,1)S(1)} %bitcast.72), channel_id=1, source_target_pairs={{0,12},{4,0},{8,4},{12,8},{16,28},{20,16},{24,20},{28,24},{1,13},{... | collective-permute-start | bytes 147464 | tf_op jit(solution)/shard_map/ppermute | solution.py:65
  104.4 9.9 %collective-permute-start.12 = (bf16[8,24,128]{2,1,0:T(8,128)(2,1)S(1)}, bf16[8,24,128]{2,1,0:T(8,128)(2,1)S(1)}, u32[]{:S(2)}, u32[]{:S(2)}) collective-permute-start(bf16[8,24,128]{2,1,0:T(8,128)(2,1)S(1)} %bitcast.71), channel_id=1, source_target_pairs={{0,8},{4,12},{8,0},{12,4},{16,24},{20,28},{24,16},{28,20},{1,9},{5... | collective-permute-start | bytes 147464 | tf_op jit(solution)/shard_map/ppermute | solution.py:65
  105.3 10.0 %collective-permute-start.13 = (bf16[8,24,128]{2,1,0:T(8,128)(2,1)S(1)}, bf16[8,24,128]{2,1,0:T(8,128)(2,1)S(1)}, u32[]{:S(2)}, u32[]{:S(2)}) collective-permute-start(bf16[8,24,128]{2,1,0:T(8,128)(2,1)S(1)} %bitcast.70), channel_id=1, source_target_pairs={{0,4},{4,8},{8,12},{12,0},{16,20},{20,24},{24,28},{28,16},{1,5},{5... | collective-permute-start | bytes 147464 | tf_op jit(solution)/shard_map/ppermute | solution.py:65
  106.2 9.1 %collective-permute-start.14 = (bf16[8,24,128]{2,1,0:T(8,128)(2,1)S(1)}, bf16[8,24,128]{2,1,0:T(8,128)(2,1)S(1)}, u32[]{:S(2)}, u32[]{:S(2)}) collective-permute-start(bf16[8,24,128]{2,1,0:T(8,128)(2,1)S(1)} %bitcast.69), channel_id=1, source_target_pairs={{0,16},{4,20},{8,24},{12,28},{16,0},{20,4},{24,8},{28,12},{1,17},{... | collective-permute-start | bytes 147464 | tf_op jit(solution)/shard_map/ppermute | solution.py:65
  107.8 7.6 %collective-permute-start.15 = (bf16[8,24,128]{2,1,0:T(8,128)(2,1)S(1)}, bf16[8,24,128]{2,1,0:T(8,128)(2,1)S(1)}, u32[]{:S(2)}, u32[]{:S(2)}) collective-permute-start(bf16[8,24,128]{2,1,0:T(8,128)(2,1)S(1)} %bitcast.68), channel_id=1, source_target_pairs={{0,28},{4,16},{8,20},{12,24},{16,12},{20,0},{24,4},{28,8},{1,29},{... | collective-permute-start | bytes 147464 | tf_op jit(solution)/shard_map/ppermute | solution.py:65
  111.8 8.1 %collective-permute-start.16 = (bf16[8,24,128]{2,1,0:T(8,128)(2,1)S(1)}, bf16[8,24,128]{2,1,0:T(8,128)(2,1)S(1)}, u32[]{:S(2)}, u32[]{:S(2)}) collective-permute-start(bf16[8,24,128]{2,1,0:T(8,128)(2,1)S(1)} %bitcast.67), channel_id=1, source_target_pairs={{0,24},{4,28},{8,16},{12,20},{16,8},{20,12},{24,0},{28,4},{1,25},{... | collective-permute-start | bytes 147464 | tf_op jit(solution)/shard_map/ppermute | solution.py:65
  114.2 7.8 %collective-permute-start.17 = (bf16[8,24,128]{2,1,0:T(8,128)(2,1)S(1)}, bf16[8,24,128]{2,1,0:T(8,128)(2,1)S(1)}, u32[]{:S(2)}, u32[]{:S(2)}) collective-permute-start(bf16[8,24,128]{2,1,0:T(8,128)(2,1)S(1)} %bitcast.66), channel_id=1, source_target_pairs={{0,20},{4,24},{8,28},{12,16},{16,4},{20,8},{24,12},{28,0},{1,21},{... | collective-permute-start | bytes 147464 | tf_op jit(solution)/shard_map/ppermute | solution.py:65
Sparse Core Ops, SparseCore 0:
  18.8 48.5 all-gather.1

commit v2 on v0

v2 whole, which is shorter than its diff:
```python
import jax
import jax.numpy as jnp
from jax import lax
from jax.sharding import Mesh, PartitionSpec as P

AXES = ("z", "h", "x", "l", "k")
SIZES = {"z": 8, "h": 2, "x": 4, "l": 2, "k": 2}
ARRIVAL = (0, -1, 1, -2, 2, -3, 3, 4)


def shift(value, axis, step):
    size = SIZES[axis]
    return lax.ppermute(value, axis, [(i, (i + step) % size) for i in range(size)])


def after(values, others):
    return lax.optimization_barrier((tuple(values), tuple(others)))[0]


def far_of(below, above):
    half = below.shape[0] // 2
    return [shift(below[:half], "x", 1), shift(above[half:], "x", -1)]


def product(lines, gathered):
    return lax.dot_general(
        lines, gathered, (((1,), (1,)), ((), ())), preferred_element_type=jnp.float32
    )


def local(amplitudes, integrals, ab_symmetry, cd_symmetry, ij_symmetry):
    rows = amplitudes.shape[0]
    width = integrals.shape[1]
    at = {name: lax.axis_index(name) for name in AXES}
    l, k = at["l"], at["k"]

    first = ((at["z"] * 2 + at["h"]) * 4 + at["x"]) * rows
    slab_labels = lax.dynamic_slice_in_dim(ij_symmetry, first, rows)

    def columns(l, k):
        start = (l * 2 + k) * width
        labels = lax.dynamic_slice_in_dim(cd_symmetry, start, width)
        part = lax.dynamic_slice_in_dim(amplitudes, start, width, axis=1)
        return jnp.where(slab_labels[:, None] == labels[None, :], part, jnp.zeros_like(part))

    far = shift(jnp.concatenate([columns(1 - l, k), columns(1 - l, 1 - k)], axis=0), "l", 1)
    give = jnp.concatenate([columns(l, 1 - k), far[rows:]], axis=0)
    slabs = jnp.concatenate([columns(l, k), far[:rows], shift(give, "k", 1)], axis=0)

    half = 2 * rows
    up, down = [slabs], [slabs]
    for _ in range(3):
        up.append(shift(up[-1], "z", 1))
        down.append(shift(down[-1], "z", -1))
    opposite = [shift(up[-1][:half], "z", 1), shift(down[-1][half:], "z", -1)]

    below, above = shift(integrals, "x", 1), shift(integrals, "x", -1)
    (block,) = after((integrals,), (below, above))
    other = shift(block, "h", 1)
    middle = far_of(below, above)
    gathered = [integrals, below, *middle, above]
    (other,) = after((other,), middle)
    below, above = shift(other, "x", 1), shift(other, "x", -1)
    gathered += [other, below, *far_of(below, above), above]
    gathered = jnp.concatenate(gathered, axis=0)

    def core_sum(parts):
        n = len(parts)
        own = jnp.concatenate([p[:half] for p in parts], axis=0)
        got = shift(product(jnp.concatenate([p[half:] for p in parts], axis=0), gathered), "k", 1)
        return (product(own, gathered) + got).reshape(n, 2, rows, 8 * 128)

    def packed(summed):
        give = summed.reshape(-1, summed.shape[-1])
        top = jnp.maximum(jnp.max(jnp.abs(give), axis=0, keepdims=True), 1e-30)
        power = jnp.floor(jnp.log2(32768.0 / top))
        give = (give * jnp.exp2(power)).astype(jnp.float16)
        power = jnp.broadcast_to(power, (8, power.shape[1])).astype(jnp.float16)
        return jnp.concatenate([give, power], axis=0)

    def unpacked(got):
        n = got.shape[0] - 8
        got = got.astype(jnp.float32)
        return got[:n] * jnp.exp2(-got[n : n + 1])

    def gives(summed):
        near, other = summed[..., : 4 * 128], summed[..., 4 * 128 :]
        return packed(near[:, 1]), packed(other[:, 0]), packed(other[:, 1])

    flip = [(0, 3), (1, 2), (2, 1), (3, 0)]

    def exchanged(summed, given, in_turn):
        got_l = shift(given[0], "l", 1)
        others = after(given[1:], (got_l,)) if in_turn else given[1:]
        got_h, got_hl = shift(others[0], "h", 1), lax.ppermute(others[1], ("h", "l"), flip)
        own = summed[:, 0, :, : 4 * 128].reshape(-1, 4 * 128) + unpacked(got_l)
        return jnp.stack([own, unpacked(got_h) + unpacked(got_hl)]).astype(jnp.bfloat16)

    early = core_sum([slabs, up[1], down[1], up[2], down[2], up[3], down[3]])
    early_give = gives(early)
    opposite = after(opposite, early_give)
    early = exchanged(early, early_give, True)
    both = product(jnp.concatenate(opposite, axis=0), gathered)
    late = (both[:half] + shift(both[half:], "k", 1)).reshape(1, 2, rows, 8 * 128)
    late = exchanged(late, gives(late), False)
    result = jnp.concatenate([early, late], axis=1)
    home = [result[:, :, :128]]
    home += [shift(result[:, :, dx * 128 : dx * 128 + 128], "x", -dx) for dx in (1, 2, 3)]
    out = jnp.stack(home).reshape(4, 2, 8, rows, 128)
    order = [ARRIVAL.index(d if d < 5 else d - 8) for d in range(8)]
    out = out[:, :, jnp.array(order)].transpose(2, 1, 0, 3, 4)
    out = jnp.roll(out, (at["z"], at["h"], at["x"]), axis=(0, 1, 2)).reshape(64 * rows, 128)
    keep = ij_symmetry[:, None] == ab_symmetry[None, :]
    return jnp.where(keep, out, jnp.zeros_like(out))


def solution(mesh):
    fine = Mesh(mesh.devices.reshape(tuple(SIZES.values())), AXES)
    ab, cd = ("z", "h", "x"), ("l", "k")
    placed = (P(cd + ab, None), P(ab, cd), P(ab), P(), P(cd))
    return jax.shard_map(
        local, mesh=fine, in_specs=placed, out_specs=P(cd, ab), check_vma=False
    )
```

time: 414 us -> 104 us (0.25)
  waiting for transfers between devices: 298 us -> 34.6 us
  starting transfers between devices: 0.22 us -> 52 us
  other arithmetic: 46.5 us -> 3.82 us
  local copies, waits for them, and re-layouts: 28.7 us -> 3.52 us
  between operations: 13.4 us -> 0.59 us
  blocking collectives: 8.91 us -> 0 us
  matrix products: 14.9 us -> 7.99 us
    all_gather x1 -> x0, waiting for transfers between devices: 261 us -> none  [local(): lax.all_gather(blocks, 'ab', axis=1, tiled=True)]
    ppermute x0 -> x30, starting transfers between devices: none -> 52 us  [the longest x28 49.8 us: shift(): lax.ppermute(value, axis, [(i, (i + step) % size) for i in range(size)])]
    unnamed x1, other arithmetic: 45.2 us -> 1.2 us
    reduce_scatter x1 -> x0, waiting for transfers between devices: 37.3 us -> none  [local(): lax.psum_scatter(partial_rows, 'cd', scatter_dimension=0, tiled=True)[0]]
    ppermute x0 -> x30, waiting for transfers between devices: none -> 34.6 us  [the longest x28 33 us: shift(): lax.ppermute(value, axis, [(i, (i + step) % size) for i in range(size)])]
    all_to_all x1 -> x0, blocking collectives: 8.91 us -> none  [local(): lax.all_to_all(amplitudes[None], 'cd', split_axis=2, concat_axis=0, tiled...]
    unnamed x9 -> x28, local copies, waits for them, and re-layouts: 9.84 us -> 0.98 us
    all_to_all x2 -> x0, local copies, waits for them, and re-layouts: 8.77 us -> none  [local(): lax.all_to_all(amplitudes[None], 'cd', split_axis=2, concat_axis=0, tiled...]
  transfers between devices with their start and end apart: 2 -> 30, of which waited for: 2 -> 16; matrix products, arithmetic and copies ran while one was open for 0% -> 7% of each run, Pallas kernels for 0% -> 0%
where the time goes in v2:
time: 104 us; the launch traced here: 103 us
  starting transfers between devices  52 us (50%)
  waiting for transfers between devices  34.6 us (33%)
  matrix products  7.99 us (8%)
  other arithmetic  3.82 us (4%)
  local copies, waits for them, and re-layouts  3.52 us (3%)
    ppermute x28, starting transfers between devices, shift(): lax.ppermute(value, axis, [(i, (i + step) % size) for i in range(size)])  49.8 us
    ppermute x28, waiting for transfers between devices, shift(): lax.ppermute(value, axis, [(i, (i + step) % size) for i in range(size)])  33 us
    dot_general x3, matrix products, product(): lax.dot_general(lines, gathered, (((1,), (1,)), ((), ())), preferred_elem...  7.99 us
    ppermute x2, starting transfers between devices, exchanged(): lax.ppermute(others[1], ('h', 'l'), flip)  2.21 us
  transfers between devices with their start and end apart: 30, of which 16 were waited for; matrix products, arithmetic and copies ran while one was open for 7% of the time, Pallas kernels for 0%

profile of v2, /device:TPU:24, one launch (start us, length us, event | category | flops | bytes accessed | tf_op | source)
XLA Modules:
  0.0 102.6 jit_solution(6765729114491656153)
XLA Ops:
  5.1 1.7 %collective-permute-start.10 = (bf16[128,2048]{1,0:T(8,128)(2,1)S(1)}, bf16[128,2048]{1,0:T(8,128)(2,1)S(1)}, u32[]{:S(2)}, u32[]{:S(2)}) collective-permute-start(bf16[128,2048]{1,0:T(8,128)(2,1)S(1)} %copy-done.2), channel_id=1, source_target_pairs={{0,12},{4,0},{8,4},{12,8},{1,13},{5,1},{9,5},{13,9},{2,14},{6,2},{... | collective-permute-start | bytes 1572872 | tf_op jit(solution)/shard_map/ppermute | solution.py:13
  6.9 2.7 %collective-permute-done = bf16[48,2048]{1,0:T(8,128)(2,1)S(1)} collective-permute-done((bf16[48,2048]{1,0:T(8,128)(2,1)S(1)}, bf16[48,2048]{1,0:T(8,128)(2,1)S(1)}, u32[]{:S(2)}, u32[]{:S(2)}) %collective-permute-start) | collective-permute-done | bytes 196640 | tf_op jit(solution)/shard_map/ppermute | solution.py:13
  11.1 2.0 %collective-permute-start.2 = (bf16[96,2048]{1,0:T(8,128)(2,1)S(1)}, bf16[96,2048]{1,0:T(8,128)(2,1)S(1)}, u32[]{:S(2)}, u32[]{:S(2)}) collective-permute-start(bf16[96,2048]{1,0:T(8,128)(2,1)S(1)} %pad_maximum_fusion), channel_id=1, source_target_pairs={{0,32},{32,64},{64,96},{96,128},{128,160},{160,192},{192,224},{224... | collective-permute-start | bytes 1179656 | tf_op jit(solution)/shard_map/ppermute | solution.py:13
  13.1 4.0 %collective-permute-start.3 = (bf16[96,2048]{1,0:T(8,128)(2,1)S(1)}, bf16[96,2048]{1,0:T(8,128)(2,1)S(1)}, u32[]{:S(2)}, u32[]{:S(2)}) collective-permute-start(bf16[96,2048]{1,0:T(8,128)(2,1)S(1)} %pad_maximum_fusion), channel_id=1, source_target_pairs={{0,224},{32,0},{64,32},{96,64},{128,96},{160,128},{192,160},{224,1... | collective-permute-start | bytes 1179656 | tf_op jit(solution)/shard_map/ppermute | solution.py:13
  18.8 2.9 %collective-permute-start.11 = (bf16[64,2048]{1,0:T(8,128)(2,1)S(1)}, bf16[64,2048]{1,0:T(8,128)(2,1)S(1)}, u32[]{:S(2)}, u32[]{:S(2)}) collective-permute-start(bf16[64,2048]{1,0:T(8,128)(2,1)S(1)} %slice.201), channel_id=1, source_target_pairs={{0,12},{4,0},{8,4},{12,8},{1,13},{5,1},{9,5},{13,9},{2,14},{6,2},{... | collective-permute-start | bytes 786440 | tf_op jit(solution)/shard_map/ppermute | solution.py:13
  22.6 3.9 %collective-permute-done.9 = bf16[64,2048]{1,0:T(8,128)(2,1)S(1)} collective-permute-done((bf16[64,2048]{1,0:T(8,128)(2,1)S(1)}, bf16[64,2048]{1,0:T(8,128)(2,1)S(1)}, u32[]{:S(2)}, u32[]{:S(2)}) %collective-permute-start.9) | collective-permute-done | bytes 262176 | tf_op jit(solution)/shard_map/ppermute | solution.py:13
  26.8 1.8 %collective-permute-start.4 = (bf16[96,2048]{1,0:T(8,128)(2,1)S(1)}, bf16[96,2048]{1,0:T(8,128)(2,1)S(1)}, u32[]{:S(2)}, u32[]{:S(2)}) collective-permute-start(bf16[96,2048]{1,0:T(8,128)(2,1)S(1)} %collective-permute-done.2), channel_id=1, source_target_pairs={{0,32},{32,64},{64,96},{96,128},{128,160},{160,192},{192,224},{224... | collective-permute-start | bytes 1179656 | tf_op jit(solution)/shard_map/ppermute | solution.py:13
  28.5 4.0 %collective-permute-start.5 = (bf16[96,2048]{1,0:T(8,128)(2,1)S(1)}, bf16[96,2048]{1,0:T(8,128)(2,1)S(1)}, u32[]{:S(2)}, u32[]{:S(2)}) collective-permute-start(bf16[96,2048]{1,0:T(8,128)(2,1)S(1)} %collective-permute-done.3), channel_id=1, source_target_pairs={{0,224},{32,0},{64,32},{96,64},{128,96},{160,128},{192,160},{224,1... | collective-permute-start | bytes 1179656 | tf_op jit(solution)/shard_map/ppermute | solution.py:13
  32.6 2.7 %collective-permute-done.12 = bf16[128,2048]{1,0:T(8,128)(2,1)S(1)} collective-permute-done((bf16[128,2048]{1,0:T(8,128)(2,1)S(1)}, bf16[128,2048]{1,0:T(8,128)(2,1)S(1)}, u32[]{:S(2)}, u32[]{:S(2)}) %collective-permute-start.12) | collective-permute-done | bytes 524320 | tf_op jit(solution)/shard_map/ppermute | solution.py:13
  35.5 3.0 %collective-permute-start.15 = (bf16[128,2048]{1,0:T(8,128)(2,1)S(1)}, bf16[128,2048]{1,0:T(8,128)(2,1)S(1)}, u32[]{:S(2)}, u32[]{:S(2)}) collective-permute-start(bf16[128,2048]{1,0:T(8,128)(2,1)S(1)} %collective-permute-done.12), channel_id=1, source_target_pairs={{0,12},{4,0},{8,4},{12,8},{1,13},{5,1},{9,5},{13,9},{2,14},{6,2},{... | collective-permute-start | bytes 1572872 | tf_op jit(solution)/shard_map/ppermute | solution.py:13
  40.4 4.0 %collective-permute-start.7 = (bf16[96,2048]{1,0:T(8,128)(2,1)S(1)}, bf16[96,2048]{1,0:T(8,128)(2,1)S(1)}, u32[]{:S(2)}, u32[]{:S(2)}) collective-permute-start(bf16[96,2048]{1,0:T(8,128)(2,1)S(1)} %collective-permute-done.5), channel_id=1, source_target_pairs={{0,224},{32,0},{64,32},{96,64},{128,96},{160,128},{192,160},{224,1... | collective-permute-start | bytes 1179656 | tf_op jit(solution)/shard_map/ppermute | solution.py:13
  44.5 3.1 %collective-permute-done.13 = bf16[128,2048]{1,0:T(8,128)(2,1)S(1)} collective-permute-done((bf16[128,2048]{1,0:T(8,128)(2,1)S(1)}, bf16[128,2048]{1,0:T(8,128)(2,1)S(1)}, u32[]{:S(2)}, u32[]{:S(2)}) %collective-permute-start.13) | collective-permute-done | bytes 524320 | tf_op jit(solution)/shard_map/ppermute | solution.py:13
  48.1 3.2 %collective-permute-start.16 = (bf16[64,2048]{1,0:T(8,128)(2,1)S(1)}, bf16[64,2048]{1,0:T(8,128)(2,1)S(1)}, u32[]{:S(2)}, u32[]{:S(2)}) collective-permute-start(bf16[64,2048]{1,0:T(8,128)(2,1)S(1)} %slice.203), channel_id=1, source_target_pairs={{0,12},{4,0},{8,4},{12,8},{1,13},{5,1},{9,5},{13,9},{2,14},{6,2},{... | collective-permute-start | bytes 786440 | tf_op jit(solution)/shard_map/ppermute | solution.py:13
  51.4 4.1 %collective-permute-done.14 = bf16[64,2048]{1,0:T(8,128)(2,1)S(1)} collective-permute-done((bf16[64,2048]{1,0:T(8,128)(2,1)S(1)}, bf16[64,2048]{1,0:T(8,128)(2,1)S(1)}, u32[]{:S(2)}, u32[]{:S(2)}) %collective-permute-start.14) | collective-permute-done | bytes 262176 | tf_op jit(solution)/shard_map/ppermute | solution.py:13
  55.6 2.8 %fusion.42 = f32[336,1024]{1,0:T(8,128)} fusion(bf16[336,2048]{1,0:T(8,128)(2,1)S(1)} %get-tuple-element.37, bf16[1024,2048]{1,0:T(8,128)(2,1)S(1)} %constant_dynamic-update-slice_fusion.3), kind=kOutput, calls=%fused_computation.133 | convolution fusion | flops 1409286144 | bytes 6946816 | tf_op jit(solution)/shard_map/dot_general | solution.py:26
  60.0 4.0 %collective-permute-start.22 = (bf16[48,2048]{1,0:T(8,128)(2,1)S(1)}, bf16[48,2048]{1,0:T(8,128)(2,1)S(1)}, u32[]{:S(2)}, u32[]{:S(2)}) collective-permute-start(bf16[48,2048]{1,0:T(8,128)(2,1)S(1)} %get-tuple-element.38), channel_id=1, source_target_pairs={{0,224},{32,0},{64,32},{96,64},{128,96},{160,128},{192,160},{224,1... | collective-permute-start | bytes 589832 | tf_op jit(solution)/shard_map/ppermute | solution.py:13
  64.0 3.8 %convolution_add_fusion = f32[336,1024]{1,0:T(8,128)S(1)} fusion(f32[336,1024]{1,0:T(8,128)S(1)} %collective-permute-done.17, bf16[336,2048]{1,0:T(8,128)(2,1)S(1)} %get-tuple-element.36, bf16[1024,2048]{1,0:T(8,128)(2,1)} %copy-done), kind=kOutput, calls=%fused_computation.1 | convolution fusion | flops 1409630208 | bytes 8323072 | tf_op jit(solution)/shard_map/dot_general | solution.py:26
  71.7 3.2 %collective-permute-done.18 = f16[176,512]{1,0:T(8,128)(2,1)S(1)} collective-permute-done((f16[176,512]{1,0:T(8,128)(2,1)S(1)}, f16[176,512]{1,0:T(8,128)(2,1)S(1)}, u32[]{:S(2)}, u32[]{:S(2)}) %collective-permute-start.18) | collective-permute-done | bytes 180256 | tf_op jit(solution)/shard_map/ppermute | solution.py:13
  75.9 2.3 %collective-permute-start.19 = (f16[176,512]{1,0:T(8,128)(2,1)S(1)}, f16[176,512]{1,0:T(8,128)(2,1)S(1)}, u32[]{:S(2)}, u32[]{:S(2)}) collective-permute-start(f16[176,512]{1,0:T(8,128)(2,1)S(1)} %pad_maximum_fusion.5), channel_id=1, source_target_pairs={{0,16},{16,0},{1,17},{17,1},{2,18},{18,2},{3,19},{19,3},{4,20},{20... | collective-permute-start | bytes 540680 | tf_op jit(solution)/shard_map/ppermute | solution.py:13
  79.4 3.8 %collective-permute-done.24 = f16[32,512]{1,0:T(8,128)(2,1)S(1)} collective-permute-done((f16[32,512]{1,0:T(8,128)(2,1)S(1)}, f16[32,512]{1,0:T(8,128)(2,1)S(1)}, u32[]{:S(2)}, u32[]{:S(2)}) %collective-permute-start.24) | collective-permute-done | bytes 32800 | tf_op jit(solution)/shard_map/ppermute | solution.py:13
  84.4 2.4 %collective-permute-start.25 = (f16[32,512]{1,0:T(8,128)(2,1)S(1)}, f16[32,512]{1,0:T(8,128)(2,1)S(1)}, u32[]{:S(2)}, u32[]{:S(2)}) collective-permute-start(f16[32,512]{1,0:T(8,128)(2,1)S(1)} %pad_maximum_fusion.8), channel_id=1, source_target_pairs={{0,16},{16,0},{1,17},{17,1},{2,18},{18,2},{3,19},{19,3},{4,20},{20... | collective-permute-start | bytes 98312 | tf_op jit(solution)/shard_map/ppermute | solution.py:13
  86.8 1.7 %collective-permute-done.26 = f16[32,512]{1,0:T(8,128)(2,1)S(1)} collective-permute-done((f16[32,512]{1,0:T(8,128)(2,1)S(1)}, f16[32,512]{1,0:T(8,128)(2,1)S(1)}, u32[]{:S(2)}, u32[]{:S(2)}) %collective-permute-start.26) | collective-permute-done | bytes 32800 | tf_op jit(solution)/shard_map/ppermute | solution.py:95
  90.6 4.8 %collective-permute-start.28 = (bf16[2,192,128]{2,1,0:T(8,128)(2,1)S(1)}, bf16[2,192,128]{2,1,0:T(8,128)(2,1)S(1)}, u32[]{:S(2)}, u32[]{:S(2)}) collective-permute-start(bf16[2,192,128]{2,1,0:T(8,128)(2,1)S(1)} %get-tuple-element.34), channel_id=1, source_target_pairs={{0,8},{4,12},{8,0},{12,4},{1,9},{5,13},{9,1},{13,5},{2,10},{6,14},... | collective-permute-start | bytes 294920 | tf_op jit(solution)/shard_map/ppermute | solution.py:13
  96.5 2.5 %collective-permute-done.28 = bf16[2,192,128]{2,1,0:T(8,128)(2,1)S(1)} collective-permute-done((bf16[2,192,128]{2,1,0:T(8,128)(2,1)S(1)}, bf16[2,192,128]{2,1,0:T(8,128)(2,1)S(1)}, u32[]{:S(2)}, u32[]{:S(2)}) %collective-permute-start.28) | collective-permute-done | bytes 98336 | tf_op jit(solution)/shard_map/ppermute | solution.py:13
  (130 shorter events, 27.9 us)
Async XLA Ops:
  2.8 6.7 %collective-permute-start = (bf16[48,2048]{1,0:T(8,128)(2,1)S(1)}, bf16[48,2048]{1,0:T(8,128)(2,1)S(1)}, u32[]{:S(2)}, u32[]{:S(2)}) collective-permute-start(bf16[48,2048]{1,0:T(8,128)(2,1)S(1)} %pad_maximum_fusion.2), channel_id=1, source_target_pairs={{0,2},{2,0},{1,3},{3,1},{4,6},{6,4},{5,7},{7,5},{8,10},{10,8},{9,1... | collective-permute-start | bytes 589832 | tf_op jit(solution)/shard_map/ppermute | solution.py:13
  3.6 14.6 %collective-permute-start.8 = (bf16[128,2048]{1,0:T(8,128)(2,1)S(1)}, bf16[128,2048]{1,0:T(8,128)(2,1)S(1)}, u32[]{:S(2)}, u32[]{:S(2)}) collective-permute-start(bf16[128,2048]{1,0:T(8,128)(2,1)S(1)} %copy-done.2), channel_id=1, source_target_pairs={{0,4},{4,8},{8,12},{12,0},{1,5},{5,9},{9,13},{13,1},{2,6},{6,10},{... | collective-permute-start | bytes 1572872 | tf_op jit(solution)/shard_map/ppermute | solution.py:13
  5.1 13.6 %collective-permute-start.10 = (bf16[128,2048]{1,0:T(8,128)(2,1)S(1)}, bf16[128,2048]{1,0:T(8,128)(2,1)S(1)}, u32[]{:S(2)}, u32[]{:S(2)}) collective-permute-start(bf16[128,2048]{1,0:T(8,128)(2,1)S(1)} %copy-done.2), channel_id=1, source_target_pairs={{0,12},{4,0},{8,4},{12,8},{1,13},{5,1},{9,5},{13,9},{2,14},{6,2},{... | collective-permute-start | bytes 1572872 | tf_op jit(solution)/shard_map/ppermute | solution.py:13
  11.1 15.6 %collective-permute-start.2 = (bf16[96,2048]{1,0:T(8,128)(2,1)S(1)}, bf16[96,2048]{1,0:T(8,128)(2,1)S(1)}, u32[]{:S(2)}, u32[]{:S(2)}) collective-permute-start(bf16[96,2048]{1,0:T(8,128)(2,1)S(1)} %pad_maximum_fusion), channel_id=1, source_target_pairs={{0,32},{32,64},{64,96},{96,128},{128,160},{160,192},{192,224},{224... | collective-permute-start | bytes 1179656 | tf_op jit(solution)/shard_map/ppermute | solution.py:13
  13.1 15.4 %collective-permute-start.3 = (bf16[96,2048]{1,0:T(8,128)(2,1)S(1)}, bf16[96,2048]{1,0:T(8,128)(2,1)S(1)}, u32[]{:S(2)}, u32[]{:S(2)}) collective-permute-start(bf16[96,2048]{1,0:T(8,128)(2,1)S(1)} %pad_maximum_fusion), channel_id=1, source_target_pairs={{0,224},{32,0},{64,32},{96,64},{128,96},{160,128},{192,160},{224,1... | collective-permute-start | bytes 1179656 | tf_op jit(solution)/shard_map/ppermute | solution.py:13
  18.3 8.3 %collective-permute-start.9 = (bf16[64,2048]{1,0:T(8,128)(2,1)S(1)}, bf16[64,2048]{1,0:T(8,128)(2,1)S(1)}, u32[]{:S(2)}, u32[]{:S(2)}) collective-permute-start(bf16[64,2048]{1,0:T(8,128)(2,1)S(1)} %slice.200), channel_id=1, source_target_pairs={{0,4},{4,8},{8,12},{12,0},{1,5},{5,9},{9,13},{13,1},{2,6},{6,10},{... | collective-permute-start | bytes 786440 | tf_op jit(solution)/shard_map/ppermute | solution.py:13
  18.8 7.9 %collective-permute-start.11 = (bf16[64,2048]{1,0:T(8,128)(2,1)S(1)}, bf16[64,2048]{1,0:T(8,128)(2,1)S(1)}, u32[]{:S(2)}, u32[]{:S(2)}) collective-permute-start(bf16[64,2048]{1,0:T(8,128)(2,1)S(1)} %slice.201), channel_id=1, source_target_pairs={{0,12},{4,0},{8,4},{12,8},{1,13},{5,1},{9,5},{13,9},{2,14},{6,2},{... | collective-permute-start | bytes 786440 | tf_op jit(solution)/shard_map/ppermute | solution.py:13
  21.7 13.6 %collective-permute-start.12 = (bf16[128,2048]{1,0:T(8,128)(2,1)S(1)}, bf16[128,2048]{1,0:T(8,128)(2,1)S(1)}, u32[]{:S(2)}, u32[]{:S(2)}) collective-permute-start(bf16[128,2048]{1,0:T(8,128)(2,1)S(1)} %copy-done.2), channel_id=1, source_target_pairs={{0,16},{16,0},{1,17},{17,1},{2,18},{18,2},{3,19},{19,3},{4,20},{20... | collective-permute-start | bytes 1572872 | tf_op jit(solution)/shard_map/ppermute | solution.py:13
  26.8 12.7 %collective-permute-start.4 = (bf16[96,2048]{1,0:T(8,128)(2,1)S(1)}, bf16[96,2048]{1,0:T(8,128)(2,1)S(1)}, u32[]{:S(2)}, u32[]{:S(2)}) collective-permute-start(bf16[96,2048]{1,0:T(8,128)(2,1)S(1)} %collective-permute-done.2), channel_id=1, source_target_pairs={{0,32},{32,64},{64,96},{96,128},{128,160},{160,192},{192,224},{224... | collective-permute-start | bytes 1179656 | tf_op jit(solution)/shard_map/ppermute | solution.py:13
  28.5 11.9 %collective-permute-start.5 = (bf16[96,2048]{1,0:T(8,128)(2,1)S(1)}, bf16[96,2048]{1,0:T(8,128)(2,1)S(1)}, u32[]{:S(2)}, u32[]{:S(2)}) collective-permute-start(bf16[96,2048]{1,0:T(8,128)(2,1)S(1)} %collective-permute-done.3), channel_id=1, source_target_pairs={{0,224},{32,0},{64,32},{96,64},{128,96},{160,128},{192,160},{224,1... | collective-permute-start | bytes 1179656 | tf_op jit(solution)/shard_map/ppermute | solution.py:13
  35.3 12.3 %collective-permute-start.13 = (bf16[128,2048]{1,0:T(8,128)(2,1)S(1)}, bf16[128,2048]{1,0:T(8,128)(2,1)S(1)}, u32[]{:S(2)}, u32[]{:S(2)}) collective-permute-start(bf16[128,2048]{1,0:T(8,128)(2,1)S(1)} %collective-permute-done.12), channel_id=1, source_target_pairs={{0,4},{4,8},{8,12},{12,0},{1,5},{5,9},{9,13},{13,1},{2,6},{6,10},{... | collective-permute-start | bytes 1572872 | tf_op jit(solution)/shard_map/ppermute | solution.py:13
  35.5 12.5 %collective-permute-start.15 = (bf16[128,2048]{1,0:T(8,128)(2,1)S(1)}, bf16[128,2048]{1,0:T(8,128)(2,1)S(1)}, u32[]{:S(2)}, u32[]{:S(2)}) collective-permute-start(bf16[128,2048]{1,0:T(8,128)(2,1)S(1)} %collective-permute-done.12), channel_id=1, source_target_pairs={{0,12},{4,0},{8,4},{12,8},{1,13},{5,1},{9,5},{13,9},{2,14},{6,2},{... | collective-permute-start | bytes 1572872 | tf_op jit(solution)/shard_map/ppermute | solution.py:13
  39.4 11.8 %collective-permute-start.6 = (bf16[96,2048]{1,0:T(8,128)(2,1)S(1)}, bf16[96,2048]{1,0:T(8,128)(2,1)S(1)}, u32[]{:S(2)}, u32[]{:S(2)}) collective-permute-start(bf16[96,2048]{1,0:T(8,128)(2,1)S(1)} %collective-permute-done.4), channel_id=1, source_target_pairs={{0,32},{32,64},{64,96},{96,128},{128,160},{160,192},{192,224},{224... | collective-permute-start | bytes 1179656 | tf_op jit(solution)/shard_map/ppermute | solution.py:13
  40.4 10.9 %collective-permute-start.7 = (bf16[96,2048]{1,0:T(8,128)(2,1)S(1)}, bf16[96,2048]{1,0:T(8,128)(2,1)S(1)}, u32[]{:S(2)}, u32[]{:S(2)}) collective-permute-start(bf16[96,2048]{1,0:T(8,128)(2,1)S(1)} %collective-permute-done.5), channel_id=1, source_target_pairs={{0,224},{32,0},{64,32},{96,64},{128,96},{160,128},{192,160},{224,1... | collective-permute-start | bytes 1179656 | tf_op jit(solution)/shard_map/ppermute | solution.py:13
  47.6 7.8 %collective-permute-start.14 = (bf16[64,2048]{1,0:T(8,128)(2,1)S(1)}, bf16[64,2048]{1,0:T(8,128)(2,1)S(1)}, u32[]{:S(2)}, u32[]{:S(2)}) collective-permute-start(bf16[64,2048]{1,0:T(8,128)(2,1)S(1)} %slice.202), channel_id=1, source_target_pairs={{0,4},{4,8},{8,12},{12,0},{1,5},{5,9},{9,13},{13,1},{2,6},{6,10},{... | collective-permute-start | bytes 786440 | tf_op jit(solution)/shard_map/ppermute | solution.py:13
  48.1 7.4 %collective-permute-start.16 = (bf16[64,2048]{1,0:T(8,128)(2,1)S(1)}, bf16[64,2048]{1,0:T(8,128)(2,1)S(1)}, u32[]{:S(2)}, u32[]{:S(2)}) collective-permute-start(bf16[64,2048]{1,0:T(8,128)(2,1)S(1)} %slice.203), channel_id=1, source_target_pairs={{0,12},{4,0},{8,4},{12,8},{1,13},{5,1},{9,5},{13,9},{2,14},{6,2},{... | collective-permute-start | bytes 786440 | tf_op jit(solution)/shard_map/ppermute | solution.py:13
  58.4 11.4 %collective-permute-start.21 = (bf16[48,2048]{1,0:T(8,128)(2,1)S(1)}, bf16[48,2048]{1,0:T(8,128)(2,1)S(1)}, u32[]{:S(2)}, u32[]{:S(2)}) collective-permute-start(bf16[48,2048]{1,0:T(8,128)(2,1)S(1)} %get-tuple-element.41), channel_id=1, source_target_pairs={{0,32},{32,64},{64,96},{96,128},{128,160},{160,192},{192,224},{224... | collective-permute-start | bytes 589832 | tf_op jit(solution)/shard_map/ppermute | solution.py:13
  60.0 9.8 %collective-permute-start.22 = (bf16[48,2048]{1,0:T(8,128)(2,1)S(1)}, bf16[48,2048]{1,0:T(8,128)(2,1)S(1)}, u32[]{:S(2)}, u32[]{:S(2)}) collective-permute-start(bf16[48,2048]{1,0:T(8,128)(2,1)S(1)} %get-tuple-element.38), channel_id=1, source_target_pairs={{0,224},{32,0},{64,32},{96,64},{128,96},{160,128},{192,160},{224,1... | collective-permute-start | bytes 589832 | tf_op jit(solution)/shard_map/ppermute | solution.py:13
  68.2 6.7 %collective-permute-start.18 = (f16[176,512]{1,0:T(8,128)(2,1)S(1)}, f16[176,512]{1,0:T(8,128)(2,1)S(1)}, u32[]{:S(2)}, u32[]{:S(2)}) collective-permute-start(f16[176,512]{1,0:T(8,128)(2,1)S(1)} %pad_maximum_fusion.4), channel_id=1, source_target_pairs={{0,2},{2,0},{1,3},{3,1},{4,6},{6,4},{5,7},{7,5},{8,10},{10,8},{9,1... | collective-permute-start | bytes 540680 | tf_op jit(solution)/shard_map/ppermute | solution.py:13
  71.5 6.9 %collective-permute-start.23 = (f32[48,1024]{1,0:T(8,128)S(1)}, f32[48,1024]{1,0:T(8,128)S(1)}, u32[]{:S(2)}, u32[]{:S(2)}) collective-permute-start(f32[48,1024]{1,0:T(8,128)S(1)} %slice.221), channel_id=1, source_target_pairs={{0,1},{1,0},{2,3},{3,2},{4,5},{5,4},{6,7},{7,6},{8,9},{9,8},{10,11... | collective-permute-start | bytes 589832 | tf_op jit(solution)/shard_map/ppermute | solution.py:13
  74.9 15.1 %collective-permute-start.20 = (f16[176,512]{1,0:T(8,128)(2,1)S(1)}, f16[176,512]{1,0:T(8,128)(2,1)S(1)}, u32[]{:S(2)}, u32[]{:S(2)}) collective-permute-start(f16[176,512]{1,0:T(8,128)(2,1)S(1)} %pad_maximum_fusion.6), channel_id=1, source_target_pairs={{0,18},{2,16},{16,2},{18,0},{1,19},{3,17},{17,3},{19,1},{4,22},{6,... | collective-permute-start | bytes 540680 | tf_op jit(solution)/shard_map/ppermute | solution.py:95
  75.9 14.1 %collective-permute-start.19 = (f16[176,512]{1,0:T(8,128)(2,1)S(1)}, f16[176,512]{1,0:T(8,128)(2,1)S(1)}, u32[]{:S(2)}, u32[]{:S(2)}) collective-permute-start(f16[176,512]{1,0:T(8,128)(2,1)S(1)} %pad_maximum_fusion.5), channel_id=1, source_target_pairs={{0,16},{16,0},{1,17},{17,1},{2,18},{18,2},{3,19},{19,3},{4,20},{20... | collective-permute-start | bytes 540680 | tf_op jit(solution)/shard_map/ppermute | solution.py:13
  90.3 6.2 %collective-permute-start.29 = (bf16[2,192,128]{2,1,0:T(8,128)(2,1)S(1)}, bf16[2,192,128]{2,1,0:T(8,128)(2,1)S(1)}, u32[]{:S(2)}, u32[]{:S(2)}) collective-permute-start(bf16[2,192,128]{2,1,0:T(8,128)(2,1)S(1)} %get-tuple-element.33), channel_id=1, source_target_pairs={{0,4},{4,8},{8,12},{12,0},{1,5},{5,9},{9,13},{13,1},{2,6},{6,10},{... | collective-permute-start | bytes 294920 | tf_op jit(solution)/shard_map/ppermute | solution.py:13
  90.6 8.4 %collective-permute-start.28 = (bf16[2,192,128]{2,1,0:T(8,128)(2,1)S(1)}, bf16[2,192,128]{2,1,0:T(8,128)(2,1)S(1)}, u32[]{:S(2)}, u32[]{:S(2)}) collective-permute-start(bf16[2,192,128]{2,1,0:T(8,128)(2,1)S(1)} %get-tuple-element.34), channel_id=1, source_target_pairs={{0,8},{4,12},{8,0},{12,4},{1,9},{5,13},{9,1},{13,5},{2,10},{6,14},... | collective-permute-start | bytes 294920 | tf_op jit(solution)/shard_map/ppermute | solution.py:13
  (12 other events, 42.5 us)

commit v3 on v2

v3 whole, which is shorter than its diff:
```python
import jax
import jax.numpy as jnp
from jax import lax
from jax.sharding import Mesh, PartitionSpec as P

AXES = ("z", "h", "x", "l", "k")
SIZES = {"z": 8, "h": 2, "x": 4, "l": 2, "k": 2}
ARRIVAL = (0, -1, 1, -2, 2, -3, 3, 4)


def shift(value, axis, step):
    size = SIZES[axis]
    return lax.ppermute(value, axis, [(i, (i + step) % size) for i in range(size)])


def after(values, others):
    return lax.optimization_barrier((tuple(values), tuple(others)))[0]


def far_of(below, above):
    half = below.shape[0] // 2
    return [shift(below[:half], "x", 1), shift(above[half:], "x", -1)]


def local(amplitudes, integrals, ab_symmetry, cd_symmetry, ij_symmetry):
    rows = amplitudes.shape[0]
    width = integrals.shape[1]
    at = {name: lax.axis_index(name) for name in AXES}
    l, k = at["l"], at["k"]

    first = ((at["z"] * 2 + at["h"]) * 4 + at["x"]) * rows
    slab_labels = lax.dynamic_slice_in_dim(ij_symmetry, first, rows)

    def columns(l, k):
        start = (l * 2 + k) * width
        labels = lax.dynamic_slice_in_dim(cd_symmetry, start, width)
        part = lax.dynamic_slice_in_dim(amplitudes, start, width, axis=1)
        return jnp.where(slab_labels[:, None] == labels[None, :], part, jnp.zeros_like(part))

    def chip_columns(l):
        return jnp.concatenate([columns(l, k), columns(l, 1 - k)], axis=1)

    far = shift(chip_columns(1 - l), "l", 1)
    slabs = jnp.concatenate([chip_columns(l), far], axis=0)

    up, down = [slabs], [slabs]
    for _ in range(3):
        up.append(shift(up[-1], "z", 1))
        down.append(shift(down[-1], "z", -1))
    opposite = lax.optimization_barrier([shift(up[-1][:rows], "z", 1), shift(down[-1][rows:], "z", -1)])
    lines = jnp.concatenate([slabs, up[1], down[1], up[2], down[2], up[3], down[3], *opposite], axis=0)

    below, above = shift(integrals, "x", 1), shift(integrals, "x", -1)
    (block,) = after((integrals,), (below, above))
    other = shift(block, "h", 1)
    middle = far_of(below, above)
    near = jnp.concatenate([integrals, below, *middle, above], axis=0)
    near_there = shift(near, "k", 1)
    (other,) = after((other,), middle)
    below, above = shift(other, "x", 1), shift(other, "x", -1)
    sides = jnp.concatenate([other, below, above], axis=0)
    sides_there = shift(sides, "k", 1)
    middle = jnp.concatenate(far_of(*after((below, above), (near_there,))), axis=0)
    (middle,) = after((middle,), (sides_there,))
    middle_there = shift(middle, "k", 1)

    def product(here, there):
        both = (here, lines[:, :width]), (there, lines[:, width:])
        parts = [
            lax.dot_general(line, block, (((1,), (1,)), ((), ())), preferred_element_type=jnp.float32)
            for block, line in both
        ]
        return (parts[0] + parts[1]).reshape(8, 2, rows, 4 * 128)

    def in_order(sides, middle):
        return jnp.concatenate([sides[:256], middle, sides[256:]], axis=0)

    near = product(near, near_there)
    other = product(in_order(sides, middle), in_order(sides_there, middle_there))

    def packed(summed):
        give = summed.reshape(-1, summed.shape[-1])
        step = jnp.maximum(jnp.max(jnp.abs(give), axis=0, keepdims=True), 1e-30) * (1 / 32512.0)
        power = jnp.ceil(jnp.log2(step) * 128.0)
        give = jnp.round(give * jnp.exp2(power * (-1 / 128.0))).astype(jnp.int16)
        power = jnp.broadcast_to(power, (8, power.shape[1])).astype(jnp.int16)
        return jnp.concatenate([give, power], axis=0)

    def unpacked(got):
        n = got.shape[0] - 8
        got = got.astype(jnp.float32)
        return got[:n] * jnp.exp2(got[n : n + 1] * (1 / 128.0))

    got_l = shift(packed(near[:, 1]), "l", 1)
    got_h = shift(packed(other[:, 0]), "h", 1)
    got_hl = lax.ppermute(packed(other[:, 1]), ("h", "l"), [(0, 3), (1, 2), (2, 1), (3, 0)])
    own = near[:, 0].reshape(-1, 4 * 128) + unpacked(got_l)
    result = jnp.stack([own, unpacked(got_h) + unpacked(got_hl)]).astype(jnp.bfloat16)
    home = [result[:, :, :128]]
    home += [shift(result[:, :, dx * 128 : dx * 128 + 128], "x", -dx) for dx in (1, 2, 3)]
    out = jnp.stack(home).reshape(4, 2, 8, rows, 128)
    order = [ARRIVAL.index(d if d < 5 else d - 8) for d in range(8)]
    out = out[:, :, jnp.array(order)].transpose(2, 1, 0, 3, 4)
    out = jnp.roll(out, (at["z"], at["h"], at["x"]), axis=(0, 1, 2)).reshape(64 * rows, 128)
    keep = ij_symmetry[:, None] == ab_symmetry[None, :]
    return jnp.where(keep, out, jnp.zeros_like(out))


def solution(mesh):
    fine = Mesh(mesh.devices.reshape(tuple(SIZES.values())), AXES)
    ab, cd = ("z", "h", "x"), ("l", "k")
    placed = (P(cd + ab, None), P(ab, cd), P(ab), P(), P(cd))
    return jax.shard_map(
        local, mesh=fine, in_specs=placed, out_specs=P(cd, ab), check_vma=False
    )
```

time: 104 us -> 92 us (0.88); the launches traced: 103 us -> 91.7 us
  starting transfers between devices: 52 us -> 36.7 us
  waiting for transfers between devices: 34.6 us -> 39.7 us
  matrix products: 7.99 us -> 5.24 us
  other arithmetic: 3.82 us -> 5.46 us
    ppermute x28 -> x26, starting transfers between devices: 49.8 us -> 36.4 us  [shift(): lax.ppermute(value, axis, [(i, (i + step) % size) for i in range(size)])]
    ppermute x2 -> x1, waiting for transfers between devices: 1.67 us -> 8.67 us  [local(): lax.ppermute(packed(other[:, 1]), ('h', 'l'), [(0, 3), (1, 2), (2, 1), (3...]
    dot_general x3 -> x4, matrix products: 7.99 us -> 5.24 us  [product(): lax.dot_general(line, block, (((1,), (1,)), ((), ())), preferred_element_...]
    ppermute x28 -> x26, waiting for transfers between devices: 33 us -> 31.1 us  [shift(): lax.ppermute(value, axis, [(i, (i + step) % size) for i in range(size)])]
    ppermute x2 -> x1, starting transfers between devices: 2.21 us -> 0.31 us  [local(): lax.ppermute(packed(other[:, 1]), ('h', 'l'), [(0, 3), (1, 2), (2, 1), (3...]
    select_n x0 -> x1, other arithmetic: none -> 1.2 us  [columns(): jnp.where(slab_labels[:, None] == labels[None, :], part, jnp.zeros_like(p...]
    unnamed x1, other arithmetic: 1.2 us -> 0.01 us
  transfers between devices with their start and end apart: 30 -> 27, of which waited for: 16 -> 13; matrix products, arithmetic and copies ran while one was open for 7% -> 9% of each run, Pallas kernels for 0% -> 0%
where the time goes in v3:
time: 92 us; the launch traced here: 91.7 us
  waiting for transfers between devices  39.7 us (43%)
  starting transfers between devices  36.7 us (40%)
  other arithmetic  5.46 us (6%)
  matrix products  5.24 us (6%)
  local copies, waits for them, and re-layouts  3.88 us (4%)
    ppermute x26, starting transfers between devices, shift(): lax.ppermute(value, axis, [(i, (i + step) % size) for i in range(size)])  36.4 us
    ppermute x26, waiting for transfers between devices, shift(): lax.ppermute(value, axis, [(i, (i + step) % size) for i in range(size)])  31.1 us
    ppermute x1, waiting for transfers between devices, local(): lax.ppermute(packed(other[:, 1]), ('h', 'l'), [(0, 3), (1, 2), (2, 1), (3...  8.67 us
    dot_general x4, matrix products, product(): lax.dot_general(line, block, (((1,), (1,)), ((), ())), preferred_element_...  5.24 us
  transfers between devices with their start and end apart: 27, of which 13 were waited for; matrix products, arithmetic and copies ran while one was open for 9% of the time, Pallas kernels for 0%

profile of v3, /device:TPU:24, one launch (start us, length us, event | category | flops | bytes accessed | tf_op | source)
XLA Modules:
  0.0 91.7 jit_solution(15214407837155471058)
XLA Ops:
  0.0 1.5 %collective-permute-start.9 = (bf16[128,2048]{1,0:T(8,128)(2,1)}, bf16[128,2048]{1,0:T(8,128)(2,1)S(1)}, u32[]{:S(2)}, u32[]{:S(2)}) collective-permute-start(bf16[128,2048]{1,0:T(8,128)(2,1)} %param.7), channel_id=1, source_target_pairs={{0,4},{4,8},{8,12},{12,0},{1,5},{5,9},{9,13},{13,1},{2,6},{6,10},{... | collective-permute-start | bytes 1572872 | tf_op jit(solution)/shard_map/ppermute | solution.py:13
  1.5 1.7 %collective-permute-start.11 = (bf16[128,2048]{1,0:T(8,128)(2,1)}, bf16[128,2048]{1,0:T(8,128)(2,1)S(1)}, u32[]{:S(2)}, u32[]{:S(2)}) collective-permute-start(bf16[128,2048]{1,0:T(8,128)(2,1)} %param.7), channel_id=1, source_target_pairs={{0,12},{4,0},{8,4},{12,8},{1,13},{5,1},{9,5},{13,9},{2,14},{6,2},{... | collective-permute-start | bytes 1572872 | tf_op jit(solution)/shard_map/ppermute | solution.py:13
  7.9 4.2 %collective-permute-done = bf16[24,4096]{1,0:T(8,128)(2,1)S(1)} collective-permute-done((bf16[24,4096]{1,0:T(8,128)(2,1)S(1)}, bf16[24,4096]{1,0:T(8,128)(2,1)S(1)}, u32[]{:S(2)}, u32[]{:S(2)}) %collective-permute-start) | collective-permute-done | bytes 196640 | tf_op jit(solution)/shard_map/ppermute | solution.py:13
  12.2 2.0 %collective-permute-start.1 = (bf16[48,4096]{1,0:T(8,128)(2,1)S(1)}, bf16[48,4096]{1,0:T(8,128)(2,1)S(1)}, u32[]{:S(2)}, u32[]{:S(2)}) collective-permute-start(bf16[48,4096]{1,0:T(8,128)(2,1)S(1)} %pad_maximum_fusion.2), channel_id=1, source_target_pairs={{0,32},{32,64},{64,96},{96,128},{128,160},{160,192},{192,224},{224... | collective-permute-start | bytes 1179656 | tf_op jit(solution)/shard_map/ppermute | solution.py:13
  14.2 4.0 %collective-permute-start.2 = (bf16[48,4096]{1,0:T(8,128)(2,1)S(1)}, bf16[48,4096]{1,0:T(8,128)(2,1)S(1)}, u32[]{:S(2)}, u32[]{:S(2)}) collective-permute-start(bf16[48,4096]{1,0:T(8,128)(2,1)S(1)} %pad_maximum_fusion.2), channel_id=1, source_target_pairs={{0,224},{32,0},{64,32},{96,64},{128,96},{160,128},{192,160},{224,1... | collective-permute-start | bytes 1179656 | tf_op jit(solution)/shard_map/ppermute | solution.py:13
  18.6 3.0 %collective-permute-start.12 = (bf16[64,2048]{1,0:T(8,128)(2,1)S(1)}, bf16[64,2048]{1,0:T(8,128)(2,1)S(1)}, u32[]{:S(2)}, u32[]{:S(2)}) collective-permute-start(bf16[64,2048]{1,0:T(8,128)(2,1)S(1)} %slice.106), channel_id=1, source_target_pairs={{0,12},{4,0},{8,4},{12,8},{1,13},{5,1},{9,5},{13,9},{2,14},{6,2},{... | collective-permute-start | bytes 786440 | tf_op jit(solution)/shard_map/ppermute | solution.py:13
  22.9 2.8 %collective-permute-done.1 = bf16[48,4096]{1,0:T(8,128)(2,1)S(1)} collective-permute-done((bf16[48,4096]{1,0:T(8,128)(2,1)S(1)}, bf16[48,4096]{1,0:T(8,128)(2,1)S(1)}, u32[]{:S(2)}, u32[]{:S(2)}) %collective-permute-start.1) | collective-permute-done | bytes 393248 | tf_op jit(solution)/shard_map/ppermute | solution.py:13
  25.8 3.3 %collective-permute-start.4 = (bf16[48,4096]{1,0:T(8,128)(2,1)S(1)}, bf16[48,4096]{1,0:T(8,128)(2,1)S(1)}, u32[]{:S(2)}, u32[]{:S(2)}) collective-permute-start(bf16[48,4096]{1,0:T(8,128)(2,1)S(1)} %collective-permute-done.2), channel_id=1, source_target_pairs={{0,224},{32,0},{64,32},{96,64},{128,96},{160,128},{192,160},{224,1... | collective-permute-start | bytes 1179656 | tf_op jit(solution)/shard_map/ppermute | solution.py:13
  29.3 6.3 %collective-permute-done.3 = bf16[48,4096]{1,0:T(8,128)(2,1)S(1)} collective-permute-done((bf16[48,4096]{1,0:T(8,128)(2,1)S(1)}, bf16[48,4096]{1,0:T(8,128)(2,1)S(1)}, u32[]{:S(2)}, u32[]{:S(2)}) %collective-permute-start.3) | collective-permute-done | bytes 393248 | tf_op jit(solution)/shard_map/ppermute | solution.py:13
  35.7 3.3 %collective-permute-start.6 = (bf16[48,4096]{1,0:T(8,128)(2,1)S(1)}, bf16[48,4096]{1,0:T(8,128)(2,1)S(1)}, u32[]{:S(2)}, u32[]{:S(2)}) collective-permute-start(bf16[48,4096]{1,0:T(8,128)(2,1)S(1)} %collective-permute-done.4), channel_id=1, source_target_pairs={{0,224},{32,0},{64,32},{96,64},{128,96},{160,128},{192,160},{224,1... | collective-permute-start | bytes 1179656 | tf_op jit(solution)/shard_map/ppermute | solution.py:13
  39.1 1.6 %collective-permute-start.17 = (bf16[128,2048]{1,0:T(8,128)(2,1)S(1)}, bf16[128,2048]{1,0:T(8,128)(2,1)S(1)}, u32[]{:S(2)}, u32[]{:S(2)}) collective-permute-start(bf16[128,2048]{1,0:T(8,128)(2,1)S(1)} %collective-permute-done.15), channel_id=1, source_target_pairs={{0,12},{4,0},{8,4},{12,8},{1,13},{5,1},{9,5},{13,9},{2,14},{6,2},{... | collective-permute-start | bytes 1572872 | tf_op jit(solution)/shard_map/ppermute | solution.py:13
  41.2 3.8 %collective-permute-done.5 = bf16[48,4096]{1,0:T(8,128)(2,1)S(1)} collective-permute-done((bf16[48,4096]{1,0:T(8,128)(2,1)S(1)}, bf16[48,4096]{1,0:T(8,128)(2,1)S(1)}, u32[]{:S(2)}, u32[]{:S(2)}) %collective-permute-start.5) | collective-permute-done | bytes 393248 | tf_op jit(solution)/shard_map/ppermute | solution.py:13
  45.3 3.4 %collective-permute-start.8 = (bf16[24,4096]{1,0:T(8,128)(2,1)S(1)}, bf16[24,4096]{1,0:T(8,128)(2,1)S(1)}, u32[]{:S(2)}, u32[]{:S(2)}) collective-permute-start(bf16[24,4096]{1,0:T(8,128)(2,1)S(1)} %slice.103), channel_id=1, source_target_pairs={{0,224},{32,0},{64,32},{96,64},{128,96},{160,128},{192,160},{224,1... | collective-permute-start | bytes 589832 | tf_op jit(solution)/shard_map/ppermute | solution.py:13
  49.2 2.5 %collective-permute-done.16 = bf16[128,2048]{1,0:T(8,128)(2,1)S(1)} collective-permute-done((bf16[128,2048]{1,0:T(8,128)(2,1)S(1)}, bf16[128,2048]{1,0:T(8,128)(2,1)S(1)}, u32[]{:S(2)}, u32[]{:S(2)}) %collective-permute-start.16) | collective-permute-done | bytes 524320 | tf_op jit(solution)/shard_map/ppermute | solution.py:13
  52.2 1.6 %collective-permute-start.19 = (bf16[64,2048]{1,0:T(8,128)(2,1)S(1)}, bf16[64,2048]{1,0:T(8,128)(2,1)S(1)}, u32[]{:S(2)}, u32[]{:S(2)}) collective-permute-start(bf16[64,2048]{1,0:T(8,128)(2,1)S(1)} %slice.87), channel_id=1, source_target_pairs={{0,12},{4,0},{8,4},{12,8},{1,13},{5,1},{9,5},{13,9},{2,14},{6,2},{... | collective-permute-start | bytes 786440 | tf_op jit(solution)/shard_map/ppermute | solution.py:13
  58.1 2.7 %collective-permute-done.19 = bf16[64,2048]{1,0:T(8,128)(2,1)S(1)} collective-permute-done((bf16[64,2048]{1,0:T(8,128)(2,1)S(1)}, bf16[64,2048]{1,0:T(8,128)(2,1)S(1)}, u32[]{:S(2)}, u32[]{:S(2)}) %collective-permute-start.19) | collective-permute-done | bytes 262176 | tf_op jit(solution)/shard_map/ppermute | solution.py:13
  60.8 1.3 %collective-permute-done.18 = bf16[64,2048]{1,0:T(8,128)(2,1)S(1)} collective-permute-done((bf16[64,2048]{1,0:T(8,128)(2,1)S(1)}, bf16[64,2048]{1,0:T(8,128)(2,1)S(1)}, u32[]{:S(2)}, u32[]{:S(2)}) %collective-permute-start.18) | collective-permute-done | bytes 262176 | tf_op jit(solution)/shard_map/ppermute | solution.py:13
  62.3 2.0 %collective-permute-done.14 = s16[200,512]{1,0:T(8,128)(2,1)} collective-permute-done((s16[200,512]{1,0:T(8,128)(2,1)}, s16[200,512]{1,0:T(8,128)(2,1)}, u32[]{:S(2)}, u32[]{:S(2)}) %collective-permute-start.14) | collective-permute-done | bytes 204832 | tf_op jit(solution)/shard_map/ppermute | solution.py:13
  65.7 2.1 %fusion.8 = f32[384,512]{1,0:T(8,128)S(1)} fusion(bf16[128,2048]{1,0:T(8,128)(2,1)S(1)} %slice.113, bf16[128,2048]{1,0:T(8,128)(2,1)} %collective-permute-done.21, bf16[256,2048]{1,0:T(8,128)(2,1)S(1)} %slice.112, bf16[384,4096]{1,0:T(8,128)(2,1)S(1)} %copy-done.4), kind=kOutput, calls=%fused_computation.9 | convolution fusion | flops 811597824 | bytes 4456448 | tf_op jit(solution)/shard_map/dot_general | solution.py:70
  69.6 2.7 %collective-permute-start.22 = (s16[200,512]{1,0:T(8,128)(2,1)S(1)}, s16[200,512]{1,0:T(8,128)(2,1)S(1)}, u32[]{:S(2)}, u32[]{:S(2)}) collective-permute-start(s16[200,512]{1,0:T(8,128)(2,1)S(1)} %pad_add_fusion.1), channel_id=1, source_target_pairs={{0,16},{16,0},{1,17},{17,1},{2,18},{18,2},{3,19},{19,3},{4,20},{20... | collective-permute-start | bytes 614408 | tf_op jit(solution)/shard_map/ppermute | solution.py:13
  72.2 8.7 %collective-permute-done.23 = s16[200,512]{1,0:T(8,128)(2,1)S(1)} collective-permute-done((s16[200,512]{1,0:T(8,128)(2,1)S(1)}, s16[200,512]{1,0:T(8,128)(2,1)S(1)}, u32[]{:S(2)}, u32[]{:S(2)}) %collective-permute-start.23) | collective-permute-done | bytes 204832 | tf_op jit(solution)/shard_map/ppermute | solution.py:96
  81.8 1.3 %collective-permute-start.25 = (bf16[2,192,128]{2,1,0:T(8,128)(2,1)S(1)}, bf16[2,192,128]{2,1,0:T(8,128)(2,1)S(1)}, u32[]{:S(2)}, u32[]{:S(2)}) collective-permute-start(bf16[2,192,128]{2,1,0:T(8,128)(2,1)S(1)} %get-tuple-element.33), channel_id=1, source_target_pairs={{0,8},{4,12},{8,0},{12,4},{1,9},{5,13},{9,1},{13,5},{2,10},{6,14},... | collective-permute-start | bytes 294920 | tf_op jit(solution)/shard_map/ppermute | solution.py:13
  83.1 1.7 %collective-permute-start.24 = (bf16[2,192,128]{2,1,0:T(8,128)(2,1)S(1)}, bf16[2,192,128]{2,1,0:T(8,128)(2,1)S(1)}, u32[]{:S(2)}, u32[]{:S(2)}) collective-permute-start(bf16[2,192,128]{2,1,0:T(8,128)(2,1)S(1)} %get-tuple-element.31), channel_id=1, source_target_pairs={{0,12},{4,0},{8,4},{12,8},{1,13},{5,1},{9,5},{13,9},{2,14},{6,2},{... | collective-permute-start | bytes 294920 | tf_op jit(solution)/shard_map/ppermute | solution.py:13
  84.8 4.0 %collective-permute-done.26 = bf16[2,192,128]{2,1,0:T(8,128)(2,1)S(1)} collective-permute-done((bf16[2,192,128]{2,1,0:T(8,128)(2,1)S(1)}, bf16[2,192,128]{2,1,0:T(8,128)(2,1)S(1)}, u32[]{:S(2)}, u32[]{:S(2)}) %collective-permute-start.26) | collective-permute-done | bytes 98336 | tf_op jit(solution)/shard_map/ppermute | solution.py:13
  (111 shorter events, 19.4 us)
Async XLA Ops:
  0.0 18.2 %collective-permute-start.9 = (bf16[128,2048]{1,0:T(8,128)(2,1)}, bf16[128,2048]{1,0:T(8,128)(2,1)S(1)}, u32[]{:S(2)}, u32[]{:S(2)}) collective-permute-start(bf16[128,2048]{1,0:T(8,128)(2,1)} %param.7), channel_id=1, source_target_pairs={{0,4},{4,8},{8,12},{12,0},{1,5},{5,9},{9,13},{13,1},{2,6},{6,10},{... | collective-permute-start | bytes 1572872 | tf_op jit(solution)/shard_map/ppermute | solution.py:13
  1.5 17.1 %collective-permute-start.11 = (bf16[128,2048]{1,0:T(8,128)(2,1)}, bf16[128,2048]{1,0:T(8,128)(2,1)S(1)}, u32[]{:S(2)}, u32[]{:S(2)}) collective-permute-start(bf16[128,2048]{1,0:T(8,128)(2,1)} %param.7), channel_id=1, source_target_pairs={{0,12},{4,0},{8,4},{12,8},{1,13},{5,1},{9,5},{13,9},{2,14},{6,2},{... | collective-permute-start | bytes 1572872 | tf_op jit(solution)/shard_map/ppermute | solution.py:13
  12.2 13.6 %collective-permute-start.1 = (bf16[48,4096]{1,0:T(8,128)(2,1)S(1)}, bf16[48,4096]{1,0:T(8,128)(2,1)S(1)}, u32[]{:S(2)}, u32[]{:S(2)}) collective-permute-start(bf16[48,4096]{1,0:T(8,128)(2,1)S(1)} %pad_maximum_fusion.2), channel_id=1, source_target_pairs={{0,32},{32,64},{64,96},{96,128},{128,160},{160,192},{192,224},{224... | collective-permute-start | bytes 1179656 | tf_op jit(solution)/shard_map/ppermute | solution.py:13
  14.2 11.6 %collective-permute-start.2 = (bf16[48,4096]{1,0:T(8,128)(2,1)S(1)}, bf16[48,4096]{1,0:T(8,128)(2,1)S(1)}, u32[]{:S(2)}, u32[]{:S(2)}) collective-permute-start(bf16[48,4096]{1,0:T(8,128)(2,1)S(1)} %pad_maximum_fusion.2), channel_id=1, source_target_pairs={{0,224},{32,0},{64,32},{96,64},{128,96},{160,128},{192,160},{224,1... | collective-permute-start | bytes 1179656 | tf_op jit(solution)/shard_map/ppermute | solution.py:13
  18.3 10.9 %collective-permute-start.10 = (bf16[64,2048]{1,0:T(8,128)(2,1)S(1)}, bf16[64,2048]{1,0:T(8,128)(2,1)S(1)}, u32[]{:S(2)}, u32[]{:S(2)}) collective-permute-start(bf16[64,2048]{1,0:T(8,128)(2,1)S(1)} %slice.105), channel_id=1, source_target_pairs={{0,4},{4,8},{8,12},{12,0},{1,5},{5,9},{9,13},{13,1},{2,6},{6,10},{... | collective-permute-start | bytes 786440 | tf_op jit(solution)/shard_map/ppermute | solution.py:13
  18.6 10.5 %collective-permute-start.12 = (bf16[64,2048]{1,0:T(8,128)(2,1)S(1)}, bf16[64,2048]{1,0:T(8,128)(2,1)S(1)}, u32[]{:S(2)}, u32[]{:S(2)}) collective-permute-start(bf16[64,2048]{1,0:T(8,128)(2,1)S(1)} %slice.106), channel_id=1, source_target_pairs={{0,12},{4,0},{8,4},{12,8},{1,13},{5,1},{9,5},{13,9},{2,14},{6,2},{... | collective-permute-start | bytes 786440 | tf_op jit(solution)/shard_map/ppermute | solution.py:13
  21.7 17.4 %collective-permute-start.15 = (bf16[128,2048]{1,0:T(8,128)(2,1)S(1)}, bf16[128,2048]{1,0:T(8,128)(2,1)S(1)}, u32[]{:S(2)}, u32[]{:S(2)}) collective-permute-start(bf16[128,2048]{1,0:T(8,128)(2,1)S(1)} %copy-done), channel_id=1, source_target_pairs={{0,16},{16,0},{1,17},{17,1},{2,18},{18,2},{3,19},{19,3},{4,20},{20... | collective-permute-start | bytes 1572872 | tf_op jit(solution)/shard_map/ppermute | solution.py:13
  25.7 9.9 %collective-permute-start.3 = (bf16[48,4096]{1,0:T(8,128)(2,1)S(1)}, bf16[48,4096]{1,0:T(8,128)(2,1)S(1)}, u32[]{:S(2)}, u32[]{:S(2)}) collective-permute-start(bf16[48,4096]{1,0:T(8,128)(2,1)S(1)} %collective-permute-done.1), channel_id=1, source_target_pairs={{0,32},{32,64},{64,96},{96,128},{128,160},{160,192},{192,224},{224... | collective-permute-start | bytes 1179656 | tf_op jit(solution)/shard_map/ppermute | solution.py:13
  25.8 9.9 %collective-permute-start.4 = (bf16[48,4096]{1,0:T(8,128)(2,1)S(1)}, bf16[48,4096]{1,0:T(8,128)(2,1)S(1)}, u32[]{:S(2)}, u32[]{:S(2)}) collective-permute-start(bf16[48,4096]{1,0:T(8,128)(2,1)S(1)} %collective-permute-done.2), channel_id=1, source_target_pairs={{0,224},{32,0},{64,32},{96,64},{128,96},{160,128},{192,160},{224,1... | collective-permute-start | bytes 1179656 | tf_op jit(solution)/shard_map/ppermute | solution.py:13
  29.2 22.9 %collective-permute-start.13 = (bf16[512,2048]{1,0:T(8,128)(2,1)S(1)}, bf16[512,2048]{1,0:T(8,128)(2,1)S(1)}, u32[]{:S(2)}, u32[]{:S(2)}) collective-permute-start(bf16[512,2048]{1,0:T(8,128)(2,1)S(1)} %constant_dynamic-update-slice_fusion.9), channel_id=1, source_target_pairs={{0,1},{1,0},{2,3},{3,2},{4,5},{5,4},{6,7},{7,6},{8,9},{9,8},{10,11... | collective-permute-start | bytes 6291464 | tf_op jit(solution)/shard_map/ppermute | solution.py:13
  35.7 9.3 %collective-permute-start.5 = (bf16[48,4096]{1,0:T(8,128)(2,1)S(1)}, bf16[48,4096]{1,0:T(8,128)(2,1)S(1)}, u32[]{:S(2)}, u32[]{:S(2)}) collective-permute-start(bf16[48,4096]{1,0:T(8,128)(2,1)S(1)} %collective-permute-done.3), channel_id=1, source_target_pairs={{0,32},{32,64},{64,96},{96,128},{128,160},{160,192},{192,224},{224... | collective-permute-start | bytes 1179656 | tf_op jit(solution)/shard_map/ppermute | solution.py:13
  35.7 9.5 %collective-permute-start.6 = (bf16[48,4096]{1,0:T(8,128)(2,1)S(1)}, bf16[48,4096]{1,0:T(8,128)(2,1)S(1)}, u32[]{:S(2)}, u32[]{:S(2)}) collective-permute-start(bf16[48,4096]{1,0:T(8,128)(2,1)S(1)} %collective-permute-done.4), channel_id=1, source_target_pairs={{0,224},{32,0},{64,32},{96,64},{128,96},{160,128},{192,160},{224,1... | collective-permute-start | bytes 1179656 | tf_op jit(solution)/shard_map/ppermute | solution.py:13
  39.1 10.1 %collective-permute-start.17 = (bf16[128,2048]{1,0:T(8,128)(2,1)S(1)}, bf16[128,2048]{1,0:T(8,128)(2,1)S(1)}, u32[]{:S(2)}, u32[]{:S(2)}) collective-permute-start(bf16[128,2048]{1,0:T(8,128)(2,1)S(1)} %collective-permute-done.15), channel_id=1, source_target_pairs={{0,12},{4,0},{8,4},{12,8},{1,13},{5,1},{9,5},{13,9},{2,14},{6,2},{... | collective-permute-start | bytes 1572872 | tf_op jit(solution)/shard_map/ppermute | solution.py:13
  40.7 11.0 %collective-permute-start.16 = (bf16[128,2048]{1,0:T(8,128)(2,1)S(1)}, bf16[128,2048]{1,0:T(8,128)(2,1)S(1)}, u32[]{:S(2)}, u32[]{:S(2)}) collective-permute-start(bf16[128,2048]{1,0:T(8,128)(2,1)S(1)} %collective-permute-done.15), channel_id=1, source_target_pairs={{0,4},{4,8},{8,12},{12,0},{1,5},{5,9},{9,13},{13,1},{2,6},{6,10},{... | collective-permute-start | bytes 1572872 | tf_op jit(solution)/shard_map/ppermute | solution.py:13
  45.0 7.1 %collective-permute-start.7 = (bf16[24,4096]{1,0:T(8,128)(2,1)S(1)}, bf16[24,4096]{1,0:T(8,128)(2,1)S(1)}, u32[]{:S(2)}, u32[]{:S(2)}) collective-permute-start(bf16[24,4096]{1,0:T(8,128)(2,1)S(1)} %slice.102), channel_id=1, source_target_pairs={{0,32},{32,64},{64,96},{96,128},{128,160},{160,192},{192,224},{224... | collective-permute-start | bytes 589832 | tf_op jit(solution)/shard_map/ppermute | solution.py:13
  45.3 6.8 %collective-permute-start.8 = (bf16[24,4096]{1,0:T(8,128)(2,1)S(1)}, bf16[24,4096]{1,0:T(8,128)(2,1)S(1)}, u32[]{:S(2)}, u32[]{:S(2)}) collective-permute-start(bf16[24,4096]{1,0:T(8,128)(2,1)S(1)} %slice.103), channel_id=1, source_target_pairs={{0,224},{32,0},{64,32},{96,64},{128,96},{160,128},{192,160},{224,1... | collective-permute-start | bytes 589832 | tf_op jit(solution)/shard_map/ppermute | solution.py:13
  51.8 10.4 %collective-permute-start.20 = (bf16[384,2048]{1,0:T(8,128)(2,1)S(1)}, bf16[384,2048]{1,0:T(8,128)(2,1)S(1)}, u32[]{:S(2)}, u32[]{:S(2)}) collective-permute-start(bf16[384,2048]{1,0:T(8,128)(2,1)S(1)} %pad_maximum_fusion), channel_id=1, source_target_pairs={{0,1},{1,0},{2,3},{3,2},{4,5},{5,4},{6,7},{7,6},{8,9},{9,8},{10,11... | collective-permute-start | bytes 4718600 | tf_op jit(solution)/shard_map/ppermute | solution.py:13
  52.2 8.6 %collective-permute-start.19 = (bf16[64,2048]{1,0:T(8,128)(2,1)S(1)}, bf16[64,2048]{1,0:T(8,128)(2,1)S(1)}, u32[]{:S(2)}, u32[]{:S(2)}) collective-permute-start(bf16[64,2048]{1,0:T(8,128)(2,1)S(1)} %slice.87), channel_id=1, source_target_pairs={{0,12},{4,0},{8,4},{12,8},{1,13},{5,1},{9,5},{13,9},{2,14},{6,2},{... | collective-permute-start | bytes 786440 | tf_op jit(solution)/shard_map/ppermute | solution.py:13
  53.8 8.3 %collective-permute-start.18 = (bf16[64,2048]{1,0:T(8,128)(2,1)S(1)}, bf16[64,2048]{1,0:T(8,128)(2,1)S(1)}, u32[]{:S(2)}, u32[]{:S(2)}) collective-permute-start(bf16[64,2048]{1,0:T(8,128)(2,1)S(1)} %slice.86), channel_id=1, source_target_pairs={{0,4},{4,8},{8,12},{12,0},{1,5},{5,9},{9,13},{13,1},{2,6},{6,10},{... | collective-permute-start | bytes 786440 | tf_op jit(solution)/shard_map/ppermute | solution.py:13
  57.3 7.1 %collective-permute-start.14 = (s16[200,512]{1,0:T(8,128)(2,1)}, s16[200,512]{1,0:T(8,128)(2,1)}, u32[]{:S(2)}, u32[]{:S(2)}) collective-permute-start(s16[200,512]{1,0:T(8,128)(2,1)} %pad_add_fusion), channel_id=1, source_target_pairs={{0,2},{2,0},{1,3},{3,1},{4,6},{6,4},{5,7},{7,5},{8,10},{10,8},{9,1... | collective-permute-start | bytes 614408 | tf_op jit(solution)/shard_map/ppermute | solution.py:13
  69.1 11.8 %collective-permute-start.23 = (s16[200,512]{1,0:T(8,128)(2,1)S(1)}, s16[200,512]{1,0:T(8,128)(2,1)S(1)}, u32[]{:S(2)}, u32[]{:S(2)}) collective-permute-start(s16[200,512]{1,0:T(8,128)(2,1)S(1)} %pad_add_fusion.2), channel_id=1, source_target_pairs={{0,18},{2,16},{16,2},{18,0},{1,19},{3,17},{17,3},{19,1},{4,22},{6,... | collective-permute-start | bytes 614408 | tf_op jit(solution)/shard_map/ppermute | solution.py:96
  69.6 11.4 %collective-permute-start.22 = (s16[200,512]{1,0:T(8,128)(2,1)S(1)}, s16[200,512]{1,0:T(8,128)(2,1)S(1)}, u32[]{:S(2)}, u32[]{:S(2)}) collective-permute-start(s16[200,512]{1,0:T(8,128)(2,1)S(1)} %pad_add_fusion.1), channel_id=1, source_target_pairs={{0,16},{16,0},{1,17},{17,1},{2,18},{18,2},{3,19},{19,3},{4,20},{20... | collective-permute-start | bytes 614408 | tf_op jit(solution)/shard_map/ppermute | solution.py:13
  81.3 7.5 %collective-permute-start.26 = (bf16[2,192,128]{2,1,0:T(8,128)(2,1)S(1)}, bf16[2,192,128]{2,1,0:T(8,128)(2,1)S(1)}, u32[]{:S(2)}, u32[]{:S(2)}) collective-permute-start(bf16[2,192,128]{2,1,0:T(8,128)(2,1)S(1)} %get-tuple-element.32), channel_id=1, source_target_pairs={{0,4},{4,8},{8,12},{12,0},{1,5},{5,9},{9,13},{13,1},{2,6},{6,10},{... | collective-permute-start | bytes 294920 | tf_op jit(solution)/shard_map/ppermute | solution.py:13
  81.8 7.0 %collective-permute-start.25 = (bf16[2,192,128]{2,1,0:T(8,128)(2,1)S(1)}, bf16[2,192,128]{2,1,0:T(8,128)(2,1)S(1)}, u32[]{:S(2)}, u32[]{:S(2)}) collective-permute-start(bf16[2,192,128]{2,1,0:T(8,128)(2,1)S(1)} %get-tuple-element.33), channel_id=1, source_target_pairs={{0,8},{4,12},{8,0},{12,4},{1,9},{5,13},{9,1},{13,5},{2,10},{6,14},... | collective-permute-start | bytes 294920 | tf_op jit(solution)/shard_map/ppermute | solution.py:13
  (11 other events, 94.5 us)

commit v4 on v3

--- a/solution.py
+++ b/solution.py
@@ -40,7 +40,8 @@
     def chip_columns(l):
         return jnp.concatenate([columns(l, k), columns(l, 1 - k)], axis=1)
 
-    far = shift(chip_columns(1 - l), "l", 1)
+    give = chip_columns(1 - l)
+    far = shift(give, "l", 1)
     slabs = jnp.concatenate([chip_columns(l), far], axis=0)
 
     up, down = [slabs], [slabs]
@@ -50,21 +51,22 @@
     opposite = lax.optimization_barrier([shift(up[-1][:rows], "z", 1), shift(down[-1][rows:], "z", -1)])
     lines = jnp.concatenate([slabs, up[1], down[1], up[2], down[2], up[3], down[3], *opposite], axis=0)
 
-    below, above = shift(integrals, "x", 1), shift(integrals, "x", -1)
-    (block,) = after((integrals,), (below, above))
+    (block,) = after((integrals,), (give,))
+    below, above = shift(block, "x", 1), shift(block, "x", -1)
+    (block,) = after((integrals,), (far,))
     other = shift(block, "h", 1)
     middle = far_of(below, above)
-    near = jnp.concatenate([integrals, below, *middle, above], axis=0)
+    middle = jnp.concatenate(middle, axis=0)
+    near = jnp.concatenate([integrals, below, middle, above], axis=0)
     near_there = shift(near, "k", 1)
-    (other,) = after((other,), middle)
+    (other,) = after((other,), (middle,))
+    middle = shift(middle, "h", 1)
     below, above = shift(other, "x", 1), shift(other, "x", -1)
     sides = jnp.concatenate([other, below, above], axis=0)
     sides_there = shift(sides, "k", 1)
-    middle = jnp.concatenate(far_of(*after((below, above), (near_there,))), axis=0)
-    (middle,) = after((middle,), (sides_there,))
     middle_there = shift(middle, "k", 1)
 
-    def product(here, there):
+    def product(lines, here, there):
         both = (here, lines[:, :width]), (there, lines[:, width:])
         parts = [
             lax.dot_general(line, block, (((1,), (1,)), ((), ())), preferred_element_type=jnp.float32)
@@ -75,8 +77,7 @@
     def in_order(sides, middle):
         return jnp.concatenate([sides[:256], middle, sides[256:]], axis=0)
 
-    near = product(near, near_there)
-    other = product(in_order(sides, middle), in_order(sides_there, middle_there))
+    other = product(lines, in_order(sides, middle), in_order(sides_there, middle_there))
 
     def packed(summed):
         give = summed.reshape(-1, summed.shape[-1])
@@ -91,9 +92,11 @@
         got = got.astype(jnp.float32)
         return got[:n] * jnp.exp2(got[n : n + 1] * (1 / 128.0))
 
+    to_h, to_hl = packed(other[:, 0]), packed(other[:, 1])
+    near = product(after((lines,), (to_h, to_hl))[0], near, near_there)
     got_l = shift(packed(near[:, 1]), "l", 1)
-    got_h = shift(packed(other[:, 0]), "h", 1)
-    got_hl = lax.ppermute(packed(other[:, 1]), ("h", "l"), [(0, 3), (1, 2), (2, 1), (3, 0)])
+    got_h = shift(to_h, "h", 1)
+    got_hl = lax.ppermute(to_hl, ("h", "l"), [(0, 3), (1, 2), (2, 1), (3, 0)])
     own = near[:, 0].reshape(-1, 4 * 128) + unpacked(got_l)
     result = jnp.stack([own, unpacked(got_h) + unpacked(got_hl)]).astype(jnp.bfloat16)
     home = [result[:, :, :128]]

time: 92 us -> 83.4 us (0.907); the launches traced: 91.7 us -> 81.8 us
  waiting for transfers between devices: 39.7 us -> 27.2 us
  local copies, waits for them, and re-layouts: 3.88 us -> 7.66 us
  matrix products: 5.24 us -> 4.03 us
  starting transfers between devices: 36.7 us -> 37.9 us
  other arithmetic: 5.46 us -> 4.53 us
    ppermute x26 -> x25, waiting for transfers between devices: 31.1 us -> 23.3 us  [shift(): lax.ppermute(value, axis, [(i, (i + step) % size) for i in range(size)])]
    ppermute x1, waiting for transfers between devices: 8.67 us -> 3.96 us  [local(): got_hl = lax.ppermute(to_hl, ('h', 'l'), [(0, 3), (1, 2), (2, 1), (3, 0)])]
    unnamed x28 -> x22, local copies, waits for them, and re-layouts: 1.38 us -> 5.13 us
    ppermute x1, starting transfers between devices: 0.31 us -> 2.85 us  [local(): got_hl = lax.ppermute(to_hl, ('h', 'l'), [(0, 3), (1, 2), (2, 1), (3, 0)])]
    ppermute x26 -> x25, starting transfers between devices: 36.4 us -> 35 us  [shift(): lax.ppermute(value, axis, [(i, (i + step) % size) for i in range(size)])]
    dot_general x4, matrix products: 5.24 us -> 4.03 us  [product(): lax.dot_general(line, block, (((1,), (1,)), ((), ())), preferred_element_...]
    convert_element_type x3, other arithmetic: 1.11 us -> 0.18 us  [unpacked(): got = got.astype(jnp.float32)]
  transfers between devices with their start and end apart: 27 -> 26, of which waited for: 13 -> 12; matrix products, arithmetic and copies ran while one was open for 9% -> 13% of each run, Pallas kernels for 0% -> 0%
where the time goes in v4:
time: 83.4 us; the launch traced here: 81.8 us
  starting transfers between devices  37.9 us (45%)
  waiting for transfers between devices  27.2 us (33%)
  local copies, waits for them, and re-layouts  7.66 us (9%)
  other arithmetic  4.53 us (5%)
  matrix products  4.03 us (5%)
    ppermute x25, starting transfers between devices, shift(): lax.ppermute(value, axis, [(i, (i + step) % size) for i in range(size)])  35 us
    ppermute x25, waiting for transfers between devices, shift(): lax.ppermute(value, axis, [(i, (i + step) % size) for i in range(size)])  23.3 us
    unnamed x22, local copies, waits for them, and re-layouts  5.13 us
    dot_general x4, matrix products, product(): lax.dot_general(line, block, (((1,), (1,)), ((), ())), preferred_element_...  4.03 us
    ppermute x1, waiting for transfers between devices, local(): got_hl = lax.ppermute(to_hl, ('h', 'l'), [(0, 3), (1, 2), (2, 1), (3, 0)])  3.96 us
    ppermute x1, starting transfers between devices, local(): got_hl = lax.ppermute(to_hl, ('h', 'l'), [(0, 3), (1, 2), (2, 1), (3, 0)])  2.85 us
  transfers between devices with their start and end apart: 26, of which 12 were waited for; matrix products, arithmetic and copies ran while one was open for 13% of the time, Pallas kernels for 0%

profile of v4, /device:TPU:24, one launch (start us, length us, event | category | flops | bytes accessed | tf_op | source)
XLA Modules:
  0.0 81.8 jit_solution(7020864515720689778)
XLA Ops:
  1.6 1.2 %compare_select_fusion.4 = (bf16[24,2048]{1,0:T(8,128)(2,1)S(1)}, bf16[24,2048]{1,0:T(8,128)(2,1)S(1)}, bf16[24,2048]{1,0:T(8,128)(2,1)S(1)}, bf16[24,2048]{1,0:T(8,128)(2,1)S(1)}) fusion(bf16[24,8192]{1,0:T(8,128)(2,1)} %param.6, s32[]{:T(128)S(6)} %select_n.73, s32[2048]{0:T(1024)S(1)} %get-tuple-element.36, s32[24]{0:T(128)S(1)} %dynamic_slice.39, ...), kind=kLoop, calls=%fused_computation.70 | loop fusion | flops 393216 | bytes 819312 | tf_op jit(solution)/shard_map/jit(_where)/select_n | solution.py:38
  3.6 1.5 %collective-permute-start.10 = (bf16[128,2048]{1,0:T(8,128)(2,1)}, bf16[128,2048]{1,0:T(8,128)(2,1)S(1)}, u32[]{:S(2)}, u32[]{:S(2)}) collective-permute-start(bf16[128,2048]{1,0:T(8,128)(2,1)} %param.7), channel_id=1, source_target_pairs={{0,4},{4,8},{8,12},{12,0},{1,5},{5,9},{9,13},{13,1},{2,6},{6,10},{... | collective-permute-start | bytes 1572872 | tf_op jit(solution)/shard_map/ppermute | solution.py:13
  5.1 1.7 %collective-permute-start.12 = (bf16[128,2048]{1,0:T(8,128)(2,1)}, bf16[128,2048]{1,0:T(8,128)(2,1)S(1)}, u32[]{:S(2)}, u32[]{:S(2)}) collective-permute-start(bf16[128,2048]{1,0:T(8,128)(2,1)} %param.7), channel_id=1, source_target_pairs={{0,12},{4,0},{8,4},{12,8},{1,13},{5,1},{9,5},{13,9},{2,14},{6,2},{... | collective-permute-start | bytes 1572872 | tf_op jit(solution)/shard_map/ppermute | solution.py:13
  9.6 2.0 %collective-permute-start.1 = (bf16[48,4096]{1,0:T(8,128)(2,1)S(1)}, bf16[48,4096]{1,0:T(8,128)(2,1)S(1)}, u32[]{:S(2)}, u32[]{:S(2)}) collective-permute-start(bf16[48,4096]{1,0:T(8,128)(2,1)S(1)} %pad_maximum_fusion.1), channel_id=1, source_target_pairs={{0,32},{32,64},{64,96},{96,128},{128,160},{160,192},{192,224},{224... | collective-permute-start | bytes 1179656 | tf_op jit(solution)/shard_map/ppermute | solution.py:13
  11.6 4.0 %collective-permute-start.2 = (bf16[48,4096]{1,0:T(8,128)(2,1)S(1)}, bf16[48,4096]{1,0:T(8,128)(2,1)S(1)}, u32[]{:S(2)}, u32[]{:S(2)}) collective-permute-start(bf16[48,4096]{1,0:T(8,128)(2,1)S(1)} %pad_maximum_fusion.1), channel_id=1, source_target_pairs={{0,224},{32,0},{64,32},{96,64},{128,96},{160,128},{192,160},{224,1... | collective-permute-start | bytes 1179656 | tf_op jit(solution)/shard_map/ppermute | solution.py:13
  15.6 1.2 %collective-permute-start.9 = (bf16[128,2048]{1,0:T(8,128)(2,1)S(1)}, bf16[128,2048]{1,0:T(8,128)(2,1)S(1)}, u32[]{:S(2)}, u32[]{:S(2)}) collective-permute-start(bf16[128,2048]{1,0:T(8,128)(2,1)S(1)} %copy-done), channel_id=1, source_target_pairs={{0,16},{16,0},{1,17},{17,1},{2,18},{18,2},{3,19},{19,3},{4,20},{20... | collective-permute-start | bytes 1572872 | tf_op jit(solution)/shard_map/ppermute | solution.py:13
  19.1 2.8 %collective-permute-start.13 = (bf16[64,2048]{1,0:T(8,128)(2,1)S(1)}, bf16[64,2048]{1,0:T(8,128)(2,1)S(1)}, u32[]{:S(2)}, u32[]{:S(2)}) collective-permute-start(bf16[64,2048]{1,0:T(8,128)(2,1)S(1)} %slice.104), channel_id=1, source_target_pairs={{0,12},{4,0},{8,4},{12,8},{1,13},{5,1},{9,5},{13,9},{2,14},{6,2},{... | collective-permute-start | bytes 786440 | tf_op jit(solution)/shard_map/ppermute | solution.py:13
  21.9 1.8 %collective-permute-done.1 = bf16[48,4096]{1,0:T(8,128)(2,1)S(1)} collective-permute-done((bf16[48,4096]{1,0:T(8,128)(2,1)S(1)}, bf16[48,4096]{1,0:T(8,128)(2,1)S(1)}, u32[]{:S(2)}, u32[]{:S(2)}) %collective-permute-start.1) | collective-permute-done | bytes 393248 | tf_op jit(solution)/shard_map/ppermute | solution.py:13
  24.7 3.9 %collective-permute-start.4 = (bf16[48,4096]{1,0:T(8,128)(2,1)S(1)}, bf16[48,4096]{1,0:T(8,128)(2,1)S(1)}, u32[]{:S(2)}, u32[]{:S(2)}) collective-permute-start(bf16[48,4096]{1,0:T(8,128)(2,1)S(1)} %collective-permute-done.2), channel_id=1, source_target_pairs={{0,224},{32,0},{64,32},{96,64},{128,96},{160,128},{192,160},{224,1... | collective-permute-start | bytes 1179656 | tf_op jit(solution)/shard_map/ppermute | solution.py:13
  29.6 1.5 %collective-permute-start.14 = (bf16[128,2048]{1,0:T(8,128)(2,1)S(1)}, bf16[128,2048]{1,0:T(8,128)(2,1)S(1)}, u32[]{:S(2)}, u32[]{:S(2)}) collective-permute-start(bf16[128,2048]{1,0:T(8,128)(2,1)S(1)} %collective-permute-done.9), channel_id=1, source_target_pairs={{0,4},{4,8},{8,12},{12,0},{1,5},{5,9},{9,13},{13,1},{2,6},{6,10},{... | collective-permute-start | bytes 1572872 | tf_op jit(solution)/shard_map/ppermute | solution.py:13
  31.1 1.8 %collective-permute-start.16 = (bf16[128,2048]{1,0:T(8,128)(2,1)S(1)}, bf16[128,2048]{1,0:T(8,128)(2,1)S(1)}, u32[]{:S(2)}, u32[]{:S(2)}) collective-permute-start(bf16[128,2048]{1,0:T(8,128)(2,1)S(1)} %collective-permute-done.9), channel_id=1, source_target_pairs={{0,12},{4,0},{8,4},{12,8},{1,13},{5,1},{9,5},{13,9},{2,14},{6,2},{... | collective-permute-start | bytes 1572872 | tf_op jit(solution)/shard_map/ppermute | solution.py:13
  32.9 1.2 %collective-permute-start.15 = (bf16[128,2048]{1,0:T(8,128)(2,1)S(1)}, bf16[128,2048]{1,0:T(8,128)(2,1)S(1)}, u32[]{:S(2)}, u32[]{:S(2)}) collective-permute-start(bf16[128,2048]{1,0:T(8,128)(2,1)S(1)} %get-tuple-element.33), channel_id=1, source_target_pairs={{0,16},{16,0},{1,17},{17,1},{2,18},{18,2},{3,19},{19,3},{4,20},{20... | collective-permute-start | bytes 1572872 | tf_op jit(solution)/shard_map/ppermute | solution.py:13
  36.0 3.2 %collective-permute-start.6 = (bf16[48,4096]{1,0:T(8,128)(2,1)S(1)}, bf16[48,4096]{1,0:T(8,128)(2,1)S(1)}, u32[]{:S(2)}, u32[]{:S(2)}) collective-permute-start(bf16[48,4096]{1,0:T(8,128)(2,1)S(1)} %collective-permute-done.4), channel_id=1, source_target_pairs={{0,224},{32,0},{64,32},{96,64},{128,96},{160,128},{192,160},{224,1... | collective-permute-start | bytes 1179656 | tf_op jit(solution)/shard_map/ppermute | solution.py:13
  40.0 2.5 %collective-permute-done.14 = bf16[128,2048]{1,0:T(8,128)(2,1)S(1)} collective-permute-done((bf16[128,2048]{1,0:T(8,128)(2,1)S(1)}, bf16[128,2048]{1,0:T(8,128)(2,1)S(1)}, u32[]{:S(2)}, u32[]{:S(2)}) %collective-permute-start.14) | collective-permute-done | bytes 524320 | tf_op jit(solution)/shard_map/ppermute | solution.py:13
  43.3 2.2 %collective-permute-done.15 = bf16[128,2048]{1,0:T(8,128)(2,1)S(1)} collective-permute-done((bf16[128,2048]{1,0:T(8,128)(2,1)S(1)}, bf16[128,2048]{1,0:T(8,128)(2,1)S(1)}, u32[]{:S(2)}, u32[]{:S(2)}) %collective-permute-start.15) | collective-permute-done | bytes 524320 | tf_op jit(solution)/shard_map/ppermute | solution.py:13
  45.6 3.3 %collective-permute-start.8 = (bf16[24,4096]{1,0:T(8,128)(2,1)S(1)}, bf16[24,4096]{1,0:T(8,128)(2,1)S(1)}, u32[]{:S(2)}, u32[]{:S(2)}) collective-permute-start(bf16[24,4096]{1,0:T(8,128)(2,1)S(1)} %slice.101), channel_id=1, source_target_pairs={{0,224},{32,0},{64,32},{96,64},{128,96},{160,128},{192,160},{224,1... | collective-permute-start | bytes 589832 | tf_op jit(solution)/shard_map/ppermute | solution.py:13
  49.0 5.1 %collective-permute-done.7 = bf16[24,4096]{1,0:T(8,128)(2,1)S(1)} collective-permute-done((bf16[24,4096]{1,0:T(8,128)(2,1)S(1)}, bf16[24,4096]{1,0:T(8,128)(2,1)S(1)}, u32[]{:S(2)}, u32[]{:S(2)}) %collective-permute-start.7) | collective-permute-done | bytes 196640 | tf_op jit(solution)/shard_map/ppermute | solution.py:13
  56.7 1.2 %collective-permute-start.21 = (s16[200,512]{1,0:T(8,128)(2,1)S(1)}, s16[200,512]{1,0:T(8,128)(2,1)S(1)}, u32[]{:S(2)}, u32[]{:S(2)}) collective-permute-start(s16[200,512]{1,0:T(8,128)(2,1)S(1)} %get-tuple-element.46), channel_id=1, source_target_pairs={{0,16},{16,0},{1,17},{17,1},{2,18},{18,2},{3,19},{19,3},{4,20},{20... | collective-permute-start | bytes 614408 | tf_op jit(solution)/shard_map/ppermute | solution.py:13
  57.9 2.8 %collective-permute-start.22 = (s16[200,512]{1,0:T(8,128)(2,1)S(1)}, s16[200,512]{1,0:T(8,128)(2,1)S(1)}, u32[]{:S(2)}, u32[]{:S(2)}) collective-permute-start(s16[200,512]{1,0:T(8,128)(2,1)S(1)} %get-tuple-element.47), channel_id=1, source_target_pairs={{0,18},{2,16},{16,2},{18,0},{1,19},{3,17},{17,3},{19,1},{4,22},{6,... | collective-permute-start | bytes 614408 | tf_op jit(solution)/shard_map/ppermute | solution.py:99
  63.1 2.2 %collective-permute-done.21 = s16[200,512]{1,0:T(8,128)(2,1)S(1)} collective-permute-done((s16[200,512]{1,0:T(8,128)(2,1)S(1)}, s16[200,512]{1,0:T(8,128)(2,1)S(1)}, u32[]{:S(2)}, u32[]{:S(2)}) %collective-permute-start.21) | collective-permute-done | bytes 204832 | tf_op jit(solution)/shard_map/ppermute | solution.py:13
  65.4 4.0 %collective-permute-done.22 = s16[200,512]{1,0:T(8,128)(2,1)S(1)} collective-permute-done((s16[200,512]{1,0:T(8,128)(2,1)S(1)}, s16[200,512]{1,0:T(8,128)(2,1)S(1)}, u32[]{:S(2)}, u32[]{:S(2)}) %collective-permute-start.22) | collective-permute-done | bytes 204832 | tf_op jit(solution)/shard_map/ppermute | solution.py:99
  69.8 1.6 %collective-permute-start.23 = (bf16[2,192,128]{2,1,0:T(8,128)(2,1)S(1)}, bf16[2,192,128]{2,1,0:T(8,128)(2,1)S(1)}, u32[]{:S(2)}, u32[]{:S(2)}) collective-permute-start(bf16[2,192,128]{2,1,0:T(8,128)(2,1)S(1)} %get-tuple-element.29), channel_id=1, source_target_pairs={{0,12},{4,0},{8,4},{12,8},{1,13},{5,1},{9,5},{13,9},{2,14},{6,2},{... | collective-permute-start | bytes 294920 | tf_op jit(solution)/shard_map/ppermute | solution.py:13
  73.0 2.5 %collective-permute-done.23 = bf16[2,192,128]{2,1,0:T(8,128)(2,1)S(1)} collective-permute-done((bf16[2,192,128]{2,1,0:T(8,128)(2,1)S(1)}, bf16[2,192,128]{2,1,0:T(8,128)(2,1)S(1)}, u32[]{:S(2)}, u32[]{:S(2)}) %collective-permute-start.23) | collective-permute-done | bytes 98336 | tf_op jit(solution)/shard_map/ppermute | solution.py:13
  75.6 2.9 %collective-permute-done.24 = bf16[2,192,128]{2,1,0:T(8,128)(2,1)S(1)} collective-permute-done((bf16[2,192,128]{2,1,0:T(8,128)(2,1)S(1)}, bf16[2,192,128]{2,1,0:T(8,128)(2,1)S(1)}, u32[]{:S(2)}, u32[]{:S(2)}) %collective-permute-start.24) | collective-permute-done | bytes 98336 | tf_op jit(solution)/shard_map/ppermute | solution.py:13
  (99 shorter events, 23.1 us)
Async XLA Ops:
  2.8 6.7 %collective-permute-start = (bf16[24,4096]{1,0:T(8,128)(2,1)S(1)}, bf16[24,4096]{1,0:T(8,128)(2,1)S(1)}, u32[]{:S(2)}, u32[]{:S(2)}) collective-permute-start(bf16[24,4096]{1,0:T(8,128)(2,1)S(1)} %pad_maximum_fusion.3), channel_id=1, source_target_pairs={{0,2},{2,0},{1,3},{3,1},{4,6},{6,4},{5,7},{7,5},{8,10},{10,8},{9,1... | collective-permute-start | bytes 589832 | tf_op jit(solution)/shard_map/ppermute | solution.py:13
  3.6 14.8 %collective-permute-start.10 = (bf16[128,2048]{1,0:T(8,128)(2,1)}, bf16[128,2048]{1,0:T(8,128)(2,1)S(1)}, u32[]{:S(2)}, u32[]{:S(2)}) collective-permute-start(bf16[128,2048]{1,0:T(8,128)(2,1)} %param.7), channel_id=1, source_target_pairs={{0,4},{4,8},{8,12},{12,0},{1,5},{5,9},{9,13},{13,1},{2,6},{6,10},{... | collective-permute-start | bytes 1572872 | tf_op jit(solution)/shard_map/ppermute | solution.py:13
  5.1 14.0 %collective-permute-start.12 = (bf16[128,2048]{1,0:T(8,128)(2,1)}, bf16[128,2048]{1,0:T(8,128)(2,1)S(1)}, u32[]{:S(2)}, u32[]{:S(2)}) collective-permute-start(bf16[128,2048]{1,0:T(8,128)(2,1)} %param.7), channel_id=1, source_target_pairs={{0,12},{4,0},{8,4},{12,8},{1,13},{5,1},{9,5},{13,9},{2,14},{6,2},{... | collective-permute-start | bytes 1572872 | tf_op jit(solution)/shard_map/ppermute | solution.py:13
  9.6 14.2 %collective-permute-start.1 = (bf16[48,4096]{1,0:T(8,128)(2,1)S(1)}, bf16[48,4096]{1,0:T(8,128)(2,1)S(1)}, u32[]{:S(2)}, u32[]{:S(2)}) collective-permute-start(bf16[48,4096]{1,0:T(8,128)(2,1)S(1)} %pad_maximum_fusion.1), channel_id=1, source_target_pairs={{0,32},{32,64},{64,96},{96,128},{128,160},{160,192},{192,224},{224... | collective-permute-start | bytes 1179656 | tf_op jit(solution)/shard_map/ppermute | solution.py:13
  11.6 13.2 %collective-permute-start.2 = (bf16[48,4096]{1,0:T(8,128)(2,1)S(1)}, bf16[48,4096]{1,0:T(8,128)(2,1)S(1)}, u32[]{:S(2)}, u32[]{:S(2)}) collective-permute-start(bf16[48,4096]{1,0:T(8,128)(2,1)S(1)} %pad_maximum_fusion.1), channel_id=1, source_target_pairs={{0,224},{32,0},{64,32},{96,64},{128,96},{160,128},{192,160},{224,1... | collective-permute-start | bytes 1179656 | tf_op jit(solution)/shard_map/ppermute | solution.py:13
  15.6 14.0 %collective-permute-start.9 = (bf16[128,2048]{1,0:T(8,128)(2,1)S(1)}, bf16[128,2048]{1,0:T(8,128)(2,1)S(1)}, u32[]{:S(2)}, u32[]{:S(2)}) collective-permute-start(bf16[128,2048]{1,0:T(8,128)(2,1)S(1)} %copy-done), channel_id=1, source_target_pairs={{0,16},{16,0},{1,17},{17,1},{2,18},{18,2},{3,19},{19,3},{4,20},{20... | collective-permute-start | bytes 1572872 | tf_op jit(solution)/shard_map/ppermute | solution.py:13
  18.5 11.0 %collective-permute-start.11 = (bf16[64,2048]{1,0:T(8,128)(2,1)S(1)}, bf16[64,2048]{1,0:T(8,128)(2,1)S(1)}, u32[]{:S(2)}, u32[]{:S(2)}) collective-permute-start(bf16[64,2048]{1,0:T(8,128)(2,1)S(1)} %slice.103), channel_id=1, source_target_pairs={{0,4},{4,8},{8,12},{12,0},{1,5},{5,9},{9,13},{13,1},{2,6},{6,10},{... | collective-permute-start | bytes 786440 | tf_op jit(solution)/shard_map/ppermute | solution.py:13
  19.1 10.4 %collective-permute-start.13 = (bf16[64,2048]{1,0:T(8,128)(2,1)S(1)}, bf16[64,2048]{1,0:T(8,128)(2,1)S(1)}, u32[]{:S(2)}, u32[]{:S(2)}) collective-permute-start(bf16[64,2048]{1,0:T(8,128)(2,1)S(1)} %slice.104), channel_id=1, source_target_pairs={{0,12},{4,0},{8,4},{12,8},{1,13},{5,1},{9,5},{13,9},{2,14},{6,2},{... | collective-permute-start | bytes 786440 | tf_op jit(solution)/shard_map/ppermute | solution.py:13
  23.7 11.5 %collective-permute-start.3 = (bf16[48,4096]{1,0:T(8,128)(2,1)S(1)}, bf16[48,4096]{1,0:T(8,128)(2,1)S(1)}, u32[]{:S(2)}, u32[]{:S(2)}) collective-permute-start(bf16[48,4096]{1,0:T(8,128)(2,1)S(1)} %collective-permute-done.1), channel_id=1, source_target_pairs={{0,32},{32,64},{64,96},{96,128},{128,160},{160,192},{192,224},{224... | collective-permute-start | bytes 1179656 | tf_op jit(solution)/shard_map/ppermute | solution.py:13
  24.7 11.3 %collective-permute-start.4 = (bf16[48,4096]{1,0:T(8,128)(2,1)S(1)}, bf16[48,4096]{1,0:T(8,128)(2,1)S(1)}, u32[]{:S(2)}, u32[]{:S(2)}) collective-permute-start(bf16[48,4096]{1,0:T(8,128)(2,1)S(1)} %collective-permute-done.2), channel_id=1, source_target_pairs={{0,224},{32,0},{64,32},{96,64},{128,96},{160,128},{192,160},{224,1... | collective-permute-start | bytes 1179656 | tf_op jit(solution)/shard_map/ppermute | solution.py:13
  29.6 12.9 %collective-permute-start.14 = (bf16[128,2048]{1,0:T(8,128)(2,1)S(1)}, bf16[128,2048]{1,0:T(8,128)(2,1)S(1)}, u32[]{:S(2)}, u32[]{:S(2)}) collective-permute-start(bf16[128,2048]{1,0:T(8,128)(2,1)S(1)} %collective-permute-done.9), channel_id=1, source_target_pairs={{0,4},{4,8},{8,12},{12,0},{1,5},{5,9},{9,13},{13,1},{2,6},{6,10},{... | collective-permute-start | bytes 1572872 | tf_op jit(solution)/shard_map/ppermute | solution.py:13
  31.1 11.4 %collective-permute-start.16 = (bf16[128,2048]{1,0:T(8,128)(2,1)S(1)}, bf16[128,2048]{1,0:T(8,128)(2,1)S(1)}, u32[]{:S(2)}, u32[]{:S(2)}) collective-permute-start(bf16[128,2048]{1,0:T(8,128)(2,1)S(1)} %collective-permute-done.9), channel_id=1, source_target_pairs={{0,12},{4,0},{8,4},{12,8},{1,13},{5,1},{9,5},{13,9},{2,14},{6,2},{... | collective-permute-start | bytes 1572872 | tf_op jit(solution)/shard_map/ppermute | solution.py:13
  32.9 12.6 %collective-permute-start.15 = (bf16[128,2048]{1,0:T(8,128)(2,1)S(1)}, bf16[128,2048]{1,0:T(8,128)(2,1)S(1)}, u32[]{:S(2)}, u32[]{:S(2)}) collective-permute-start(bf16[128,2048]{1,0:T(8,128)(2,1)S(1)} %get-tuple-element.33), channel_id=1, source_target_pairs={{0,16},{16,0},{1,17},{17,1},{2,18},{18,2},{3,19},{19,3},{4,20},{20... | collective-permute-start | bytes 1572872 | tf_op jit(solution)/shard_map/ppermute | solution.py:13
  35.2 10.3 %collective-permute-start.5 = (bf16[48,4096]{1,0:T(8,128)(2,1)S(1)}, bf16[48,4096]{1,0:T(8,128)(2,1)S(1)}, u32[]{:S(2)}, u32[]{:S(2)}) collective-permute-start(bf16[48,4096]{1,0:T(8,128)(2,1)S(1)} %collective-permute-done.3), channel_id=1, source_target_pairs={{0,32},{32,64},{64,96},{96,128},{128,160},{160,192},{192,224},{224... | collective-permute-start | bytes 1179656 | tf_op jit(solution)/shard_map/ppermute | solution.py:13
  36.0 9.6 %collective-permute-start.6 = (bf16[48,4096]{1,0:T(8,128)(2,1)S(1)}, bf16[48,4096]{1,0:T(8,128)(2,1)S(1)}, u32[]{:S(2)}, u32[]{:S(2)}) collective-permute-start(bf16[48,4096]{1,0:T(8,128)(2,1)S(1)} %collective-permute-done.4), channel_id=1, source_target_pairs={{0,224},{32,0},{64,32},{96,64},{128,96},{160,128},{192,160},{224,1... | collective-permute-start | bytes 1179656 | tf_op jit(solution)/shard_map/ppermute | solution.py:13
  42.5 18.2 %collective-permute-start.19 = (bf16[512,2048]{1,0:T(8,128)(2,1)S(1)}, bf16[512,2048]{1,0:T(8,128)(2,1)S(1)}, u32[]{:S(2)}, u32[]{:S(2)}) collective-permute-start(bf16[512,2048]{1,0:T(8,128)(2,1)S(1)} %constant_dynamic-update-slice_fusion.11), channel_id=1, source_target_pairs={{0,1},{1,0},{2,3},{3,2},{4,5},{5,4},{6,7},{7,6},{8,9},{9,8},{10,11... | collective-permute-start | bytes 6291464 | tf_op jit(solution)/shard_map/ppermute | solution.py:13
  42.7 12.5 %collective-permute-start.17 = (bf16[384,2048]{1,0:T(8,128)(2,1)S(1)}, bf16[384,2048]{1,0:T(8,128)(2,1)S(1)}, u32[]{:S(2)}, u32[]{:S(2)}) collective-permute-start(bf16[384,2048]{1,0:T(8,128)(2,1)S(1)} %pad_maximum_fusion), channel_id=1, source_target_pairs={{0,1},{1,0},{2,3},{3,2},{4,5},{5,4},{6,7},{7,6},{8,9},{9,8},{10,11... | collective-permute-start | bytes 4718600 | tf_op jit(solution)/shard_map/ppermute | solution.py:13
  45.5 9.9 %collective-permute-start.18 = (bf16[128,2048]{1,0:T(8,128)(2,1)S(1)}, bf16[128,2048]{1,0:T(8,128)(2,1)S(1)}, u32[]{:S(2)}, u32[]{:S(2)}) collective-permute-start(bf16[128,2048]{1,0:T(8,128)(2,1)S(1)} %collective-permute-done.15), channel_id=1, source_target_pairs={{0,1},{1,0},{2,3},{3,2},{4,5},{5,4},{6,7},{7,6},{8,9},{9,8},{10,11... | collective-permute-start | bytes 1572872 | tf_op jit(solution)/shard_map/ppermute | solution.py:13
  45.5 8.6 %collective-permute-start.7 = (bf16[24,4096]{1,0:T(8,128)(2,1)S(1)}, bf16[24,4096]{1,0:T(8,128)(2,1)S(1)}, u32[]{:S(2)}, u32[]{:S(2)}) collective-permute-start(bf16[24,4096]{1,0:T(8,128)(2,1)S(1)} %slice.100), channel_id=1, source_target_pairs={{0,32},{32,64},{64,96},{96,128},{128,160},{160,192},{192,224},{224... | collective-permute-start | bytes 589832 | tf_op jit(solution)/shard_map/ppermute | solution.py:13
  45.6 8.5 %collective-permute-start.8 = (bf16[24,4096]{1,0:T(8,128)(2,1)S(1)}, bf16[24,4096]{1,0:T(8,128)(2,1)S(1)}, u32[]{:S(2)}, u32[]{:S(2)}) collective-permute-start(bf16[24,4096]{1,0:T(8,128)(2,1)S(1)} %slice.101), channel_id=1, source_target_pairs={{0,224},{32,0},{64,32},{96,64},{128,96},{160,128},{192,160},{224,1... | collective-permute-start | bytes 589832 | tf_op jit(solution)/shard_map/ppermute | solution.py:13
  56.7 8.6 %collective-permute-start.21 = (s16[200,512]{1,0:T(8,128)(2,1)S(1)}, s16[200,512]{1,0:T(8,128)(2,1)S(1)}, u32[]{:S(2)}, u32[]{:S(2)}) collective-permute-start(s16[200,512]{1,0:T(8,128)(2,1)S(1)} %get-tuple-element.46), channel_id=1, source_target_pairs={{0,16},{16,0},{1,17},{17,1},{2,18},{18,2},{3,19},{19,3},{4,20},{20... | collective-permute-start | bytes 614408 | tf_op jit(solution)/shard_map/ppermute | solution.py:13
  57.9 11.5 %collective-permute-start.22 = (s16[200,512]{1,0:T(8,128)(2,1)S(1)}, s16[200,512]{1,0:T(8,128)(2,1)S(1)}, u32[]{:S(2)}, u32[]{:S(2)}) collective-permute-start(s16[200,512]{1,0:T(8,128)(2,1)S(1)} %get-tuple-element.47), channel_id=1, source_target_pairs={{0,18},{2,16},{16,2},{18,0},{1,19},{3,17},{17,3},{19,1},{4,22},{6,... | collective-permute-start | bytes 614408 | tf_op jit(solution)/shard_map/ppermute | solution.py:99
  71.4 7.0 %collective-permute-start.24 = (bf16[2,192,128]{2,1,0:T(8,128)(2,1)S(1)}, bf16[2,192,128]{2,1,0:T(8,128)(2,1)S(1)}, u32[]{:S(2)}, u32[]{:S(2)}) collective-permute-start(bf16[2,192,128]{2,1,0:T(8,128)(2,1)S(1)} %get-tuple-element.31), channel_id=1, source_target_pairs={{0,8},{4,12},{8,0},{12,4},{1,9},{5,13},{9,1},{13,5},{2,10},{6,14},... | collective-permute-start | bytes 294920 | tf_op jit(solution)/shard_map/ppermute | solution.py:13
  72.2 7.3 %collective-permute-start.25 = (bf16[2,192,128]{2,1,0:T(8,128)(2,1)S(1)}, bf16[2,192,128]{2,1,0:T(8,128)(2,1)S(1)}, u32[]{:S(2)}, u32[]{:S(2)}) collective-permute-start(bf16[2,192,128]{2,1,0:T(8,128)(2,1)S(1)} %get-tuple-element.30), channel_id=1, source_target_pairs={{0,4},{4,8},{8,12},{12,0},{1,5},{5,9},{9,13},{13,1},{2,6},{6,10},{... | collective-permute-start | bytes 294920 | tf_op jit(solution)/shard_map/ppermute | solution.py:13
  (7 other events, 69.0 us)

commit v5 on v4

--- a/solution.py
+++ b/solution.py
@@ -5,7 +5,6 @@
 
 AXES = ("z", "h", "x", "l", "k")
 SIZES = {"z": 8, "h": 2, "x": 4, "l": 2, "k": 2}
-ARRIVAL = (0, -1, 1, -2, 2, -3, 3, 4)
 
 
 def shift(value, axis, step):
@@ -42,27 +41,33 @@
 
     give = chip_columns(1 - l)
     far = shift(give, "l", 1)
-    slabs = jnp.concatenate([chip_columns(l), far], axis=0)
+    mine = chip_columns(l)
+    slabs = jnp.concatenate([mine, far], axis=0)
 
     up, down = [slabs], [slabs]
     for _ in range(3):
         up.append(shift(up[-1], "z", 1))
         down.append(shift(down[-1], "z", -1))
-    opposite = lax.optimization_barrier([shift(up[-1][:rows], "z", 1), shift(down[-1][rows:], "z", -1)])
-    lines = jnp.concatenate([slabs, up[1], down[1], up[2], down[2], up[3], down[3], *opposite], axis=0)
+    opposite = [shift(up[-1][:rows], "z", 1), shift(down[-1][rows:], "z", -1)]
+    opposite = lax.optimization_barrier(opposite)
+    lines = jnp.zeros((8, 2 * rows, 2 * width), amplitudes.dtype)
+    blocks = [slabs, up[1], down[1], up[2], down[2], up[3], down[3], jnp.concatenate(opposite, axis=0)]
+    for step, block in zip((0, -1, 1, -2, 2, -3, 3, 4), blocks):
+        lines = lax.dynamic_update_index_in_dim(lines, block, (at["z"] + step) % 8, 0)
+    lines = lines.reshape(16 * rows, 2 * width)
 
-    (block,) = after((integrals,), (give,))
+    masked = integrals
+    (block,) = after((masked,), (give,))
     below, above = shift(block, "x", 1), shift(block, "x", -1)
-    (block,) = after((integrals,), (far,))
+    (block,) = after((masked,), (far,))
     other = shift(block, "h", 1)
-    middle = far_of(below, above)
-    middle = jnp.concatenate(middle, axis=0)
-    near = jnp.concatenate([integrals, below, middle, above], axis=0)
-    near_there = shift(near, "k", 1)
+    middle = jnp.concatenate(far_of(below, above), axis=0)
+    near = jnp.concatenate([masked, below, middle, above], axis=0)
     (other,) = after((other,), (middle,))
     middle = shift(middle, "h", 1)
     below, above = shift(other, "x", 1), shift(other, "x", -1)
     sides = jnp.concatenate([other, below, above], axis=0)
+    near_there = shift(near, "k", 1)
     sides_there = shift(sides, "k", 1)
     middle_there = shift(middle, "k", 1)
 
@@ -93,18 +98,19 @@
         return got[:n] * jnp.exp2(got[n : n + 1] * (1 / 128.0))
 
     to_h, to_hl = packed(other[:, 0]), packed(other[:, 1])
-    near = product(after((lines,), (to_h, to_hl))[0], near, near_there)
+    near = product(after((lines,), (to_hl,))[0], near, near_there)
     got_l = shift(packed(near[:, 1]), "l", 1)
     got_h = shift(to_h, "h", 1)
     got_hl = lax.ppermute(to_hl, ("h", "l"), [(0, 3), (1, 2), (2, 1), (3, 0)])
     own = near[:, 0].reshape(-1, 4 * 128) + unpacked(got_l)
-    result = jnp.stack([own, unpacked(got_h) + unpacked(got_hl)]).astype(jnp.bfloat16)
+    other = unpacked(got_h) + unpacked(got_hl)
+    result = jnp.stack([own, other]).astype(jnp.bfloat16)
     home = [result[:, :, :128]]
     home += [shift(result[:, :, dx * 128 : dx * 128 + 128], "x", -dx) for dx in (1, 2, 3)]
+
     out = jnp.stack(home).reshape(4, 2, 8, rows, 128)
-    order = [ARRIVAL.index(d if d < 5 else d - 8) for d in range(8)]
-    out = out[:, :, jnp.array(order)].transpose(2, 1, 0, 3, 4)
-    out = jnp.roll(out, (at["z"], at["h"], at["x"]), axis=(0, 1, 2)).reshape(64 * rows, 128)
+    out = out.transpose(2, 1, 0, 3, 4)
+    out = jnp.roll(out, (at["h"], at["x"],), axis=(1, 2,)).reshape(64 * rows, 128)
     keep = ij_symmetry[:, None] == ab_symmetry[None, :]
     return jnp.where(keep, out, jnp.zeros_like(out))
 

time: 83.4 us -> 81.1 us (0.972); the launches traced: 81.8 us -> 80.5 us
  local copies, waits for them, and re-layouts: 7.66 us -> 3.67 us
  waiting for transfers between devices: 27.2 us -> 30.4 us
    ppermute x25, waiting for transfers between devices: 23.3 us -> 28.8 us  [shift(): lax.ppermute(value, axis, [(i, (i + step) % size) for i in range(size)])]
    unnamed x22 -> x10, local copies, waits for them, and re-layouts: 5.13 us -> 1.24 us
    ppermute x1, waiting for transfers between devices: 3.96 us -> 1.64 us  [local(): got_hl = lax.ppermute(to_hl, ('h', 'l'), [(0, 3), (1, 2), (2, 1), (3, 0)])]
    ppermute x25, starting transfers between devices: 35 us -> 37 us  [shift(): lax.ppermute(value, axis, [(i, (i + step) % size) for i in range(size)])]
    ppermute x1, starting transfers between devices: 2.85 us -> 1.15 us  [local(): got_hl = lax.ppermute(to_hl, ('h', 'l'), [(0, 3), (1, 2), (2, 1), (3, 0)])]
  transfers between devices with their start and end apart: 26 -> 26, of which waited for: 12 -> 14; matrix products, arithmetic and copies ran while one was open for 13% -> 9% of each run, Pallas kernels for 0% -> 0%
where the time goes in v5:
time: 81.1 us; the launch traced here: 80.5 us
  starting transfers between devices  38.2 us (47%)
  waiting for transfers between devices  30.4 us (37%)
  matrix products  4.04 us (5%)
  other arithmetic  3.73 us (5%)
  local copies, waits for them, and re-layouts  3.67 us (5%)
    ppermute x25, starting transfers between devices, shift(): lax.ppermute(value, axis, [(i, (i + step) % size) for i in range(size)])  37 us
    ppermute x25, waiting for transfers between devices, shift(): lax.ppermute(value, axis, [(i, (i + step) % size) for i in range(size)])  28.8 us
    dot_general x4, matrix products, product(): lax.dot_general(line, block, (((1,), (1,)), ((), ())), preferred_element_...  4.04 us
    ppermute x1, waiting for transfers between devices, local(): got_hl = lax.ppermute(to_hl, ('h', 'l'), [(0, 3), (1, 2), (2, 1), (3, 0)])  1.64 us
  transfers between devices with their start and end apart: 26, of which 14 were waited for; matrix products, arithmetic and copies ran while one was open for 9% of the time, Pallas kernels for 0%

profile of v5, /device:TPU:24, one launch (start us, length us, event | category | flops | bytes accessed | tf_op | source)
XLA Modules:
  0.0 80.5 jit_solution(9600786546122091322)
XLA Ops:
  3.6 1.5 %collective-permute-start.10 = (bf16[128,2048]{1,0:T(8,128)(2,1)}, bf16[128,2048]{1,0:T(8,128)(2,1)S(1)}, u32[]{:S(2)}, u32[]{:S(2)}) collective-permute-start(bf16[128,2048]{1,0:T(8,128)(2,1)} %param.6), channel_id=1, source_target_pairs={{0,4},{4,8},{8,12},{12,0},{1,5},{5,9},{9,13},{13,1},{2,6},{6,10},{... | collective-permute-start | bytes 1572872 | tf_op jit(solution)/shard_map/ppermute | solution.py:12
  5.1 1.7 %collective-permute-start.12 = (bf16[128,2048]{1,0:T(8,128)(2,1)}, bf16[128,2048]{1,0:T(8,128)(2,1)S(1)}, u32[]{:S(2)}, u32[]{:S(2)}) collective-permute-start(bf16[128,2048]{1,0:T(8,128)(2,1)} %param.6), channel_id=1, source_target_pairs={{0,12},{4,0},{8,4},{12,8},{1,13},{5,1},{9,5},{13,9},{2,14},{6,2},{... | collective-permute-start | bytes 1572872 | tf_op jit(solution)/shard_map/ppermute | solution.py:12
  8.0 1.5 %collective-permute-done = bf16[24,4096]{1,0:T(8,128)(2,1)S(1)} collective-permute-done((bf16[24,4096]{1,0:T(8,128)(2,1)S(1)}, bf16[24,4096]{1,0:T(8,128)(2,1)S(1)}, u32[]{:S(2)}, u32[]{:S(2)}) %collective-permute-start) | collective-permute-done | bytes 196640 | tf_op jit(solution)/shard_map/ppermute | solution.py:12
  9.6 2.0 %collective-permute-start.1 = (bf16[48,4096]{1,0:T(8,128)(2,1)S(1)}, bf16[48,4096]{1,0:T(8,128)(2,1)S(1)}, u32[]{:S(2)}, u32[]{:S(2)}) collective-permute-start(bf16[48,4096]{1,0:T(8,128)(2,1)S(1)} %pad_maximum_fusion.1), channel_id=1, source_target_pairs={{0,32},{32,64},{64,96},{96,128},{128,160},{160,192},{192,224},{224... | collective-permute-start | bytes 1179656 | tf_op jit(solution)/shard_map/ppermute | solution.py:12
  11.6 4.0 %collective-permute-start.2 = (bf16[48,4096]{1,0:T(8,128)(2,1)S(1)}, bf16[48,4096]{1,0:T(8,128)(2,1)S(1)}, u32[]{:S(2)}, u32[]{:S(2)}) collective-permute-start(bf16[48,4096]{1,0:T(8,128)(2,1)S(1)} %pad_maximum_fusion.1), channel_id=1, source_target_pairs={{0,224},{32,0},{64,32},{96,64},{128,96},{160,128},{192,160},{224,1... | collective-permute-start | bytes 1179656 | tf_op jit(solution)/shard_map/ppermute | solution.py:12
  15.6 1.2 %collective-permute-start.9 = (bf16[128,2048]{1,0:T(8,128)(2,1)S(1)}, bf16[128,2048]{1,0:T(8,128)(2,1)S(1)}, u32[]{:S(2)}, u32[]{:S(2)}) collective-permute-start(bf16[128,2048]{1,0:T(8,128)(2,1)S(1)} %copy-done), channel_id=1, source_target_pairs={{0,16},{16,0},{1,17},{17,1},{2,18},{18,2},{3,19},{19,3},{4,20},{20... | collective-permute-start | bytes 1572872 | tf_op jit(solution)/shard_map/ppermute | solution.py:12
  18.9 3.0 %collective-permute-start.13 = (bf16[64,2048]{1,0:T(8,128)(2,1)S(1)}, bf16[64,2048]{1,0:T(8,128)(2,1)S(1)}, u32[]{:S(2)}, u32[]{:S(2)}) collective-permute-start(bf16[64,2048]{1,0:T(8,128)(2,1)S(1)} %slice.102), channel_id=1, source_target_pairs={{0,12},{4,0},{8,4},{12,8},{1,13},{5,1},{9,5},{13,9},{2,14},{6,2},{... | collective-permute-start | bytes 786440 | tf_op jit(solution)/shard_map/ppermute | solution.py:12
  21.9 1.8 %collective-permute-done.1 = bf16[48,4096]{1,0:T(8,128)(2,1)S(1)} collective-permute-done((bf16[48,4096]{1,0:T(8,128)(2,1)S(1)}, bf16[48,4096]{1,0:T(8,128)(2,1)S(1)}, u32[]{:S(2)}, u32[]{:S(2)}) %collective-permute-start.1) | collective-permute-done | bytes 393248 | tf_op jit(solution)/shard_map/ppermute | solution.py:12
  23.9 4.0 %collective-permute-start.4 = (bf16[48,4096]{1,0:T(8,128)(2,1)S(1)}, bf16[48,4096]{1,0:T(8,128)(2,1)S(1)}, u32[]{:S(2)}, u32[]{:S(2)}) collective-permute-start(bf16[48,4096]{1,0:T(8,128)(2,1)S(1)} %collective-permute-done.2), channel_id=1, source_target_pairs={{0,224},{32,0},{64,32},{96,64},{128,96},{160,128},{192,160},{224,1... | collective-permute-start | bytes 1179656 | tf_op jit(solution)/shard_map/ppermute | solution.py:12
  28.1 1.5 %collective-permute-done.9 = bf16[128,2048]{1,0:T(8,128)(2,1)S(1)} collective-permute-done((bf16[128,2048]{1,0:T(8,128)(2,1)S(1)}, bf16[128,2048]{1,0:T(8,128)(2,1)S(1)}, u32[]{:S(2)}, u32[]{:S(2)}) %collective-permute-start.9) | collective-permute-done | bytes 524320 | tf_op jit(solution)/shard_map/ppermute | solution.py:12
  29.6 1.5 %collective-permute-start.14 = (bf16[128,2048]{1,0:T(8,128)(2,1)S(1)}, bf16[128,2048]{1,0:T(8,128)(2,1)S(1)}, u32[]{:S(2)}, u32[]{:S(2)}) collective-permute-start(bf16[128,2048]{1,0:T(8,128)(2,1)S(1)} %collective-permute-done.9), channel_id=1, source_target_pairs={{0,4},{4,8},{8,12},{12,0},{1,5},{5,9},{9,13},{13,1},{2,6},{6,10},{... | collective-permute-start | bytes 1572872 | tf_op jit(solution)/shard_map/ppermute | solution.py:12
  31.1 1.7 %collective-permute-start.16 = (bf16[128,2048]{1,0:T(8,128)(2,1)S(1)}, bf16[128,2048]{1,0:T(8,128)(2,1)S(1)}, u32[]{:S(2)}, u32[]{:S(2)}) collective-permute-start(bf16[128,2048]{1,0:T(8,128)(2,1)S(1)} %collective-permute-done.9), channel_id=1, source_target_pairs={{0,12},{4,0},{8,4},{12,8},{1,13},{5,1},{9,5},{13,9},{2,14},{6,2},{... | collective-permute-start | bytes 1572872 | tf_op jit(solution)/shard_map/ppermute | solution.py:12
  32.8 1.2 %collective-permute-start.15 = (bf16[128,2048]{1,0:T(8,128)(2,1)S(1)}, bf16[128,2048]{1,0:T(8,128)(2,1)S(1)}, u32[]{:S(2)}, u32[]{:S(2)}) collective-permute-start(bf16[128,2048]{1,0:T(8,128)(2,1)S(1)} %get-tuple-element.33), channel_id=1, source_target_pairs={{0,16},{16,0},{1,17},{17,1},{2,18},{18,2},{3,19},{19,3},{4,20},{20... | collective-permute-start | bytes 1572872 | tf_op jit(solution)/shard_map/ppermute | solution.py:12
  35.2 3.2 %collective-permute-start.6 = (bf16[48,4096]{1,0:T(8,128)(2,1)S(1)}, bf16[48,4096]{1,0:T(8,128)(2,1)S(1)}, u32[]{:S(2)}, u32[]{:S(2)}) collective-permute-start(bf16[48,4096]{1,0:T(8,128)(2,1)S(1)} %collective-permute-done.4), channel_id=1, source_target_pairs={{0,224},{32,0},{64,32},{96,64},{128,96},{160,128},{192,160},{224,1... | collective-permute-start | bytes 1179656 | tf_op jit(solution)/shard_map/ppermute | solution.py:12
  38.5 3.9 %collective-permute-done.14 = bf16[128,2048]{1,0:T(8,128)(2,1)S(1)} collective-permute-done((bf16[128,2048]{1,0:T(8,128)(2,1)S(1)}, bf16[128,2048]{1,0:T(8,128)(2,1)S(1)}, u32[]{:S(2)}, u32[]{:S(2)}) %collective-permute-start.14) | collective-permute-done | bytes 524320 | tf_op jit(solution)/shard_map/ppermute | solution.py:12
  43.2 2.2 %collective-permute-done.15 = bf16[128,2048]{1,0:T(8,128)(2,1)S(1)} collective-permute-done((bf16[128,2048]{1,0:T(8,128)(2,1)S(1)}, bf16[128,2048]{1,0:T(8,128)(2,1)S(1)}, u32[]{:S(2)}, u32[]{:S(2)}) %collective-permute-start.15) | collective-permute-done | bytes 524320 | tf_op jit(solution)/shard_map/ppermute | solution.py:12
  45.5 3.3 %collective-permute-start.8 = (bf16[24,4096]{1,0:T(8,128)(2,1)S(1)}, bf16[24,4096]{1,0:T(8,128)(2,1)S(1)}, u32[]{:S(2)}, u32[]{:S(2)}) collective-permute-start(bf16[24,4096]{1,0:T(8,128)(2,1)S(1)} %slice.99), channel_id=1, source_target_pairs={{0,224},{32,0},{64,32},{96,64},{128,96},{160,128},{192,160},{224,1... | collective-permute-start | bytes 589832 | tf_op jit(solution)/shard_map/ppermute | solution.py:12
  48.9 5.2 %collective-permute-done.7 = bf16[24,4096]{1,0:T(8,128)(2,1)S(1)} collective-permute-done((bf16[24,4096]{1,0:T(8,128)(2,1)S(1)}, bf16[24,4096]{1,0:T(8,128)(2,1)S(1)}, u32[]{:S(2)}, u32[]{:S(2)}) %collective-permute-start.7) | collective-permute-done | bytes 196640 | tf_op jit(solution)/shard_map/ppermute | solution.py:12
  57.8 2.4 %collective-permute-start.21 = (s16[200,512]{1,0:T(8,128)(2,1)S(1)}, s16[200,512]{1,0:T(8,128)(2,1)S(1)}, u32[]{:S(2)}, u32[]{:S(2)}) collective-permute-start(s16[200,512]{1,0:T(8,128)(2,1)S(1)} %pad_add_fusion.2), channel_id=1, source_target_pairs={{0,16},{16,0},{1,17},{17,1},{2,18},{18,2},{3,19},{19,3},{4,20},{20... | collective-permute-start | bytes 614408 | tf_op jit(solution)/shard_map/ppermute | solution.py:12
  63.2 4.0 %collective-permute-done.21 = s16[200,512]{1,0:T(8,128)(2,1)S(1)} collective-permute-done((s16[200,512]{1,0:T(8,128)(2,1)S(1)}, s16[200,512]{1,0:T(8,128)(2,1)S(1)}, u32[]{:S(2)}, u32[]{:S(2)}) %collective-permute-start.21) | collective-permute-done | bytes 204832 | tf_op jit(solution)/shard_map/ppermute | solution.py:12
  67.3 1.6 %collective-permute-done.22 = s16[200,512]{1,0:T(8,128)(2,1)S(1)} collective-permute-done((s16[200,512]{1,0:T(8,128)(2,1)S(1)}, s16[200,512]{1,0:T(8,128)(2,1)S(1)}, u32[]{:S(2)}, u32[]{:S(2)}) %collective-permute-start.22) | collective-permute-done | bytes 204832 | tf_op jit(solution)/shard_map/ppermute | solution.py:104
  70.2 1.6 %collective-permute-start.23 = (bf16[2,192,128]{2,1,0:T(8,128)(2,1)S(1)}, bf16[2,192,128]{2,1,0:T(8,128)(2,1)S(1)}, u32[]{:S(2)}, u32[]{:S(2)}) collective-permute-start(bf16[2,192,128]{2,1,0:T(8,128)(2,1)S(1)} %get-tuple-element.29), channel_id=1, source_target_pairs={{0,12},{4,0},{8,4},{12,8},{1,13},{5,1},{9,5},{13,9},{2,14},{6,2},{... | collective-permute-start | bytes 294920 | tf_op jit(solution)/shard_map/ppermute | solution.py:12
  73.4 1.8 %collective-permute-done.23 = bf16[2,192,128]{2,1,0:T(8,128)(2,1)S(1)} collective-permute-done((bf16[2,192,128]{2,1,0:T(8,128)(2,1)S(1)}, bf16[2,192,128]{2,1,0:T(8,128)(2,1)S(1)}, u32[]{:S(2)}, u32[]{:S(2)}) %collective-permute-start.23) | collective-permute-done | bytes 98336 | tf_op jit(solution)/shard_map/ppermute | solution.py:12
  75.2 2.8 %collective-permute-done.24 = bf16[2,192,128]{2,1,0:T(8,128)(2,1)S(1)} collective-permute-done((bf16[2,192,128]{2,1,0:T(8,128)(2,1)S(1)}, bf16[2,192,128]{2,1,0:T(8,128)(2,1)S(1)}, u32[]{:S(2)}, u32[]{:S(2)}) %collective-permute-start.24) | collective-permute-done | bytes 98336 | tf_op jit(solution)/shard_map/ppermute | solution.py:12
  (92 shorter events, 21.3 us)
Async XLA Ops:
  2.8 6.7 %collective-permute-start = (bf16[24,4096]{1,0:T(8,128)(2,1)S(1)}, bf16[24,4096]{1,0:T(8,128)(2,1)S(1)}, u32[]{:S(2)}, u32[]{:S(2)}) collective-permute-start(bf16[24,4096]{1,0:T(8,128)(2,1)S(1)} %pad_maximum_fusion.2), channel_id=1, source_target_pairs={{0,2},{2,0},{1,3},{3,1},{4,6},{6,4},{5,7},{7,5},{8,10},{10,8},{9,1... | collective-permute-start | bytes 589832 | tf_op jit(solution)/shard_map/ppermute | solution.py:12
  3.6 14.8 %collective-permute-start.10 = (bf16[128,2048]{1,0:T(8,128)(2,1)}, bf16[128,2048]{1,0:T(8,128)(2,1)S(1)}, u32[]{:S(2)}, u32[]{:S(2)}) collective-permute-start(bf16[128,2048]{1,0:T(8,128)(2,1)} %param.6), channel_id=1, source_target_pairs={{0,4},{4,8},{8,12},{12,0},{1,5},{5,9},{9,13},{13,1},{2,6},{6,10},{... | collective-permute-start | bytes 1572872 | tf_op jit(solution)/shard_map/ppermute | solution.py:12
  5.1 13.7 %collective-permute-start.12 = (bf16[128,2048]{1,0:T(8,128)(2,1)}, bf16[128,2048]{1,0:T(8,128)(2,1)S(1)}, u32[]{:S(2)}, u32[]{:S(2)}) collective-permute-start(bf16[128,2048]{1,0:T(8,128)(2,1)} %param.6), channel_id=1, source_target_pairs={{0,12},{4,0},{8,4},{12,8},{1,13},{5,1},{9,5},{13,9},{2,14},{6,2},{... | collective-permute-start | bytes 1572872 | tf_op jit(solution)/shard_map/ppermute | solution.py:12
  9.6 14.2 %collective-permute-start.1 = (bf16[48,4096]{1,0:T(8,128)(2,1)S(1)}, bf16[48,4096]{1,0:T(8,128)(2,1)S(1)}, u32[]{:S(2)}, u32[]{:S(2)}) collective-permute-start(bf16[48,4096]{1,0:T(8,128)(2,1)S(1)} %pad_maximum_fusion.1), channel_id=1, source_target_pairs={{0,32},{32,64},{64,96},{96,128},{128,160},{160,192},{192,224},{224... | collective-permute-start | bytes 1179656 | tf_op jit(solution)/shard_map/ppermute | solution.py:12
  11.6 12.4 %collective-permute-start.2 = (bf16[48,4096]{1,0:T(8,128)(2,1)S(1)}, bf16[48,4096]{1,0:T(8,128)(2,1)S(1)}, u32[]{:S(2)}, u32[]{:S(2)}) collective-permute-start(bf16[48,4096]{1,0:T(8,128)(2,1)S(1)} %pad_maximum_fusion.1), channel_id=1, source_target_pairs={{0,224},{32,0},{64,32},{96,64},{128,96},{160,128},{192,160},{224,1... | collective-permute-start | bytes 1179656 | tf_op jit(solution)/shard_map/ppermute | solution.py:12
  15.6 14.0 %collective-permute-start.9 = (bf16[128,2048]{1,0:T(8,128)(2,1)S(1)}, bf16[128,2048]{1,0:T(8,128)(2,1)S(1)}, u32[]{:S(2)}, u32[]{:S(2)}) collective-permute-start(bf16[128,2048]{1,0:T(8,128)(2,1)S(1)} %copy-done), channel_id=1, source_target_pairs={{0,16},{16,0},{1,17},{17,1},{2,18},{18,2},{3,19},{19,3},{4,20},{20... | collective-permute-start | bytes 1572872 | tf_op jit(solution)/shard_map/ppermute | solution.py:12
  18.5 9.6 %collective-permute-start.11 = (bf16[64,2048]{1,0:T(8,128)(2,1)S(1)}, bf16[64,2048]{1,0:T(8,128)(2,1)S(1)}, u32[]{:S(2)}, u32[]{:S(2)}) collective-permute-start(bf16[64,2048]{1,0:T(8,128)(2,1)S(1)} %slice.101), channel_id=1, source_target_pairs={{0,4},{4,8},{8,12},{12,0},{1,5},{5,9},{9,13},{13,1},{2,6},{6,10},{... | collective-permute-start | bytes 786440 | tf_op jit(solution)/shard_map/ppermute | solution.py:12
  18.9 9.2 %collective-permute-start.13 = (bf16[64,2048]{1,0:T(8,128)(2,1)S(1)}, bf16[64,2048]{1,0:T(8,128)(2,1)S(1)}, u32[]{:S(2)}, u32[]{:S(2)}) collective-permute-start(bf16[64,2048]{1,0:T(8,128)(2,1)S(1)} %slice.102), channel_id=1, source_target_pairs={{0,12},{4,0},{8,4},{12,8},{1,13},{5,1},{9,5},{13,9},{2,14},{6,2},{... | collective-permute-start | bytes 786440 | tf_op jit(solution)/shard_map/ppermute | solution.py:12
  23.7 11.5 %collective-permute-start.3 = (bf16[48,4096]{1,0:T(8,128)(2,1)S(1)}, bf16[48,4096]{1,0:T(8,128)(2,1)S(1)}, u32[]{:S(2)}, u32[]{:S(2)}) collective-permute-start(bf16[48,4096]{1,0:T(8,128)(2,1)S(1)} %collective-permute-done.1), channel_id=1, source_target_pairs={{0,32},{32,64},{64,96},{96,128},{128,160},{160,192},{192,224},{224... | collective-permute-start | bytes 1179656 | tf_op jit(solution)/shard_map/ppermute | solution.py:12
  23.9 11.3 %collective-permute-start.4 = (bf16[48,4096]{1,0:T(8,128)(2,1)S(1)}, bf16[48,4096]{1,0:T(8,128)(2,1)S(1)}, u32[]{:S(2)}, u32[]{:S(2)}) collective-permute-start(bf16[48,4096]{1,0:T(8,128)(2,1)S(1)} %collective-permute-done.2), channel_id=1, source_target_pairs={{0,224},{32,0},{64,32},{96,64},{128,96},{160,128},{192,160},{224,1... | collective-permute-start | bytes 1179656 | tf_op jit(solution)/shard_map/ppermute | solution.py:12
  29.6 12.8 %collective-permute-start.14 = (bf16[128,2048]{1,0:T(8,128)(2,1)S(1)}, bf16[128,2048]{1,0:T(8,128)(2,1)S(1)}, u32[]{:S(2)}, u32[]{:S(2)}) collective-permute-start(bf16[128,2048]{1,0:T(8,128)(2,1)S(1)} %collective-permute-done.9), channel_id=1, source_target_pairs={{0,4},{4,8},{8,12},{12,0},{1,5},{5,9},{9,13},{13,1},{2,6},{6,10},{... | collective-permute-start | bytes 1572872 | tf_op jit(solution)/shard_map/ppermute | solution.py:12
  31.1 11.3 %collective-permute-start.16 = (bf16[128,2048]{1,0:T(8,128)(2,1)S(1)}, bf16[128,2048]{1,0:T(8,128)(2,1)S(1)}, u32[]{:S(2)}, u32[]{:S(2)}) collective-permute-start(bf16[128,2048]{1,0:T(8,128)(2,1)S(1)} %collective-permute-done.9), channel_id=1, source_target_pairs={{0,12},{4,0},{8,4},{12,8},{1,13},{5,1},{9,5},{13,9},{2,14},{6,2},{... | collective-permute-start | bytes 1572872 | tf_op jit(solution)/shard_map/ppermute | solution.py:12
  32.8 12.5 %collective-permute-start.15 = (bf16[128,2048]{1,0:T(8,128)(2,1)S(1)}, bf16[128,2048]{1,0:T(8,128)(2,1)S(1)}, u32[]{:S(2)}, u32[]{:S(2)}) collective-permute-start(bf16[128,2048]{1,0:T(8,128)(2,1)S(1)} %get-tuple-element.33), channel_id=1, source_target_pairs={{0,16},{16,0},{1,17},{17,1},{2,18},{18,2},{3,19},{19,3},{4,20},{20... | collective-permute-start | bytes 1572872 | tf_op jit(solution)/shard_map/ppermute | solution.py:12
  35.2 10.2 %collective-permute-start.5 = (bf16[48,4096]{1,0:T(8,128)(2,1)S(1)}, bf16[48,4096]{1,0:T(8,128)(2,1)S(1)}, u32[]{:S(2)}, u32[]{:S(2)}) collective-permute-start(bf16[48,4096]{1,0:T(8,128)(2,1)S(1)} %collective-permute-done.3), channel_id=1, source_target_pairs={{0,32},{32,64},{64,96},{96,128},{128,160},{160,192},{192,224},{224... | collective-permute-start | bytes 1179656 | tf_op jit(solution)/shard_map/ppermute | solution.py:12
  35.2 10.3 %collective-permute-start.6 = (bf16[48,4096]{1,0:T(8,128)(2,1)S(1)}, bf16[48,4096]{1,0:T(8,128)(2,1)S(1)}, u32[]{:S(2)}, u32[]{:S(2)}) collective-permute-start(bf16[48,4096]{1,0:T(8,128)(2,1)S(1)} %collective-permute-done.4), channel_id=1, source_target_pairs={{0,224},{32,0},{64,32},{96,64},{128,96},{160,128},{192,160},{224,1... | collective-permute-start | bytes 1179656 | tf_op jit(solution)/shard_map/ppermute | solution.py:12
  42.4 17.8 %collective-permute-start.19 = (bf16[512,2048]{1,0:T(8,128)(2,1)S(1)}, bf16[512,2048]{1,0:T(8,128)(2,1)S(1)}, u32[]{:S(2)}, u32[]{:S(2)}) collective-permute-start(bf16[512,2048]{1,0:T(8,128)(2,1)S(1)} %constant_dynamic-update-slice_fusion.2), channel_id=1, source_target_pairs={{0,1},{1,0},{2,3},{3,2},{4,5},{5,4},{6,7},{7,6},{8,9},{9,8},{10,11... | collective-permute-start | bytes 6291464 | tf_op jit(solution)/shard_map/ppermute | solution.py:12
  42.6 12.5 %collective-permute-start.17 = (bf16[384,2048]{1,0:T(8,128)(2,1)S(1)}, bf16[384,2048]{1,0:T(8,128)(2,1)S(1)}, u32[]{:S(2)}, u32[]{:S(2)}) collective-permute-start(bf16[384,2048]{1,0:T(8,128)(2,1)S(1)} %pad_maximum_fusion), channel_id=1, source_target_pairs={{0,1},{1,0},{2,3},{3,2},{4,5},{5,4},{6,7},{7,6},{8,9},{9,8},{10,11... | collective-permute-start | bytes 4718600 | tf_op jit(solution)/shard_map/ppermute | solution.py:12
  45.4 9.9 %collective-permute-start.18 = (bf16[128,2048]{1,0:T(8,128)(2,1)S(1)}, bf16[128,2048]{1,0:T(8,128)(2,1)S(1)}, u32[]{:S(2)}, u32[]{:S(2)}) collective-permute-start(bf16[128,2048]{1,0:T(8,128)(2,1)S(1)} %collective-permute-done.15), channel_id=1, source_target_pairs={{0,1},{1,0},{2,3},{3,2},{4,5},{5,4},{6,7},{7,6},{8,9},{9,8},{10,11... | collective-permute-start | bytes 1572872 | tf_op jit(solution)/shard_map/ppermute | solution.py:12
  45.4 8.7 %collective-permute-start.7 = (bf16[24,4096]{1,0:T(8,128)(2,1)S(1)}, bf16[24,4096]{1,0:T(8,128)(2,1)S(1)}, u32[]{:S(2)}, u32[]{:S(2)}) collective-permute-start(bf16[24,4096]{1,0:T(8,128)(2,1)S(1)} %slice.98), channel_id=1, source_target_pairs={{0,32},{32,64},{64,96},{96,128},{128,160},{160,192},{192,224},{224... | collective-permute-start | bytes 589832 | tf_op jit(solution)/shard_map/ppermute | solution.py:12
  45.5 8.5 %collective-permute-start.8 = (bf16[24,4096]{1,0:T(8,128)(2,1)S(1)}, bf16[24,4096]{1,0:T(8,128)(2,1)S(1)}, u32[]{:S(2)}, u32[]{:S(2)}) collective-permute-start(bf16[24,4096]{1,0:T(8,128)(2,1)S(1)} %slice.99), channel_id=1, source_target_pairs={{0,224},{32,0},{64,32},{96,64},{128,96},{160,128},{192,160},{224,1... | collective-permute-start | bytes 589832 | tf_op jit(solution)/shard_map/ppermute | solution.py:12
  56.5 12.5 %collective-permute-start.22 = (s16[200,512]{1,0:T(8,128)(2,1)S(1)}, s16[200,512]{1,0:T(8,128)(2,1)S(1)}, u32[]{:S(2)}, u32[]{:S(2)}) collective-permute-start(s16[200,512]{1,0:T(8,128)(2,1)S(1)} %pad_add_fusion), channel_id=1, source_target_pairs={{0,18},{2,16},{16,2},{18,0},{1,19},{3,17},{17,3},{19,1},{4,22},{6,... | collective-permute-start | bytes 614408 | tf_op jit(solution)/shard_map/ppermute | solution.py:104
  57.8 9.5 %collective-permute-start.21 = (s16[200,512]{1,0:T(8,128)(2,1)S(1)}, s16[200,512]{1,0:T(8,128)(2,1)S(1)}, u32[]{:S(2)}, u32[]{:S(2)}) collective-permute-start(s16[200,512]{1,0:T(8,128)(2,1)S(1)} %pad_add_fusion.2), channel_id=1, source_target_pairs={{0,16},{16,0},{1,17},{17,1},{2,18},{18,2},{3,19},{19,3},{4,20},{20... | collective-permute-start | bytes 614408 | tf_op jit(solution)/shard_map/ppermute | solution.py:12
  62.4 7.4 %collective-permute-start.20 = (s16[200,512]{1,0:T(8,128)(2,1)S(1)}, s16[200,512]{1,0:T(8,128)(2,1)S(1)}, u32[]{:S(2)}, u32[]{:S(2)}) collective-permute-start(s16[200,512]{1,0:T(8,128)(2,1)S(1)} %pad_add_fusion.1), channel_id=1, source_target_pairs={{0,2},{2,0},{1,3},{3,1},{4,6},{6,4},{5,7},{7,5},{8,10},{10,8},{9,1... | collective-permute-start | bytes 614408 | tf_op jit(solution)/shard_map/ppermute | solution.py:12
  72.5 6.6 %collective-permute-start.25 = (bf16[2,192,128]{2,1,0:T(8,128)(2,1)S(1)}, bf16[2,192,128]{2,1,0:T(8,128)(2,1)S(1)}, u32[]{:S(2)}, u32[]{:S(2)}) collective-permute-start(bf16[2,192,128]{2,1,0:T(8,128)(2,1)S(1)} %get-tuple-element.30), channel_id=1, source_target_pairs={{0,4},{4,8},{8,12},{12,0},{1,5},{5,9},{9,13},{13,1},{2,6},{6,10},{... | collective-permute-start | bytes 294920 | tf_op jit(solution)/shard_map/ppermute | solution.py:12
  (5 other events, 46.2 us)

commit v6 on v5

--- a/solution.py
+++ b/solution.py
@@ -63,7 +63,6 @@
     other = shift(block, "h", 1)
     middle = jnp.concatenate(far_of(below, above), axis=0)
     near = jnp.concatenate([masked, below, middle, above], axis=0)
-    (other,) = after((other,), (middle,))
     middle = shift(middle, "h", 1)
     below, above = shift(other, "x", 1), shift(other, "x", -1)
     sides = jnp.concatenate([other, below, above], axis=0)

time: 81.1 us -> 80.6 us (level)
    ppermute x25, waiting for transfers between devices: 28.8 us -> 27.3 us  [shift(): lax.ppermute(value, axis, [(i, (i + step) % size) for i in range(size)])]
    ppermute x1, waiting for transfers between devices: 1.64 us -> 2.91 us  [local(): got_hl = lax.ppermute(to_hl, ('h', 'l'), [(0, 3), (1, 2), (2, 1), (3, 0)])]
    ppermute x25, starting transfers between devices: 37 us -> 38.1 us  [shift(): lax.ppermute(value, axis, [(i, (i + step) % size) for i in range(size)])]
    ppermute x1, starting transfers between devices: 1.15 us -> 0.31 us  [local(): got_hl = lax.ppermute(to_hl, ('h', 'l'), [(0, 3), (1, 2), (2, 1), (3, 0)])]
where the time goes in v6:
time: 80.6 us; the launch traced here: 80.4 us
  starting transfers between devices  38.4 us (48%)
  waiting for transfers between devices  30.2 us (37%)
  matrix products  4.04 us (5%)
  other arithmetic  3.7 us (5%)
  local copies, waits for them, and re-layouts  3.64 us (5%)
    ppermute x25, starting transfers between devices, shift(): lax.ppermute(value, axis, [(i, (i + step) % size) for i in range(size)])  38.1 us
    ppermute x25, waiting for transfers between devices, shift(): lax.ppermute(value, axis, [(i, (i + step) % size) for i in range(size)])  27.3 us
    dot_general x4, matrix products, product(): lax.dot_general(line, block, (((1,), (1,)), ((), ())), preferred_element_...  4.04 us
    ppermute x1, waiting for transfers between devices, local(): got_hl = lax.ppermute(to_hl, ('h', 'l'), [(0, 3), (1, 2), (2, 1), (3, 0)])  2.91 us
  transfers between devices with their start and end apart: 26, of which 14 were waited for; matrix products, arithmetic and copies ran while one was open for 9% of the time, Pallas kernels for 0%

profile of v6, /device:TPU:24, one launch (start us, length us, event | category | flops | bytes accessed | tf_op | source)
XLA Modules:
  0.0 80.4 jit_solution(2062682114716714939)
XLA Ops:
  3.6 1.5 %collective-permute-start.11 = (bf16[128,2048]{1,0:T(8,128)(2,1)}, bf16[128,2048]{1,0:T(8,128)(2,1)S(1)}, u32[]{:S(2)}, u32[]{:S(2)}) collective-permute-start(bf16[128,2048]{1,0:T(8,128)(2,1)} %param.6), channel_id=1, source_target_pairs={{0,4},{4,8},{8,12},{12,0},{1,5},{5,9},{9,13},{13,1},{2,6},{6,10},{... | collective-permute-start | bytes 1572872 | tf_op jit(solution)/shard_map/ppermute | solution.py:12
  5.1 1.7 %collective-permute-start.13 = (bf16[128,2048]{1,0:T(8,128)(2,1)}, bf16[128,2048]{1,0:T(8,128)(2,1)S(1)}, u32[]{:S(2)}, u32[]{:S(2)}) collective-permute-start(bf16[128,2048]{1,0:T(8,128)(2,1)} %param.6), channel_id=1, source_target_pairs={{0,12},{4,0},{8,4},{12,8},{1,13},{5,1},{9,5},{13,9},{2,14},{6,2},{... | collective-permute-start | bytes 1572872 | tf_op jit(solution)/shard_map/ppermute | solution.py:12
  8.0 1.5 %collective-permute-done = bf16[24,4096]{1,0:T(8,128)(2,1)S(1)} collective-permute-done((bf16[24,4096]{1,0:T(8,128)(2,1)S(1)}, bf16[24,4096]{1,0:T(8,128)(2,1)S(1)}, u32[]{:S(2)}, u32[]{:S(2)}) %collective-permute-start) | collective-permute-done | bytes 196640 | tf_op jit(solution)/shard_map/ppermute | solution.py:12
  9.6 2.0 %collective-permute-start.1 = (bf16[48,4096]{1,0:T(8,128)(2,1)S(1)}, bf16[48,4096]{1,0:T(8,128)(2,1)S(1)}, u32[]{:S(2)}, u32[]{:S(2)}) collective-permute-start(bf16[48,4096]{1,0:T(8,128)(2,1)S(1)} %pad_maximum_fusion.2), channel_id=1, source_target_pairs={{0,32},{32,64},{64,96},{96,128},{128,160},{160,192},{192,224},{224... | collective-permute-start | bytes 1179656 | tf_op jit(solution)/shard_map/ppermute | solution.py:12
  11.6 4.0 %collective-permute-start.2 = (bf16[48,4096]{1,0:T(8,128)(2,1)S(1)}, bf16[48,4096]{1,0:T(8,128)(2,1)S(1)}, u32[]{:S(2)}, u32[]{:S(2)}) collective-permute-start(bf16[48,4096]{1,0:T(8,128)(2,1)S(1)} %pad_maximum_fusion.2), channel_id=1, source_target_pairs={{0,224},{32,0},{64,32},{96,64},{128,96},{160,128},{192,160},{224,1... | collective-permute-start | bytes 1179656 | tf_op jit(solution)/shard_map/ppermute | solution.py:12
  18.9 3.0 %collective-permute-start.14 = (bf16[64,2048]{1,0:T(8,128)(2,1)S(1)}, bf16[64,2048]{1,0:T(8,128)(2,1)S(1)}, u32[]{:S(2)}, u32[]{:S(2)}) collective-permute-start(bf16[64,2048]{1,0:T(8,128)(2,1)S(1)} %slice.102), channel_id=1, source_target_pairs={{0,12},{4,0},{8,4},{12,8},{1,13},{5,1},{9,5},{13,9},{2,14},{6,2},{... | collective-permute-start | bytes 786440 | tf_op jit(solution)/shard_map/ppermute | solution.py:12
  21.9 1.8 %collective-permute-done.1 = bf16[48,4096]{1,0:T(8,128)(2,1)S(1)} collective-permute-done((bf16[48,4096]{1,0:T(8,128)(2,1)S(1)}, bf16[48,4096]{1,0:T(8,128)(2,1)S(1)}, u32[]{:S(2)}, u32[]{:S(2)}) %collective-permute-start.1) | collective-permute-done | bytes 393248 | tf_op jit(solution)/shard_map/ppermute | solution.py:12
  23.9 4.0 %collective-permute-start.4 = (bf16[48,4096]{1,0:T(8,128)(2,1)S(1)}, bf16[48,4096]{1,0:T(8,128)(2,1)S(1)}, u32[]{:S(2)}, u32[]{:S(2)}) collective-permute-start(bf16[48,4096]{1,0:T(8,128)(2,1)S(1)} %collective-permute-done.2), channel_id=1, source_target_pairs={{0,224},{32,0},{64,32},{96,64},{128,96},{160,128},{192,160},{224,1... | collective-permute-start | bytes 1179656 | tf_op jit(solution)/shard_map/ppermute | solution.py:12
  28.0 1.6 %collective-permute-done.9 = bf16[128,2048]{1,0:T(8,128)(2,1)S(1)} collective-permute-done((bf16[128,2048]{1,0:T(8,128)(2,1)S(1)}, bf16[128,2048]{1,0:T(8,128)(2,1)S(1)}, u32[]{:S(2)}, u32[]{:S(2)}) %collective-permute-start.9) | collective-permute-done | bytes 524320 | tf_op jit(solution)/shard_map/ppermute | solution.py:12
  29.6 1.5 %collective-permute-start.10 = (bf16[128,2048]{1,0:T(8,128)(2,1)S(1)}, bf16[128,2048]{1,0:T(8,128)(2,1)S(1)}, u32[]{:S(2)}, u32[]{:S(2)}) collective-permute-start(bf16[128,2048]{1,0:T(8,128)(2,1)S(1)} %collective-permute-done.9), channel_id=1, source_target_pairs={{0,4},{4,8},{8,12},{12,0},{1,5},{5,9},{9,13},{13,1},{2,6},{6,10},{... | collective-permute-start | bytes 1572872 | tf_op jit(solution)/shard_map/ppermute | solution.py:12
  31.1 1.7 %collective-permute-start.16 = (bf16[128,2048]{1,0:T(8,128)(2,1)S(1)}, bf16[128,2048]{1,0:T(8,128)(2,1)S(1)}, u32[]{:S(2)}, u32[]{:S(2)}) collective-permute-start(bf16[128,2048]{1,0:T(8,128)(2,1)S(1)} %collective-permute-done.9), channel_id=1, source_target_pairs={{0,12},{4,0},{8,4},{12,8},{1,13},{5,1},{9,5},{13,9},{2,14},{6,2},{... | collective-permute-start | bytes 1572872 | tf_op jit(solution)/shard_map/ppermute | solution.py:12
  32.9 1.3 %collective-permute-start.15 = (bf16[128,2048]{1,0:T(8,128)(2,1)S(1)}, bf16[128,2048]{1,0:T(8,128)(2,1)S(1)}, u32[]{:S(2)}, u32[]{:S(2)}) collective-permute-start(bf16[128,2048]{1,0:T(8,128)(2,1)S(1)} %pad_maximum_fusion.1), channel_id=1, source_target_pairs={{0,16},{16,0},{1,17},{17,1},{2,18},{18,2},{3,19},{19,3},{4,20},{20... | collective-permute-start | bytes 1572872 | tf_op jit(solution)/shard_map/ppermute | solution.py:12
  35.2 3.2 %collective-permute-start.6 = (bf16[48,4096]{1,0:T(8,128)(2,1)S(1)}, bf16[48,4096]{1,0:T(8,128)(2,1)S(1)}, u32[]{:S(2)}, u32[]{:S(2)}) collective-permute-start(bf16[48,4096]{1,0:T(8,128)(2,1)S(1)} %collective-permute-done.4), channel_id=1, source_target_pairs={{0,224},{32,0},{64,32},{96,64},{128,96},{160,128},{192,160},{224,1... | collective-permute-start | bytes 1179656 | tf_op jit(solution)/shard_map/ppermute | solution.py:12
  38.5 3.9 %collective-permute-done.10 = bf16[128,2048]{1,0:T(8,128)(2,1)S(1)} collective-permute-done((bf16[128,2048]{1,0:T(8,128)(2,1)S(1)}, bf16[128,2048]{1,0:T(8,128)(2,1)S(1)}, u32[]{:S(2)}, u32[]{:S(2)}) %collective-permute-start.10) | collective-permute-done | bytes 524320 | tf_op jit(solution)/shard_map/ppermute | solution.py:12
  43.1 2.4 %collective-permute-done.15 = bf16[128,2048]{1,0:T(8,128)(2,1)S(1)} collective-permute-done((bf16[128,2048]{1,0:T(8,128)(2,1)S(1)}, bf16[128,2048]{1,0:T(8,128)(2,1)S(1)}, u32[]{:S(2)}, u32[]{:S(2)}) %collective-permute-start.15) | collective-permute-done | bytes 524320 | tf_op jit(solution)/shard_map/ppermute | solution.py:12
  45.7 3.3 %collective-permute-start.8 = (bf16[24,4096]{1,0:T(8,128)(2,1)S(1)}, bf16[24,4096]{1,0:T(8,128)(2,1)S(1)}, u32[]{:S(2)}, u32[]{:S(2)}) collective-permute-start(bf16[24,4096]{1,0:T(8,128)(2,1)S(1)} %slice.99), channel_id=1, source_target_pairs={{0,224},{32,0},{64,32},{96,64},{128,96},{160,128},{192,160},{224,1... | collective-permute-start | bytes 589832 | tf_op jit(solution)/shard_map/ppermute | solution.py:12
  49.0 5.1 %collective-permute-done.7 = bf16[24,4096]{1,0:T(8,128)(2,1)S(1)} collective-permute-done((bf16[24,4096]{1,0:T(8,128)(2,1)S(1)}, bf16[24,4096]{1,0:T(8,128)(2,1)S(1)}, u32[]{:S(2)}, u32[]{:S(2)}) %collective-permute-start.7) | collective-permute-done | bytes 196640 | tf_op jit(solution)/shard_map/ppermute | solution.py:12
  57.0 2.7 %collective-permute-start.21 = (s16[200,512]{1,0:T(8,128)(2,1)S(1)}, s16[200,512]{1,0:T(8,128)(2,1)S(1)}, u32[]{:S(2)}, u32[]{:S(2)}) collective-permute-start(s16[200,512]{1,0:T(8,128)(2,1)S(1)} %pad_add_fusion.2), channel_id=1, source_target_pairs={{0,16},{16,0},{1,17},{17,1},{2,18},{18,2},{3,19},{19,3},{4,20},{20... | collective-permute-start | bytes 614408 | tf_op jit(solution)/shard_map/ppermute | solution.py:12
  61.9 1.4 %collective-permute-start.20 = (s16[200,512]{1,0:T(8,128)(2,1)S(1)}, s16[200,512]{1,0:T(8,128)(2,1)S(1)}, u32[]{:S(2)}, u32[]{:S(2)}) collective-permute-start(s16[200,512]{1,0:T(8,128)(2,1)S(1)} %pad_add_fusion.1), channel_id=1, source_target_pairs={{0,2},{2,0},{1,3},{3,1},{4,6},{6,4},{5,7},{7,5},{8,10},{10,8},{9,1... | collective-permute-start | bytes 614408 | tf_op jit(solution)/shard_map/ppermute | solution.py:12
  63.3 2.7 %collective-permute-done.21 = s16[200,512]{1,0:T(8,128)(2,1)S(1)} collective-permute-done((s16[200,512]{1,0:T(8,128)(2,1)S(1)}, s16[200,512]{1,0:T(8,128)(2,1)S(1)}, u32[]{:S(2)}, u32[]{:S(2)}) %collective-permute-start.21) | collective-permute-done | bytes 204832 | tf_op jit(solution)/shard_map/ppermute | solution.py:12
  66.1 2.9 %collective-permute-done.22 = s16[200,512]{1,0:T(8,128)(2,1)S(1)} collective-permute-done((s16[200,512]{1,0:T(8,128)(2,1)S(1)}, s16[200,512]{1,0:T(8,128)(2,1)S(1)}, u32[]{:S(2)}, u32[]{:S(2)}) %collective-permute-start.22) | collective-permute-done | bytes 204832 | tf_op jit(solution)/shard_map/ppermute | solution.py:103
  70.1 1.6 %collective-permute-start.23 = (bf16[2,192,128]{2,1,0:T(8,128)(2,1)S(1)}, bf16[2,192,128]{2,1,0:T(8,128)(2,1)S(1)}, u32[]{:S(2)}, u32[]{:S(2)}) collective-permute-start(bf16[2,192,128]{2,1,0:T(8,128)(2,1)S(1)} %get-tuple-element.27), channel_id=1, source_target_pairs={{0,12},{4,0},{8,4},{12,8},{1,13},{5,1},{9,5},{13,9},{2,14},{6,2},{... | collective-permute-start | bytes 294920 | tf_op jit(solution)/shard_map/ppermute | solution.py:12
  73.4 1.4 %collective-permute-done.23 = bf16[2,192,128]{2,1,0:T(8,128)(2,1)S(1)} collective-permute-done((bf16[2,192,128]{2,1,0:T(8,128)(2,1)S(1)}, bf16[2,192,128]{2,1,0:T(8,128)(2,1)S(1)}, u32[]{:S(2)}, u32[]{:S(2)}) %collective-permute-start.23) | collective-permute-done | bytes 98336 | tf_op jit(solution)/shard_map/ppermute | solution.py:12
  74.8 3.1 %collective-permute-done.24 = bf16[2,192,128]{2,1,0:T(8,128)(2,1)S(1)} collective-permute-done((bf16[2,192,128]{2,1,0:T(8,128)(2,1)S(1)}, bf16[2,192,128]{2,1,0:T(8,128)(2,1)S(1)}, u32[]{:S(2)}, u32[]{:S(2)}) %collective-permute-start.24) | collective-permute-done | bytes 98336 | tf_op jit(solution)/shard_map/ppermute | solution.py:12
  (93 shorter events, 20.5 us)
Async XLA Ops:
  2.8 6.7 %collective-permute-start = (bf16[24,4096]{1,0:T(8,128)(2,1)S(1)}, bf16[24,4096]{1,0:T(8,128)(2,1)S(1)}, u32[]{:S(2)}, u32[]{:S(2)}) collective-permute-start(bf16[24,4096]{1,0:T(8,128)(2,1)S(1)} %pad_maximum_fusion.3), channel_id=1, source_target_pairs={{0,2},{2,0},{1,3},{3,1},{4,6},{6,4},{5,7},{7,5},{8,10},{10,8},{9,1... | collective-permute-start | bytes 589832 | tf_op jit(solution)/shard_map/ppermute | solution.py:12
  3.6 14.8 %collective-permute-start.11 = (bf16[128,2048]{1,0:T(8,128)(2,1)}, bf16[128,2048]{1,0:T(8,128)(2,1)S(1)}, u32[]{:S(2)}, u32[]{:S(2)}) collective-permute-start(bf16[128,2048]{1,0:T(8,128)(2,1)} %param.6), channel_id=1, source_target_pairs={{0,4},{4,8},{8,12},{12,0},{1,5},{5,9},{9,13},{13,1},{2,6},{6,10},{... | collective-permute-start | bytes 1572872 | tf_op jit(solution)/shard_map/ppermute | solution.py:12
  5.1 13.7 %collective-permute-start.13 = (bf16[128,2048]{1,0:T(8,128)(2,1)}, bf16[128,2048]{1,0:T(8,128)(2,1)S(1)}, u32[]{:S(2)}, u32[]{:S(2)}) collective-permute-start(bf16[128,2048]{1,0:T(8,128)(2,1)} %param.6), channel_id=1, source_target_pairs={{0,12},{4,0},{8,4},{12,8},{1,13},{5,1},{9,5},{13,9},{2,14},{6,2},{... | collective-permute-start | bytes 1572872 | tf_op jit(solution)/shard_map/ppermute | solution.py:12
  9.6 14.2 %collective-permute-start.1 = (bf16[48,4096]{1,0:T(8,128)(2,1)S(1)}, bf16[48,4096]{1,0:T(8,128)(2,1)S(1)}, u32[]{:S(2)}, u32[]{:S(2)}) collective-permute-start(bf16[48,4096]{1,0:T(8,128)(2,1)S(1)} %pad_maximum_fusion.2), channel_id=1, source_target_pairs={{0,32},{32,64},{64,96},{96,128},{128,160},{160,192},{192,224},{224... | collective-permute-start | bytes 1179656 | tf_op jit(solution)/shard_map/ppermute | solution.py:12
  11.6 12.4 %collective-permute-start.2 = (bf16[48,4096]{1,0:T(8,128)(2,1)S(1)}, bf16[48,4096]{1,0:T(8,128)(2,1)S(1)}, u32[]{:S(2)}, u32[]{:S(2)}) collective-permute-start(bf16[48,4096]{1,0:T(8,128)(2,1)S(1)} %pad_maximum_fusion.2), channel_id=1, source_target_pairs={{0,224},{32,0},{64,32},{96,64},{128,96},{160,128},{192,160},{224,1... | collective-permute-start | bytes 1179656 | tf_op jit(solution)/shard_map/ppermute | solution.py:12
  15.6 14.0 %collective-permute-start.9 = (bf16[128,2048]{1,0:T(8,128)(2,1)S(1)}, bf16[128,2048]{1,0:T(8,128)(2,1)S(1)}, u32[]{:S(2)}, u32[]{:S(2)}) collective-permute-start(bf16[128,2048]{1,0:T(8,128)(2,1)S(1)} %copy-done), channel_id=1, source_target_pairs={{0,16},{16,0},{1,17},{17,1},{2,18},{18,2},{3,19},{19,3},{4,20},{20... | collective-permute-start | bytes 1572872 | tf_op jit(solution)/shard_map/ppermute | solution.py:12
  18.5 12.6 %collective-permute-start.12 = (bf16[64,2048]{1,0:T(8,128)(2,1)S(1)}, bf16[64,2048]{1,0:T(8,128)(2,1)S(1)}, u32[]{:S(2)}, u32[]{:S(2)}) collective-permute-start(bf16[64,2048]{1,0:T(8,128)(2,1)S(1)} %slice.101), channel_id=1, source_target_pairs={{0,4},{4,8},{8,12},{12,0},{1,5},{5,9},{9,13},{13,1},{2,6},{6,10},{... | collective-permute-start | bytes 786440 | tf_op jit(solution)/shard_map/ppermute | solution.py:12
  18.9 14.0 %collective-permute-start.14 = (bf16[64,2048]{1,0:T(8,128)(2,1)S(1)}, bf16[64,2048]{1,0:T(8,128)(2,1)S(1)}, u32[]{:S(2)}, u32[]{:S(2)}) collective-permute-start(bf16[64,2048]{1,0:T(8,128)(2,1)S(1)} %slice.102), channel_id=1, source_target_pairs={{0,12},{4,0},{8,4},{12,8},{1,13},{5,1},{9,5},{13,9},{2,14},{6,2},{... | collective-permute-start | bytes 786440 | tf_op jit(solution)/shard_map/ppermute | solution.py:12
  23.7 11.5 %collective-permute-start.3 = (bf16[48,4096]{1,0:T(8,128)(2,1)S(1)}, bf16[48,4096]{1,0:T(8,128)(2,1)S(1)}, u32[]{:S(2)}, u32[]{:S(2)}) collective-permute-start(bf16[48,4096]{1,0:T(8,128)(2,1)S(1)} %collective-permute-done.1), channel_id=1, source_target_pairs={{0,32},{32,64},{64,96},{96,128},{128,160},{160,192},{192,224},{224... | collective-permute-start | bytes 1179656 | tf_op jit(solution)/shard_map/ppermute | solution.py:12
  23.9 11.3 %collective-permute-start.4 = (bf16[48,4096]{1,0:T(8,128)(2,1)S(1)}, bf16[48,4096]{1,0:T(8,128)(2,1)S(1)}, u32[]{:S(2)}, u32[]{:S(2)}) collective-permute-start(bf16[48,4096]{1,0:T(8,128)(2,1)S(1)} %collective-permute-done.2), channel_id=1, source_target_pairs={{0,224},{32,0},{64,32},{96,64},{128,96},{160,128},{192,160},{224,1... | collective-permute-start | bytes 1179656 | tf_op jit(solution)/shard_map/ppermute | solution.py:12
  29.6 12.8 %collective-permute-start.10 = (bf16[128,2048]{1,0:T(8,128)(2,1)S(1)}, bf16[128,2048]{1,0:T(8,128)(2,1)S(1)}, u32[]{:S(2)}, u32[]{:S(2)}) collective-permute-start(bf16[128,2048]{1,0:T(8,128)(2,1)S(1)} %collective-permute-done.9), channel_id=1, source_target_pairs={{0,4},{4,8},{8,12},{12,0},{1,5},{5,9},{9,13},{13,1},{2,6},{6,10},{... | collective-permute-start | bytes 1572872 | tf_op jit(solution)/shard_map/ppermute | solution.py:12
  31.1 11.3 %collective-permute-start.16 = (bf16[128,2048]{1,0:T(8,128)(2,1)S(1)}, bf16[128,2048]{1,0:T(8,128)(2,1)S(1)}, u32[]{:S(2)}, u32[]{:S(2)}) collective-permute-start(bf16[128,2048]{1,0:T(8,128)(2,1)S(1)} %collective-permute-done.9), channel_id=1, source_target_pairs={{0,12},{4,0},{8,4},{12,8},{1,13},{5,1},{9,5},{13,9},{2,14},{6,2},{... | collective-permute-start | bytes 1572872 | tf_op jit(solution)/shard_map/ppermute | solution.py:12
  32.9 12.6 %collective-permute-start.15 = (bf16[128,2048]{1,0:T(8,128)(2,1)S(1)}, bf16[128,2048]{1,0:T(8,128)(2,1)S(1)}, u32[]{:S(2)}, u32[]{:S(2)}) collective-permute-start(bf16[128,2048]{1,0:T(8,128)(2,1)S(1)} %pad_maximum_fusion.1), channel_id=1, source_target_pairs={{0,16},{16,0},{1,17},{17,1},{2,18},{18,2},{3,19},{19,3},{4,20},{20... | collective-permute-start | bytes 1572872 | tf_op jit(solution)/shard_map/ppermute | solution.py:12
  35.2 10.3 %collective-permute-start.5 = (bf16[48,4096]{1,0:T(8,128)(2,1)S(1)}, bf16[48,4096]{1,0:T(8,128)(2,1)S(1)}, u32[]{:S(2)}, u32[]{:S(2)}) collective-permute-start(bf16[48,4096]{1,0:T(8,128)(2,1)S(1)} %collective-permute-done.3), channel_id=1, source_target_pairs={{0,32},{32,64},{64,96},{96,128},{128,160},{160,192},{192,224},{224... | collective-permute-start | bytes 1179656 | tf_op jit(solution)/shard_map/ppermute | solution.py:12
  35.2 10.4 %collective-permute-start.6 = (bf16[48,4096]{1,0:T(8,128)(2,1)S(1)}, bf16[48,4096]{1,0:T(8,128)(2,1)S(1)}, u32[]{:S(2)}, u32[]{:S(2)}) collective-permute-start(bf16[48,4096]{1,0:T(8,128)(2,1)S(1)} %collective-permute-done.4), channel_id=1, source_target_pairs={{0,224},{32,0},{64,32},{96,64},{128,96},{160,128},{192,160},{224,1... | collective-permute-start | bytes 1179656 | tf_op jit(solution)/shard_map/ppermute | solution.py:12
  42.4 17.3 %collective-permute-start.19 = (bf16[512,2048]{1,0:T(8,128)(2,1)S(1)}, bf16[512,2048]{1,0:T(8,128)(2,1)S(1)}, u32[]{:S(2)}, u32[]{:S(2)}) collective-permute-start(bf16[512,2048]{1,0:T(8,128)(2,1)S(1)} %constant_dynamic-update-slice_fusion), channel_id=1, source_target_pairs={{0,1},{1,0},{2,3},{3,2},{4,5},{5,4},{6,7},{7,6},{8,9},{9,8},{10,11... | collective-permute-start | bytes 6291464 | tf_op jit(solution)/shard_map/ppermute | solution.py:12
  42.5 11.7 %collective-permute-start.17 = (bf16[384,2048]{1,0:T(8,128)(2,1)S(1)}, bf16[384,2048]{1,0:T(8,128)(2,1)S(1)}, u32[]{:S(2)}, u32[]{:S(2)}) collective-permute-start(bf16[384,2048]{1,0:T(8,128)(2,1)S(1)} %pad_maximum_fusion), channel_id=1, source_target_pairs={{0,1},{1,0},{2,3},{3,2},{4,5},{5,4},{6,7},{7,6},{8,9},{9,8},{10,11... | collective-permute-start | bytes 4718600 | tf_op jit(solution)/shard_map/ppermute | solution.py:12
  45.5 8.8 %collective-permute-start.18 = (bf16[128,2048]{1,0:T(8,128)(2,1)S(1)}, bf16[128,2048]{1,0:T(8,128)(2,1)S(1)}, u32[]{:S(2)}, u32[]{:S(2)}) collective-permute-start(bf16[128,2048]{1,0:T(8,128)(2,1)S(1)} %collective-permute-done.15), channel_id=1, source_target_pairs={{0,1},{1,0},{2,3},{3,2},{4,5},{5,4},{6,7},{7,6},{8,9},{9,8},{10,11... | collective-permute-start | bytes 1572872 | tf_op jit(solution)/shard_map/ppermute | solution.py:12
  45.5 8.6 %collective-permute-start.7 = (bf16[24,4096]{1,0:T(8,128)(2,1)S(1)}, bf16[24,4096]{1,0:T(8,128)(2,1)S(1)}, u32[]{:S(2)}, u32[]{:S(2)}) collective-permute-start(bf16[24,4096]{1,0:T(8,128)(2,1)S(1)} %slice.98), channel_id=1, source_target_pairs={{0,32},{32,64},{64,96},{96,128},{128,160},{160,192},{192,224},{224... | collective-permute-start | bytes 589832 | tf_op jit(solution)/shard_map/ppermute | solution.py:12
  45.7 8.5 %collective-permute-start.8 = (bf16[24,4096]{1,0:T(8,128)(2,1)S(1)}, bf16[24,4096]{1,0:T(8,128)(2,1)S(1)}, u32[]{:S(2)}, u32[]{:S(2)}) collective-permute-start(bf16[24,4096]{1,0:T(8,128)(2,1)S(1)} %slice.99), channel_id=1, source_target_pairs={{0,224},{32,0},{64,32},{96,64},{128,96},{160,128},{192,160},{224,1... | collective-permute-start | bytes 589832 | tf_op jit(solution)/shard_map/ppermute | solution.py:12
  56.6 12.4 %collective-permute-start.22 = (s16[200,512]{1,0:T(8,128)(2,1)S(1)}, s16[200,512]{1,0:T(8,128)(2,1)S(1)}, u32[]{:S(2)}, u32[]{:S(2)}) collective-permute-start(s16[200,512]{1,0:T(8,128)(2,1)S(1)} %pad_add_fusion), channel_id=1, source_target_pairs={{0,18},{2,16},{16,2},{18,0},{1,19},{3,17},{17,3},{19,1},{4,22},{6,... | collective-permute-start | bytes 614408 | tf_op jit(solution)/shard_map/ppermute | solution.py:103
  57.0 9.0 %collective-permute-start.21 = (s16[200,512]{1,0:T(8,128)(2,1)S(1)}, s16[200,512]{1,0:T(8,128)(2,1)S(1)}, u32[]{:S(2)}, u32[]{:S(2)}) collective-permute-start(s16[200,512]{1,0:T(8,128)(2,1)S(1)} %pad_add_fusion.2), channel_id=1, source_target_pairs={{0,16},{16,0},{1,17},{17,1},{2,18},{18,2},{3,19},{19,3},{4,20},{20... | collective-permute-start | bytes 614408 | tf_op jit(solution)/shard_map/ppermute | solution.py:12
  61.9 7.9 %collective-permute-start.20 = (s16[200,512]{1,0:T(8,128)(2,1)S(1)}, s16[200,512]{1,0:T(8,128)(2,1)S(1)}, u32[]{:S(2)}, u32[]{:S(2)}) collective-permute-start(s16[200,512]{1,0:T(8,128)(2,1)S(1)} %pad_add_fusion.1), channel_id=1, source_target_pairs={{0,2},{2,0},{1,3},{3,1},{4,6},{6,4},{5,7},{7,5},{8,10},{10,8},{9,1... | collective-permute-start | bytes 614408 | tf_op jit(solution)/shard_map/ppermute | solution.py:12
  72.5 6.4 %collective-permute-start.25 = (bf16[2,192,128]{2,1,0:T(8,128)(2,1)S(1)}, bf16[2,192,128]{2,1,0:T(8,128)(2,1)S(1)}, u32[]{:S(2)}, u32[]{:S(2)}) collective-permute-start(bf16[2,192,128]{2,1,0:T(8,128)(2,1)S(1)} %get-tuple-element.28), channel_id=1, source_target_pairs={{0,4},{4,8},{8,12},{12,0},{1,5},{5,9},{9,13},{13,1},{2,6},{6,10},{... | collective-permute-start | bytes 294920 | tf_op jit(solution)/shard_map/ppermute | solution.py:12
  (5 other events, 46.9 us)

commit v7 on v6

--- a/solution.py
+++ b/solution.py
@@ -27,14 +27,8 @@
     at = {name: lax.axis_index(name) for name in AXES}
     l, k = at["l"], at["k"]
 
-    first = ((at["z"] * 2 + at["h"]) * 4 + at["x"]) * rows
-    slab_labels = lax.dynamic_slice_in_dim(ij_symmetry, first, rows)
-
     def columns(l, k):
-        start = (l * 2 + k) * width
-        labels = lax.dynamic_slice_in_dim(cd_symmetry, start, width)
-        part = lax.dynamic_slice_in_dim(amplitudes, start, width, axis=1)
-        return jnp.where(slab_labels[:, None] == labels[None, :], part, jnp.zeros_like(part))
+        return lax.dynamic_slice_in_dim(amplitudes, (l * 2 + k) * width, width, axis=1)
 
     def chip_columns(l):
         return jnp.concatenate([columns(l, k), columns(l, 1 - k)], axis=1)
@@ -52,7 +46,14 @@
     opposite = lax.optimization_barrier(opposite)
     lines = jnp.zeros((8, 2 * rows, 2 * width), amplitudes.dtype)
     blocks = [slabs, up[1], down[1], up[2], down[2], up[3], down[3], jnp.concatenate(opposite, axis=0)]
+    start = l * 2 * width
+    cd_labels = [lax.dynamic_slice_in_dim(cd_symmetry, start + i * width, width) for i in (k, 1 - k)]
+    cd_labels = jnp.concatenate(cd_labels)
+    labels = lax.dynamic_index_in_dim(ij_symmetry.reshape(8, 8, rows), at["h"] * 4 + at["x"], 1, keepdims=False)
+    labels = jnp.concatenate([labels, shift(labels, "l", 1)], axis=1)
     for step, block in zip((0, -1, 1, -2, 2, -3, 3, 4), blocks):
+        label = lax.dynamic_index_in_dim(labels, (at["z"] + step) % 8, 0, keepdims=False)
+        block = jnp.where(label[:, None] == cd_labels[None, :], block, jnp.zeros_like(block))
         lines = lax.dynamic_update_index_in_dim(lines, block, (at["z"] + step) % 8, 0)
     lines = lines.reshape(16 * rows, 2 * width)
 

time: 80.6 us -> 80 us (level)
  waiting for transfers between devices: 30.2 us -> 28.4 us
  local copies, waits for them, and re-layouts: 3.64 us -> 5.3 us
    ppermute x25 -> x26, waiting for transfers between devices: 27.3 us -> 25.5 us  [shift(): lax.ppermute(value, axis, [(i, (i + step) % size) for i in range(size)])]
    dynamic_update_slice x2 -> x8, other arithmetic: 0.06 us -> 1.29 us  [local(): lax.dynamic_update_index_in_dim(lines, block, (at['z'] + step) % 8, 0)]
    select_n x1 -> x0, other arithmetic: 1.2 us -> none  [columns(): jnp.where(slab_labels[:, None] == labels[None, :], part, jnp.zeros_like(p...]
    unnamed x10 -> x12, local copies, waits for them, and re-layouts: 1.2 us -> 1.99 us
    ppermute x25 -> x26, starting transfers between devices: 38.1 us -> 37.5 us  [shift(): lax.ppermute(value, axis, [(i, (i + step) % size) for i in range(size)])]
    dynamic_slice x2 -> x4, local copies, waits for them, and re-layouts: 1.58 us -> 1.87 us  [the longest x1 1.12 us: columns(): lax.dynamic_slice_in_dim(amplitudes, (l * 2 + k) * width, width, axis=1)]
  transfers between devices with their start and end apart: 26 -> 27, of which waited for: 14 -> 11; matrix products, arithmetic and copies ran while one was open for 9% -> 13% of each run, Pallas kernels for 0% -> 0%
where the time goes in v7:
time: 80 us; the launch traced here: 79.7 us
  starting transfers between devices  37.6 us (47%)
  waiting for transfers between devices  28.4 us (36%)
  local copies, waits for them, and re-layouts  5.3 us (7%)
  matrix products  4.04 us (5%)
  other arithmetic  3.82 us (5%)
    ppermute x26, starting transfers between devices, shift(): lax.ppermute(value, axis, [(i, (i + step) % size) for i in range(size)])  37.5 us
    ppermute x26, waiting for transfers between devices, shift(): lax.ppermute(value, axis, [(i, (i + step) % size) for i in range(size)])  25.5 us
    dot_general x4, matrix products, product(): lax.dot_general(line, block, (((1,), (1,)), ((), ())), preferred_element_...  4.04 us
    ppermute x1, waiting for transfers between devices, local(): got_hl = lax.ppermute(to_hl, ('h', 'l'), [(0, 3), (1, 2), (2, 1), (3, 0)])  2.91 us
    unnamed x12, local copies, waits for them, and re-layouts  1.99 us
  transfers between devices with their start and end apart: 27, of which 11 were waited for; matrix products, arithmetic and copies ran while one was open for 13% of the time, Pallas kernels for 0%

profile of v7, /device:TPU:24, one launch (start us, length us, event | category | flops | bytes accessed | tf_op | source)
XLA Modules:
  0.0 79.7 jit_solution(9175098944251247806)
XLA Ops:
  2.0 1.5 %collective-permute-start.12 = (bf16[128,2048]{1,0:T(8,128)(2,1)}, bf16[128,2048]{1,0:T(8,128)(2,1)S(1)}, u32[]{:S(2)}, u32[]{:S(2)}) collective-permute-start(bf16[128,2048]{1,0:T(8,128)(2,1)} %param.6), channel_id=1, source_target_pairs={{0,4},{4,8},{8,12},{12,0},{1,5},{5,9},{9,13},{13,1},{2,6},{6,10},{... | collective-permute-start | bytes 1572872 | tf_op jit(solution)/shard_map/ppermute | solution.py:12
  3.5 1.7 %collective-permute-start.14 = (bf16[128,2048]{1,0:T(8,128)(2,1)}, bf16[128,2048]{1,0:T(8,128)(2,1)S(1)}, u32[]{:S(2)}, u32[]{:S(2)}) collective-permute-start(bf16[128,2048]{1,0:T(8,128)(2,1)} %param.6), channel_id=1, source_target_pairs={{0,12},{4,0},{8,4},{12,8},{1,13},{5,1},{9,5},{13,9},{2,14},{6,2},{... | collective-permute-start | bytes 1572872 | tf_op jit(solution)/shard_map/ppermute | solution.py:12
  6.0 1.4 %collective-permute-start = (s32[8,24]{1,0:T(8,128)S(1)}, s32[8,24]{1,0:T(8,128)S(1)}, u32[]{:S(2)}, u32[]{:S(2)}) collective-permute-start(s32[8,24]{1,0:T(8,128)S(1)} %bitcast.99), channel_id=1, source_target_pairs={{0,2},{2,0},{1,3},{3,1},{4,6},{6,4},{5,7},{7,5},{8,10},{10,8},{9,1... | collective-permute-start | bytes 2312 | tf_op jit(solution)/shard_map/ppermute | solution.py:12
  7.4 1.9 %constant_dynamic-update-slice_fusion.4 = bf16[512,2048]{1,0:T(8,128)(2,1)} fusion(bf16[128,2048]{1,0:T(8,128)(2,1)} %param.6), kind=kLoop, calls=%fused_computation.95 | loop fusion | bytes 1048576
  10.2 2.0 %collective-permute-start.2 = (bf16[48,4096]{1,0:T(8,128)(2,1)S(1)}, bf16[48,4096]{1,0:T(8,128)(2,1)S(1)}, u32[]{:S(2)}, u32[]{:S(2)}) collective-permute-start(bf16[48,4096]{1,0:T(8,128)(2,1)S(1)} %pad_maximum_fusion.2), channel_id=1, source_target_pairs={{0,32},{32,64},{64,96},{96,128},{128,160},{160,192},{192,224},{224... | collective-permute-start | bytes 1179656 | tf_op jit(solution)/shard_map/ppermute | solution.py:12
  12.2 4.0 %collective-permute-start.3 = (bf16[48,4096]{1,0:T(8,128)(2,1)S(1)}, bf16[48,4096]{1,0:T(8,128)(2,1)S(1)}, u32[]{:S(2)}, u32[]{:S(2)}) collective-permute-start(bf16[48,4096]{1,0:T(8,128)(2,1)S(1)} %pad_maximum_fusion.2), channel_id=1, source_target_pairs={{0,224},{32,0},{64,32},{96,64},{128,96},{160,128},{192,160},{224,1... | collective-permute-start | bytes 1179656 | tf_op jit(solution)/shard_map/ppermute | solution.py:12
  16.2 1.2 %collective-permute-start.10 = (bf16[128,2048]{1,0:T(8,128)(2,1)S(1)}, bf16[128,2048]{1,0:T(8,128)(2,1)S(1)}, u32[]{:S(2)}, u32[]{:S(2)}) collective-permute-start(bf16[128,2048]{1,0:T(8,128)(2,1)S(1)} %copy-done), channel_id=1, source_target_pairs={{0,16},{16,0},{1,17},{17,1},{2,18},{18,2},{3,19},{19,3},{4,20},{20... | collective-permute-start | bytes 1572872 | tf_op jit(solution)/shard_map/ppermute | solution.py:12
  18.4 3.0 %collective-permute-start.15 = (bf16[64,2048]{1,0:T(8,128)(2,1)S(1)}, bf16[64,2048]{1,0:T(8,128)(2,1)S(1)}, u32[]{:S(2)}, u32[]{:S(2)}) collective-permute-start(bf16[64,2048]{1,0:T(8,128)(2,1)S(1)} %slice.102), channel_id=1, source_target_pairs={{0,12},{4,0},{8,4},{12,8},{1,13},{5,1},{9,5},{13,9},{2,14},{6,2},{... | collective-permute-start | bytes 786440 | tf_op jit(solution)/shard_map/ppermute | solution.py:12
  21.5 2.6 %collective-permute-done.2 = bf16[48,4096]{1,0:T(8,128)(2,1)S(1)} collective-permute-done((bf16[48,4096]{1,0:T(8,128)(2,1)S(1)}, bf16[48,4096]{1,0:T(8,128)(2,1)S(1)}, u32[]{:S(2)}, u32[]{:S(2)}) %collective-permute-start.2) | collective-permute-done | bytes 393248 | tf_op jit(solution)/shard_map/ppermute | solution.py:12
  24.1 3.2 %collective-permute-start.5 = (bf16[48,4096]{1,0:T(8,128)(2,1)S(1)}, bf16[48,4096]{1,0:T(8,128)(2,1)S(1)}, u32[]{:S(2)}, u32[]{:S(2)}) collective-permute-start(bf16[48,4096]{1,0:T(8,128)(2,1)S(1)} %collective-permute-done.3), channel_id=1, source_target_pairs={{0,224},{32,0},{64,32},{96,64},{128,96},{160,128},{192,160},{224,1... | collective-permute-start | bytes 1179656 | tf_op jit(solution)/shard_map/ppermute | solution.py:12
  27.7 2.3 %collective-permute-done.10 = bf16[128,2048]{1,0:T(8,128)(2,1)S(1)} collective-permute-done((bf16[128,2048]{1,0:T(8,128)(2,1)S(1)}, bf16[128,2048]{1,0:T(8,128)(2,1)S(1)}, u32[]{:S(2)}, u32[]{:S(2)}) %collective-permute-start.10) | collective-permute-done | bytes 524320 | tf_op jit(solution)/shard_map/ppermute | solution.py:12
  30.3 3.0 %collective-permute-start.17 = (bf16[128,2048]{1,0:T(8,128)(2,1)S(1)}, bf16[128,2048]{1,0:T(8,128)(2,1)S(1)}, u32[]{:S(2)}, u32[]{:S(2)}) collective-permute-start(bf16[128,2048]{1,0:T(8,128)(2,1)S(1)} %collective-permute-done.10), channel_id=1, source_target_pairs={{0,12},{4,0},{8,4},{12,8},{1,13},{5,1},{9,5},{13,9},{2,14},{6,2},{... | collective-permute-start | bytes 1572872 | tf_op jit(solution)/shard_map/ppermute | solution.py:12
  33.3 1.3 %collective-permute-start.16 = (bf16[128,2048]{1,0:T(8,128)(2,1)S(1)}, bf16[128,2048]{1,0:T(8,128)(2,1)S(1)}, u32[]{:S(2)}, u32[]{:S(2)}) collective-permute-start(bf16[128,2048]{1,0:T(8,128)(2,1)S(1)} %pad_maximum_fusion.1), channel_id=1, source_target_pairs={{0,16},{16,0},{1,17},{17,1},{2,18},{18,2},{3,19},{19,3},{4,20},{20... | collective-permute-start | bytes 1572872 | tf_op jit(solution)/shard_map/ppermute | solution.py:12
  34.8 3.2 %collective-permute-start.7 = (bf16[48,4096]{1,0:T(8,128)(2,1)S(1)}, bf16[48,4096]{1,0:T(8,128)(2,1)S(1)}, u32[]{:S(2)}, u32[]{:S(2)}) collective-permute-start(bf16[48,4096]{1,0:T(8,128)(2,1)S(1)} %collective-permute-done.5), channel_id=1, source_target_pairs={{0,224},{32,0},{64,32},{96,64},{128,96},{160,128},{192,160},{224,1... | collective-permute-start | bytes 1179656 | tf_op jit(solution)/shard_map/ppermute | solution.py:12
  38.3 4.2 %collective-permute-done.11 = bf16[128,2048]{1,0:T(8,128)(2,1)S(1)} collective-permute-done((bf16[128,2048]{1,0:T(8,128)(2,1)S(1)}, bf16[128,2048]{1,0:T(8,128)(2,1)S(1)}, u32[]{:S(2)}, u32[]{:S(2)}) %collective-permute-start.11) | collective-permute-done | bytes 524320 | tf_op jit(solution)/shard_map/ppermute | solution.py:12
  43.2 2.4 %collective-permute-done.16 = bf16[128,2048]{1,0:T(8,128)(2,1)S(1)} collective-permute-done((bf16[128,2048]{1,0:T(8,128)(2,1)S(1)}, bf16[128,2048]{1,0:T(8,128)(2,1)S(1)}, u32[]{:S(2)}, u32[]{:S(2)}) %collective-permute-start.16) | collective-permute-done | bytes 524320 | tf_op jit(solution)/shard_map/ppermute | solution.py:12
  45.8 3.3 %collective-permute-start.9 = (bf16[24,4096]{1,0:T(8,128)(2,1)S(1)}, bf16[24,4096]{1,0:T(8,128)(2,1)S(1)}, u32[]{:S(2)}, u32[]{:S(2)}) collective-permute-start(bf16[24,4096]{1,0:T(8,128)(2,1)S(1)} %slice.99), channel_id=1, source_target_pairs={{0,224},{32,0},{64,32},{96,64},{128,96},{160,128},{192,160},{224,1... | collective-permute-start | bytes 589832 | tf_op jit(solution)/shard_map/ppermute | solution.py:12
  49.4 4.9 %collective-permute-done.8 = bf16[24,4096]{1,0:T(8,128)(2,1)S(1)} collective-permute-done((bf16[24,4096]{1,0:T(8,128)(2,1)S(1)}, bf16[24,4096]{1,0:T(8,128)(2,1)S(1)}, u32[]{:S(2)}, u32[]{:S(2)}) %collective-permute-start.8) | collective-permute-done | bytes 196640 | tf_op jit(solution)/shard_map/ppermute | solution.py:12
  57.1 2.7 %collective-permute-start.22 = (s16[200,512]{1,0:T(8,128)(2,1)S(1)}, s16[200,512]{1,0:T(8,128)(2,1)S(1)}, u32[]{:S(2)}, u32[]{:S(2)}) collective-permute-start(s16[200,512]{1,0:T(8,128)(2,1)S(1)} %pad_add_fusion.2), channel_id=1, source_target_pairs={{0,16},{16,0},{1,17},{17,1},{2,18},{18,2},{3,19},{19,3},{4,20},{20... | collective-permute-start | bytes 614408 | tf_op jit(solution)/shard_map/ppermute | solution.py:12
  62.0 1.6 %collective-permute-start.21 = (s16[200,512]{1,0:T(8,128)(2,1)S(1)}, s16[200,512]{1,0:T(8,128)(2,1)S(1)}, u32[]{:S(2)}, u32[]{:S(2)}) collective-permute-start(s16[200,512]{1,0:T(8,128)(2,1)S(1)} %pad_add_fusion.1), channel_id=1, source_target_pairs={{0,2},{2,0},{1,3},{3,1},{4,6},{6,4},{5,7},{7,5},{8,10},{10,8},{9,1... | collective-permute-start | bytes 614408 | tf_op jit(solution)/shard_map/ppermute | solution.py:12
  63.6 2.7 %collective-permute-done.22 = s16[200,512]{1,0:T(8,128)(2,1)S(1)} collective-permute-done((s16[200,512]{1,0:T(8,128)(2,1)S(1)}, s16[200,512]{1,0:T(8,128)(2,1)S(1)}, u32[]{:S(2)}, u32[]{:S(2)}) %collective-permute-start.22) | collective-permute-done | bytes 204832 | tf_op jit(solution)/shard_map/ppermute | solution.py:12
  66.3 2.9 %collective-permute-done.23 = s16[200,512]{1,0:T(8,128)(2,1)S(1)} collective-permute-done((s16[200,512]{1,0:T(8,128)(2,1)S(1)}, s16[200,512]{1,0:T(8,128)(2,1)S(1)}, u32[]{:S(2)}, u32[]{:S(2)}) %collective-permute-start.23) | collective-permute-done | bytes 204832 | tf_op jit(solution)/shard_map/ppermute | solution.py:104
  72.4 2.6 %collective-permute-done.24 = bf16[2,192,128]{2,1,0:T(8,128)(2,1)S(1)} collective-permute-done((bf16[2,192,128]{2,1,0:T(8,128)(2,1)S(1)}, bf16[2,192,128]{2,1,0:T(8,128)(2,1)S(1)}, u32[]{:S(2)}, u32[]{:S(2)}) %collective-permute-start.24) | collective-permute-done | bytes 98336 | tf_op jit(solution)/shard_map/ppermute | solution.py:12
  75.0 2.6 %collective-permute-done.25 = bf16[2,192,128]{2,1,0:T(8,128)(2,1)S(1)} collective-permute-done((bf16[2,192,128]{2,1,0:T(8,128)(2,1)S(1)}, bf16[2,192,128]{2,1,0:T(8,128)(2,1)S(1)}, u32[]{:S(2)}, u32[]{:S(2)}) %collective-permute-start.25) | collective-permute-done | bytes 98336 | tf_op jit(solution)/shard_map/ppermute | solution.py:12
  (102 shorter events, 17.0 us)
Async XLA Ops:
  1.1 9.0 %collective-permute-start.1 = (bf16[24,4096]{1,0:T(8,128)(2,1)S(1)}, bf16[24,4096]{1,0:T(8,128)(2,1)S(1)}, u32[]{:S(2)}, u32[]{:S(2)}) collective-permute-start(bf16[24,4096]{1,0:T(8,128)(2,1)S(1)} %pad_maximum_fusion.3), channel_id=1, source_target_pairs={{0,2},{2,0},{1,3},{3,1},{4,6},{6,4},{5,7},{7,5},{8,10},{10,8},{9,1... | collective-permute-start | bytes 589832 | tf_op jit(solution)/shard_map/ppermute | solution.py:12
  2.0 16.0 %collective-permute-start.12 = (bf16[128,2048]{1,0:T(8,128)(2,1)}, bf16[128,2048]{1,0:T(8,128)(2,1)S(1)}, u32[]{:S(2)}, u32[]{:S(2)}) collective-permute-start(bf16[128,2048]{1,0:T(8,128)(2,1)} %param.6), channel_id=1, source_target_pairs={{0,4},{4,8},{8,12},{12,0},{1,5},{5,9},{9,13},{13,1},{2,6},{6,10},{... | collective-permute-start | bytes 1572872 | tf_op jit(solution)/shard_map/ppermute | solution.py:12
  3.5 14.9 %collective-permute-start.14 = (bf16[128,2048]{1,0:T(8,128)(2,1)}, bf16[128,2048]{1,0:T(8,128)(2,1)S(1)}, u32[]{:S(2)}, u32[]{:S(2)}) collective-permute-start(bf16[128,2048]{1,0:T(8,128)(2,1)} %param.6), channel_id=1, source_target_pairs={{0,12},{4,0},{8,4},{12,8},{1,13},{5,1},{9,5},{13,9},{2,14},{6,2},{... | collective-permute-start | bytes 1572872 | tf_op jit(solution)/shard_map/ppermute | solution.py:12
  10.2 13.9 %collective-permute-start.2 = (bf16[48,4096]{1,0:T(8,128)(2,1)S(1)}, bf16[48,4096]{1,0:T(8,128)(2,1)S(1)}, u32[]{:S(2)}, u32[]{:S(2)}) collective-permute-start(bf16[48,4096]{1,0:T(8,128)(2,1)S(1)} %pad_maximum_fusion.2), channel_id=1, source_target_pairs={{0,32},{32,64},{64,96},{96,128},{128,160},{160,192},{192,224},{224... | collective-permute-start | bytes 1179656 | tf_op jit(solution)/shard_map/ppermute | solution.py:12
  12.2 11.9 %collective-permute-start.3 = (bf16[48,4096]{1,0:T(8,128)(2,1)S(1)}, bf16[48,4096]{1,0:T(8,128)(2,1)S(1)}, u32[]{:S(2)}, u32[]{:S(2)}) collective-permute-start(bf16[48,4096]{1,0:T(8,128)(2,1)S(1)} %pad_maximum_fusion.2), channel_id=1, source_target_pairs={{0,224},{32,0},{64,32},{96,64},{128,96},{160,128},{192,160},{224,1... | collective-permute-start | bytes 1179656 | tf_op jit(solution)/shard_map/ppermute | solution.py:12
  16.2 13.8 %collective-permute-start.10 = (bf16[128,2048]{1,0:T(8,128)(2,1)S(1)}, bf16[128,2048]{1,0:T(8,128)(2,1)S(1)}, u32[]{:S(2)}, u32[]{:S(2)}) collective-permute-start(bf16[128,2048]{1,0:T(8,128)(2,1)S(1)} %copy-done), channel_id=1, source_target_pairs={{0,16},{16,0},{1,17},{17,1},{2,18},{18,2},{3,19},{19,3},{4,20},{20... | collective-permute-start | bytes 1572872 | tf_op jit(solution)/shard_map/ppermute | solution.py:12
  18.0 12.2 %collective-permute-start.13 = (bf16[64,2048]{1,0:T(8,128)(2,1)S(1)}, bf16[64,2048]{1,0:T(8,128)(2,1)S(1)}, u32[]{:S(2)}, u32[]{:S(2)}) collective-permute-start(bf16[64,2048]{1,0:T(8,128)(2,1)S(1)} %slice.101), channel_id=1, source_target_pairs={{0,4},{4,8},{8,12},{12,0},{1,5},{5,9},{9,13},{13,1},{2,6},{6,10},{... | collective-permute-start | bytes 786440 | tf_op jit(solution)/shard_map/ppermute | solution.py:12
  18.4 14.8 %collective-permute-start.15 = (bf16[64,2048]{1,0:T(8,128)(2,1)S(1)}, bf16[64,2048]{1,0:T(8,128)(2,1)S(1)}, u32[]{:S(2)}, u32[]{:S(2)}) collective-permute-start(bf16[64,2048]{1,0:T(8,128)(2,1)S(1)} %slice.102), channel_id=1, source_target_pairs={{0,12},{4,0},{8,4},{12,8},{1,13},{5,1},{9,5},{13,9},{2,14},{6,2},{... | collective-permute-start | bytes 786440 | tf_op jit(solution)/shard_map/ppermute | solution.py:12
  24.1 10.6 %collective-permute-start.4 = (bf16[48,4096]{1,0:T(8,128)(2,1)S(1)}, bf16[48,4096]{1,0:T(8,128)(2,1)S(1)}, u32[]{:S(2)}, u32[]{:S(2)}) collective-permute-start(bf16[48,4096]{1,0:T(8,128)(2,1)S(1)} %collective-permute-done.2), channel_id=1, source_target_pairs={{0,32},{32,64},{64,96},{96,128},{128,160},{160,192},{192,224},{224... | collective-permute-start | bytes 1179656 | tf_op jit(solution)/shard_map/ppermute | solution.py:12
  24.1 10.7 %collective-permute-start.5 = (bf16[48,4096]{1,0:T(8,128)(2,1)S(1)}, bf16[48,4096]{1,0:T(8,128)(2,1)S(1)}, u32[]{:S(2)}, u32[]{:S(2)}) collective-permute-start(bf16[48,4096]{1,0:T(8,128)(2,1)S(1)} %collective-permute-done.3), channel_id=1, source_target_pairs={{0,224},{32,0},{64,32},{96,64},{128,96},{160,128},{192,160},{224,1... | collective-permute-start | bytes 1179656 | tf_op jit(solution)/shard_map/ppermute | solution.py:12
  30.0 12.5 %collective-permute-start.11 = (bf16[128,2048]{1,0:T(8,128)(2,1)S(1)}, bf16[128,2048]{1,0:T(8,128)(2,1)S(1)}, u32[]{:S(2)}, u32[]{:S(2)}) collective-permute-start(bf16[128,2048]{1,0:T(8,128)(2,1)S(1)} %collective-permute-done.10), channel_id=1, source_target_pairs={{0,4},{4,8},{8,12},{12,0},{1,5},{5,9},{9,13},{13,1},{2,6},{6,10},{... | collective-permute-start | bytes 1572872 | tf_op jit(solution)/shard_map/ppermute | solution.py:12
  30.3 12.3 %collective-permute-start.17 = (bf16[128,2048]{1,0:T(8,128)(2,1)S(1)}, bf16[128,2048]{1,0:T(8,128)(2,1)S(1)}, u32[]{:S(2)}, u32[]{:S(2)}) collective-permute-start(bf16[128,2048]{1,0:T(8,128)(2,1)S(1)} %collective-permute-done.10), channel_id=1, source_target_pairs={{0,12},{4,0},{8,4},{12,8},{1,13},{5,1},{9,5},{13,9},{2,14},{6,2},{... | collective-permute-start | bytes 1572872 | tf_op jit(solution)/shard_map/ppermute | solution.py:12
  33.3 12.4 %collective-permute-start.16 = (bf16[128,2048]{1,0:T(8,128)(2,1)S(1)}, bf16[128,2048]{1,0:T(8,128)(2,1)S(1)}, u32[]{:S(2)}, u32[]{:S(2)}) collective-permute-start(bf16[128,2048]{1,0:T(8,128)(2,1)S(1)} %pad_maximum_fusion.1), channel_id=1, source_target_pairs={{0,16},{16,0},{1,17},{17,1},{2,18},{18,2},{3,19},{19,3},{4,20},{20... | collective-permute-start | bytes 1572872 | tf_op jit(solution)/shard_map/ppermute | solution.py:12
  34.7 11.0 %collective-permute-start.6 = (bf16[48,4096]{1,0:T(8,128)(2,1)S(1)}, bf16[48,4096]{1,0:T(8,128)(2,1)S(1)}, u32[]{:S(2)}, u32[]{:S(2)}) collective-permute-start(bf16[48,4096]{1,0:T(8,128)(2,1)S(1)} %collective-permute-done.4), channel_id=1, source_target_pairs={{0,32},{32,64},{64,96},{96,128},{128,160},{160,192},{192,224},{224... | collective-permute-start | bytes 1179656 | tf_op jit(solution)/shard_map/ppermute | solution.py:12
  34.8 11.0 %collective-permute-start.7 = (bf16[48,4096]{1,0:T(8,128)(2,1)S(1)}, bf16[48,4096]{1,0:T(8,128)(2,1)S(1)}, u32[]{:S(2)}, u32[]{:S(2)}) collective-permute-start(bf16[48,4096]{1,0:T(8,128)(2,1)S(1)} %collective-permute-done.5), channel_id=1, source_target_pairs={{0,224},{32,0},{64,32},{96,64},{128,96},{160,128},{192,160},{224,1... | collective-permute-start | bytes 1179656 | tf_op jit(solution)/shard_map/ppermute | solution.py:12
  42.5 17.2 %collective-permute-start.20 = (bf16[512,2048]{1,0:T(8,128)(2,1)S(1)}, bf16[512,2048]{1,0:T(8,128)(2,1)S(1)}, u32[]{:S(2)}, u32[]{:S(2)}) collective-permute-start(bf16[512,2048]{1,0:T(8,128)(2,1)S(1)} %constant_dynamic-update-slice_fusion), channel_id=1, source_target_pairs={{0,1},{1,0},{2,3},{3,2},{4,5},{5,4},{6,7},{7,6},{8,9},{9,8},{10,11... | collective-permute-start | bytes 6291464 | tf_op jit(solution)/shard_map/ppermute | solution.py:12
  42.6 11.8 %collective-permute-start.18 = (bf16[384,2048]{1,0:T(8,128)(2,1)S(1)}, bf16[384,2048]{1,0:T(8,128)(2,1)S(1)}, u32[]{:S(2)}, u32[]{:S(2)}) collective-permute-start(bf16[384,2048]{1,0:T(8,128)(2,1)S(1)} %pad_maximum_fusion), channel_id=1, source_target_pairs={{0,1},{1,0},{2,3},{3,2},{4,5},{5,4},{6,7},{7,6},{8,9},{9,8},{10,11... | collective-permute-start | bytes 4718600 | tf_op jit(solution)/shard_map/ppermute | solution.py:12
  45.6 9.0 %collective-permute-start.19 = (bf16[128,2048]{1,0:T(8,128)(2,1)S(1)}, bf16[128,2048]{1,0:T(8,128)(2,1)S(1)}, u32[]{:S(2)}, u32[]{:S(2)}) collective-permute-start(bf16[128,2048]{1,0:T(8,128)(2,1)S(1)} %collective-permute-done.16), channel_id=1, source_target_pairs={{0,1},{1,0},{2,3},{3,2},{4,5},{5,4},{6,7},{7,6},{8,9},{9,8},{10,11... | collective-permute-start | bytes 1572872 | tf_op jit(solution)/shard_map/ppermute | solution.py:12
  45.7 8.6 %collective-permute-start.8 = (bf16[24,4096]{1,0:T(8,128)(2,1)S(1)}, bf16[24,4096]{1,0:T(8,128)(2,1)S(1)}, u32[]{:S(2)}, u32[]{:S(2)}) collective-permute-start(bf16[24,4096]{1,0:T(8,128)(2,1)S(1)} %slice.98), channel_id=1, source_target_pairs={{0,32},{32,64},{64,96},{96,128},{128,160},{160,192},{192,224},{224... | collective-permute-start | bytes 589832 | tf_op jit(solution)/shard_map/ppermute | solution.py:12
  45.8 8.5 %collective-permute-start.9 = (bf16[24,4096]{1,0:T(8,128)(2,1)S(1)}, bf16[24,4096]{1,0:T(8,128)(2,1)S(1)}, u32[]{:S(2)}, u32[]{:S(2)}) collective-permute-start(bf16[24,4096]{1,0:T(8,128)(2,1)S(1)} %slice.99), channel_id=1, source_target_pairs={{0,224},{32,0},{64,32},{96,64},{128,96},{160,128},{192,160},{224,1... | collective-permute-start | bytes 589832 | tf_op jit(solution)/shard_map/ppermute | solution.py:12
  56.8 12.4 %collective-permute-start.23 = (s16[200,512]{1,0:T(8,128)(2,1)S(1)}, s16[200,512]{1,0:T(8,128)(2,1)S(1)}, u32[]{:S(2)}, u32[]{:S(2)}) collective-permute-start(s16[200,512]{1,0:T(8,128)(2,1)S(1)} %pad_add_fusion), channel_id=1, source_target_pairs={{0,18},{2,16},{16,2},{18,0},{1,19},{3,17},{17,3},{19,1},{4,22},{6,... | collective-permute-start | bytes 614408 | tf_op jit(solution)/shard_map/ppermute | solution.py:104
  57.1 9.2 %collective-permute-start.22 = (s16[200,512]{1,0:T(8,128)(2,1)S(1)}, s16[200,512]{1,0:T(8,128)(2,1)S(1)}, u32[]{:S(2)}, u32[]{:S(2)}) collective-permute-start(s16[200,512]{1,0:T(8,128)(2,1)S(1)} %pad_add_fusion.2), channel_id=1, source_target_pairs={{0,16},{16,0},{1,17},{17,1},{2,18},{18,2},{3,19},{19,3},{4,20},{20... | collective-permute-start | bytes 614408 | tf_op jit(solution)/shard_map/ppermute | solution.py:12
  62.0 8.1 %collective-permute-start.21 = (s16[200,512]{1,0:T(8,128)(2,1)S(1)}, s16[200,512]{1,0:T(8,128)(2,1)S(1)}, u32[]{:S(2)}, u32[]{:S(2)}) collective-permute-start(s16[200,512]{1,0:T(8,128)(2,1)S(1)} %pad_add_fusion.1), channel_id=1, source_target_pairs={{0,2},{2,0},{1,3},{3,1},{4,6},{6,4},{5,7},{7,5},{8,10},{10,8},{9,1... | collective-permute-start | bytes 614408 | tf_op jit(solution)/shard_map/ppermute | solution.py:12
  70.5 7.1 %collective-permute-start.25 = (bf16[2,192,128]{2,1,0:T(8,128)(2,1)S(1)}, bf16[2,192,128]{2,1,0:T(8,128)(2,1)S(1)}, u32[]{:S(2)}, u32[]{:S(2)}) collective-permute-start(bf16[2,192,128]{2,1,0:T(8,128)(2,1)S(1)} %get-tuple-element.25), channel_id=1, source_target_pairs={{0,8},{4,12},{8,0},{12,4},{1,9},{5,13},{9,1},{13,5},{2,10},{6,14},... | collective-permute-start | bytes 294920 | tf_op jit(solution)/shard_map/ppermute | solution.py:12
  (7 other events, 61.6 us)

commit v8 on v7

--- a/solution.py
+++ b/solution.py
@@ -43,18 +43,22 @@
         up.append(shift(up[-1], "z", 1))
         down.append(shift(down[-1], "z", -1))
     opposite = [shift(up[-1][:rows], "z", 1), shift(down[-1][rows:], "z", -1)]
-    opposite = lax.optimization_barrier(opposite)
     lines = jnp.zeros((8, 2 * rows, 2 * width), amplitudes.dtype)
-    blocks = [slabs, up[1], down[1], up[2], down[2], up[3], down[3], jnp.concatenate(opposite, axis=0)]
+    blocks = [slabs, up[1], down[1], up[2], down[2], up[3], down[3]]
     start = l * 2 * width
     cd_labels = [lax.dynamic_slice_in_dim(cd_symmetry, start + i * width, width) for i in (k, 1 - k)]
     cd_labels = jnp.concatenate(cd_labels)
     labels = lax.dynamic_index_in_dim(ij_symmetry.reshape(8, 8, rows), at["h"] * 4 + at["x"], 1, keepdims=False)
     labels = jnp.concatenate([labels, shift(labels, "l", 1)], axis=1)
-    for step, block in zip((0, -1, 1, -2, 2, -3, 3, 4), blocks):
+    def place(lines, step, block, first):
         label = lax.dynamic_index_in_dim(labels, (at["z"] + step) % 8, 0, keepdims=False)
+        label = label[first : first + block.shape[0]]
         block = jnp.where(label[:, None] == cd_labels[None, :], block, jnp.zeros_like(block))
-        lines = lax.dynamic_update_index_in_dim(lines, block, (at["z"] + step) % 8, 0)
+        return lax.dynamic_update_slice(lines, block[None], ((at["z"] + step) % 8, first, 0))
+
+    for step, block in zip((0, -1, 1, -2, 2, -3, 3), blocks):
+        lines = place(lines, step, block, 0)
+    lines = place(place(lines, 4, opposite[0], 0), 4, opposite[1], rows)
     lines = lines.reshape(16 * rows, 2 * width)
 
     masked = integrals

time: 80 us -> 80.1 us (level)
  no operation moved by 1% of the time
where the time goes in v8:
time: 80.1 us; the launch traced here: 79.8 us
  starting transfers between devices  37.6 us (47%)
  waiting for transfers between devices  28.4 us (35%)
  local copies, waits for them, and re-layouts  5.38 us (7%)
  matrix products  4.04 us (5%)
  other arithmetic  3.89 us (5%)
    ppermute x26, starting transfers between devices, shift(): lax.ppermute(value, axis, [(i, (i + step) % size) for i in range(size)])  37.5 us
    ppermute x26, waiting for transfers between devices, shift(): lax.ppermute(value, axis, [(i, (i + step) % size) for i in range(size)])  25.5 us
    dot_general x4, matrix products, product(): lax.dot_general(line, block, (((1,), (1,)), ((), ())), preferred_element_...  4.04 us
    ppermute x1, waiting for transfers between devices, local(): got_hl = lax.ppermute(to_hl, ('h', 'l'), [(0, 3), (1, 2), (2, 1), (3, 0)])  2.91 us
    unnamed x12, local copies, waits for them, and re-layouts  1.99 us
  transfers between devices with their start and end apart: 27, of which 11 were waited for; matrix products, arithmetic and copies ran while one was open for 13% of the time, Pallas kernels for 0%

profile of v8, /device:TPU:24, one launch (start us, length us, event | category | flops | bytes accessed | tf_op | source)
XLA Modules:
  0.0 79.8 jit_solution(11974694287411583530)
XLA Ops:
  2.0 1.5 %collective-permute-start.12 = (bf16[128,2048]{1,0:T(8,128)(2,1)}, bf16[128,2048]{1,0:T(8,128)(2,1)S(1)}, u32[]{:S(2)}, u32[]{:S(2)}) collective-permute-start(bf16[128,2048]{1,0:T(8,128)(2,1)} %param.6), channel_id=1, source_target_pairs={{0,4},{4,8},{8,12},{12,0},{1,5},{5,9},{9,13},{13,1},{2,6},{6,10},{... | collective-permute-start | bytes 1572872 | tf_op jit(solution)/shard_map/ppermute | solution.py:12
  3.5 1.7 %collective-permute-start.14 = (bf16[128,2048]{1,0:T(8,128)(2,1)}, bf16[128,2048]{1,0:T(8,128)(2,1)S(1)}, u32[]{:S(2)}, u32[]{:S(2)}) collective-permute-start(bf16[128,2048]{1,0:T(8,128)(2,1)} %param.6), channel_id=1, source_target_pairs={{0,12},{4,0},{8,4},{12,8},{1,13},{5,1},{9,5},{13,9},{2,14},{6,2},{... | collective-permute-start | bytes 1572872 | tf_op jit(solution)/shard_map/ppermute | solution.py:12
  6.0 1.4 %collective-permute-start = (s32[8,24]{1,0:T(8,128)S(1)}, s32[8,24]{1,0:T(8,128)S(1)}, u32[]{:S(2)}, u32[]{:S(2)}) collective-permute-start(s32[8,24]{1,0:T(8,128)S(1)} %bitcast.105), channel_id=1, source_target_pairs={{0,2},{2,0},{1,3},{3,1},{4,6},{6,4},{5,7},{7,5},{8,10},{10,8},{9,1... | collective-permute-start | bytes 2312 | tf_op jit(solution)/shard_map/ppermute | solution.py:12
  7.4 1.9 %constant_dynamic-update-slice_fusion.4 = bf16[512,2048]{1,0:T(8,128)(2,1)} fusion(bf16[128,2048]{1,0:T(8,128)(2,1)} %param.6), kind=kLoop, calls=%fused_computation.99 | loop fusion | bytes 1048576
  10.2 2.0 %collective-permute-start.2 = (bf16[48,4096]{1,0:T(8,128)(2,1)S(1)}, bf16[48,4096]{1,0:T(8,128)(2,1)S(1)}, u32[]{:S(2)}, u32[]{:S(2)}) collective-permute-start(bf16[48,4096]{1,0:T(8,128)(2,1)S(1)} %pad_maximum_fusion.2), channel_id=1, source_target_pairs={{0,32},{32,64},{64,96},{96,128},{128,160},{160,192},{192,224},{224... | collective-permute-start | bytes 1179656 | tf_op jit(solution)/shard_map/ppermute | solution.py:12
  12.2 4.0 %collective-permute-start.3 = (bf16[48,4096]{1,0:T(8,128)(2,1)S(1)}, bf16[48,4096]{1,0:T(8,128)(2,1)S(1)}, u32[]{:S(2)}, u32[]{:S(2)}) collective-permute-start(bf16[48,4096]{1,0:T(8,128)(2,1)S(1)} %pad_maximum_fusion.2), channel_id=1, source_target_pairs={{0,224},{32,0},{64,32},{96,64},{128,96},{160,128},{192,160},{224,1... | collective-permute-start | bytes 1179656 | tf_op jit(solution)/shard_map/ppermute | solution.py:12
  16.3 1.2 %collective-permute-start.10 = (bf16[128,2048]{1,0:T(8,128)(2,1)S(1)}, bf16[128,2048]{1,0:T(8,128)(2,1)S(1)}, u32[]{:S(2)}, u32[]{:S(2)}) collective-permute-start(bf16[128,2048]{1,0:T(8,128)(2,1)S(1)} %copy-done), channel_id=1, source_target_pairs={{0,16},{16,0},{1,17},{17,1},{2,18},{18,2},{3,19},{19,3},{4,20},{20... | collective-permute-start | bytes 1572872 | tf_op jit(solution)/shard_map/ppermute | solution.py:12
  18.5 3.0 %collective-permute-start.15 = (bf16[64,2048]{1,0:T(8,128)(2,1)S(1)}, bf16[64,2048]{1,0:T(8,128)(2,1)S(1)}, u32[]{:S(2)}, u32[]{:S(2)}) collective-permute-start(bf16[64,2048]{1,0:T(8,128)(2,1)S(1)} %slice.112), channel_id=1, source_target_pairs={{0,12},{4,0},{8,4},{12,8},{1,13},{5,1},{9,5},{13,9},{2,14},{6,2},{... | collective-permute-start | bytes 786440 | tf_op jit(solution)/shard_map/ppermute | solution.py:12
  21.5 2.6 %collective-permute-done.2 = bf16[48,4096]{1,0:T(8,128)(2,1)S(1)} collective-permute-done((bf16[48,4096]{1,0:T(8,128)(2,1)S(1)}, bf16[48,4096]{1,0:T(8,128)(2,1)S(1)}, u32[]{:S(2)}, u32[]{:S(2)}) %collective-permute-start.2) | collective-permute-done | bytes 393248 | tf_op jit(solution)/shard_map/ppermute | solution.py:12
  24.2 3.2 %collective-permute-start.5 = (bf16[48,4096]{1,0:T(8,128)(2,1)S(1)}, bf16[48,4096]{1,0:T(8,128)(2,1)S(1)}, u32[]{:S(2)}, u32[]{:S(2)}) collective-permute-start(bf16[48,4096]{1,0:T(8,128)(2,1)S(1)} %collective-permute-done.3), channel_id=1, source_target_pairs={{0,224},{32,0},{64,32},{96,64},{128,96},{160,128},{192,160},{224,1... | collective-permute-start | bytes 1179656 | tf_op jit(solution)/shard_map/ppermute | solution.py:12
  27.7 2.3 %collective-permute-done.10 = bf16[128,2048]{1,0:T(8,128)(2,1)S(1)} collective-permute-done((bf16[128,2048]{1,0:T(8,128)(2,1)S(1)}, bf16[128,2048]{1,0:T(8,128)(2,1)S(1)}, u32[]{:S(2)}, u32[]{:S(2)}) %collective-permute-start.10) | collective-permute-done | bytes 524320 | tf_op jit(solution)/shard_map/ppermute | solution.py:12
  30.3 3.0 %collective-permute-start.17 = (bf16[128,2048]{1,0:T(8,128)(2,1)S(1)}, bf16[128,2048]{1,0:T(8,128)(2,1)S(1)}, u32[]{:S(2)}, u32[]{:S(2)}) collective-permute-start(bf16[128,2048]{1,0:T(8,128)(2,1)S(1)} %collective-permute-done.10), channel_id=1, source_target_pairs={{0,12},{4,0},{8,4},{12,8},{1,13},{5,1},{9,5},{13,9},{2,14},{6,2},{... | collective-permute-start | bytes 1572872 | tf_op jit(solution)/shard_map/ppermute | solution.py:12
  33.3 1.3 %collective-permute-start.16 = (bf16[128,2048]{1,0:T(8,128)(2,1)S(1)}, bf16[128,2048]{1,0:T(8,128)(2,1)S(1)}, u32[]{:S(2)}, u32[]{:S(2)}) collective-permute-start(bf16[128,2048]{1,0:T(8,128)(2,1)S(1)} %pad_maximum_fusion.1), channel_id=1, source_target_pairs={{0,16},{16,0},{1,17},{17,1},{2,18},{18,2},{3,19},{19,3},{4,20},{20... | collective-permute-start | bytes 1572872 | tf_op jit(solution)/shard_map/ppermute | solution.py:12
  34.8 3.2 %collective-permute-start.7 = (bf16[48,4096]{1,0:T(8,128)(2,1)S(1)}, bf16[48,4096]{1,0:T(8,128)(2,1)S(1)}, u32[]{:S(2)}, u32[]{:S(2)}) collective-permute-start(bf16[48,4096]{1,0:T(8,128)(2,1)S(1)} %collective-permute-done.5), channel_id=1, source_target_pairs={{0,224},{32,0},{64,32},{96,64},{128,96},{160,128},{192,160},{224,1... | collective-permute-start | bytes 1179656 | tf_op jit(solution)/shard_map/ppermute | solution.py:12
  38.4 4.2 %collective-permute-done.11 = bf16[128,2048]{1,0:T(8,128)(2,1)S(1)} collective-permute-done((bf16[128,2048]{1,0:T(8,128)(2,1)S(1)}, bf16[128,2048]{1,0:T(8,128)(2,1)S(1)}, u32[]{:S(2)}, u32[]{:S(2)}) %collective-permute-start.11) | collective-permute-done | bytes 524320 | tf_op jit(solution)/shard_map/ppermute | solution.py:12
  43.3 2.4 %collective-permute-done.16 = bf16[128,2048]{1,0:T(8,128)(2,1)S(1)} collective-permute-done((bf16[128,2048]{1,0:T(8,128)(2,1)S(1)}, bf16[128,2048]{1,0:T(8,128)(2,1)S(1)}, u32[]{:S(2)}, u32[]{:S(2)}) %collective-permute-start.16) | collective-permute-done | bytes 524320 | tf_op jit(solution)/shard_map/ppermute | solution.py:12
  45.8 3.3 %collective-permute-start.9 = (bf16[24,4096]{1,0:T(8,128)(2,1)S(1)}, bf16[24,4096]{1,0:T(8,128)(2,1)S(1)}, u32[]{:S(2)}, u32[]{:S(2)}) collective-permute-start(bf16[24,4096]{1,0:T(8,128)(2,1)S(1)} %slice.109), channel_id=1, source_target_pairs={{0,224},{32,0},{64,32},{96,64},{128,96},{160,128},{192,160},{224,1... | collective-permute-start | bytes 589832 | tf_op jit(solution)/shard_map/ppermute | solution.py:12
  49.5 4.9 %collective-permute-done.8 = bf16[24,4096]{1,0:T(8,128)(2,1)S(1)} collective-permute-done((bf16[24,4096]{1,0:T(8,128)(2,1)S(1)}, bf16[24,4096]{1,0:T(8,128)(2,1)S(1)}, u32[]{:S(2)}, u32[]{:S(2)}) %collective-permute-start.8) | collective-permute-done | bytes 196640 | tf_op jit(solution)/shard_map/ppermute | solution.py:12
  57.2 2.7 %collective-permute-start.22 = (s16[200,512]{1,0:T(8,128)(2,1)S(1)}, s16[200,512]{1,0:T(8,128)(2,1)S(1)}, u32[]{:S(2)}, u32[]{:S(2)}) collective-permute-start(s16[200,512]{1,0:T(8,128)(2,1)S(1)} %pad_add_fusion.2), channel_id=1, source_target_pairs={{0,16},{16,0},{1,17},{17,1},{2,18},{18,2},{3,19},{19,3},{4,20},{20... | collective-permute-start | bytes 614408 | tf_op jit(solution)/shard_map/ppermute | solution.py:12
  62.1 1.6 %collective-permute-start.21 = (s16[200,512]{1,0:T(8,128)(2,1)S(1)}, s16[200,512]{1,0:T(8,128)(2,1)S(1)}, u32[]{:S(2)}, u32[]{:S(2)}) collective-permute-start(s16[200,512]{1,0:T(8,128)(2,1)S(1)} %pad_add_fusion.1), channel_id=1, source_target_pairs={{0,2},{2,0},{1,3},{3,1},{4,6},{6,4},{5,7},{7,5},{8,10},{10,8},{9,1... | collective-permute-start | bytes 614408 | tf_op jit(solution)/shard_map/ppermute | solution.py:12
  63.7 2.7 %collective-permute-done.22 = s16[200,512]{1,0:T(8,128)(2,1)S(1)} collective-permute-done((s16[200,512]{1,0:T(8,128)(2,1)S(1)}, s16[200,512]{1,0:T(8,128)(2,1)S(1)}, u32[]{:S(2)}, u32[]{:S(2)}) %collective-permute-start.22) | collective-permute-done | bytes 204832 | tf_op jit(solution)/shard_map/ppermute | solution.py:12
  66.5 2.9 %collective-permute-done.23 = s16[200,512]{1,0:T(8,128)(2,1)S(1)} collective-permute-done((s16[200,512]{1,0:T(8,128)(2,1)S(1)}, s16[200,512]{1,0:T(8,128)(2,1)S(1)}, u32[]{:S(2)}, u32[]{:S(2)}) %collective-permute-start.23) | collective-permute-done | bytes 204832 | tf_op jit(solution)/shard_map/ppermute | solution.py:108
  72.6 2.6 %collective-permute-done.24 = bf16[2,192,128]{2,1,0:T(8,128)(2,1)S(1)} collective-permute-done((bf16[2,192,128]{2,1,0:T(8,128)(2,1)S(1)}, bf16[2,192,128]{2,1,0:T(8,128)(2,1)S(1)}, u32[]{:S(2)}, u32[]{:S(2)}) %collective-permute-start.24) | collective-permute-done | bytes 98336 | tf_op jit(solution)/shard_map/ppermute | solution.py:12
  75.2 2.6 %collective-permute-done.25 = bf16[2,192,128]{2,1,0:T(8,128)(2,1)S(1)} collective-permute-done((bf16[2,192,128]{2,1,0:T(8,128)(2,1)S(1)}, bf16[2,192,128]{2,1,0:T(8,128)(2,1)S(1)}, u32[]{:S(2)}, u32[]{:S(2)}) %collective-permute-start.25) | collective-permute-done | bytes 98336 | tf_op jit(solution)/shard_map/ppermute | solution.py:12
  (104 shorter events, 17.1 us)
Async XLA Ops:
  1.1 9.1 %collective-permute-start.1 = (bf16[24,4096]{1,0:T(8,128)(2,1)S(1)}, bf16[24,4096]{1,0:T(8,128)(2,1)S(1)}, u32[]{:S(2)}, u32[]{:S(2)}) collective-permute-start(bf16[24,4096]{1,0:T(8,128)(2,1)S(1)} %pad_maximum_fusion.3), channel_id=1, source_target_pairs={{0,2},{2,0},{1,3},{3,1},{4,6},{6,4},{5,7},{7,5},{8,10},{10,8},{9,1... | collective-permute-start | bytes 589832 | tf_op jit(solution)/shard_map/ppermute | solution.py:12
  2.0 16.1 %collective-permute-start.12 = (bf16[128,2048]{1,0:T(8,128)(2,1)}, bf16[128,2048]{1,0:T(8,128)(2,1)S(1)}, u32[]{:S(2)}, u32[]{:S(2)}) collective-permute-start(bf16[128,2048]{1,0:T(8,128)(2,1)} %param.6), channel_id=1, source_target_pairs={{0,4},{4,8},{8,12},{12,0},{1,5},{5,9},{9,13},{13,1},{2,6},{6,10},{... | collective-permute-start | bytes 1572872 | tf_op jit(solution)/shard_map/ppermute | solution.py:12
  3.5 15.0 %collective-permute-start.14 = (bf16[128,2048]{1,0:T(8,128)(2,1)}, bf16[128,2048]{1,0:T(8,128)(2,1)S(1)}, u32[]{:S(2)}, u32[]{:S(2)}) collective-permute-start(bf16[128,2048]{1,0:T(8,128)(2,1)} %param.6), channel_id=1, source_target_pairs={{0,12},{4,0},{8,4},{12,8},{1,13},{5,1},{9,5},{13,9},{2,14},{6,2},{... | collective-permute-start | bytes 1572872 | tf_op jit(solution)/shard_map/ppermute | solution.py:12
  10.2 13.9 %collective-permute-start.2 = (bf16[48,4096]{1,0:T(8,128)(2,1)S(1)}, bf16[48,4096]{1,0:T(8,128)(2,1)S(1)}, u32[]{:S(2)}, u32[]{:S(2)}) collective-permute-start(bf16[48,4096]{1,0:T(8,128)(2,1)S(1)} %pad_maximum_fusion.2), channel_id=1, source_target_pairs={{0,32},{32,64},{64,96},{96,128},{128,160},{160,192},{192,224},{224... | collective-permute-start | bytes 1179656 | tf_op jit(solution)/shard_map/ppermute | solution.py:12
  12.2 11.9 %collective-permute-start.3 = (bf16[48,4096]{1,0:T(8,128)(2,1)S(1)}, bf16[48,4096]{1,0:T(8,128)(2,1)S(1)}, u32[]{:S(2)}, u32[]{:S(2)}) collective-permute-start(bf16[48,4096]{1,0:T(8,128)(2,1)S(1)} %pad_maximum_fusion.2), channel_id=1, source_target_pairs={{0,224},{32,0},{64,32},{96,64},{128,96},{160,128},{192,160},{224,1... | collective-permute-start | bytes 1179656 | tf_op jit(solution)/shard_map/ppermute | solution.py:12
  16.3 13.8 %collective-permute-start.10 = (bf16[128,2048]{1,0:T(8,128)(2,1)S(1)}, bf16[128,2048]{1,0:T(8,128)(2,1)S(1)}, u32[]{:S(2)}, u32[]{:S(2)}) collective-permute-start(bf16[128,2048]{1,0:T(8,128)(2,1)S(1)} %copy-done), channel_id=1, source_target_pairs={{0,16},{16,0},{1,17},{17,1},{2,18},{18,2},{3,19},{19,3},{4,20},{20... | collective-permute-start | bytes 1572872 | tf_op jit(solution)/shard_map/ppermute | solution.py:12
  18.1 12.2 %collective-permute-start.13 = (bf16[64,2048]{1,0:T(8,128)(2,1)S(1)}, bf16[64,2048]{1,0:T(8,128)(2,1)S(1)}, u32[]{:S(2)}, u32[]{:S(2)}) collective-permute-start(bf16[64,2048]{1,0:T(8,128)(2,1)S(1)} %slice.111), channel_id=1, source_target_pairs={{0,4},{4,8},{8,12},{12,0},{1,5},{5,9},{9,13},{13,1},{2,6},{6,10},{... | collective-permute-start | bytes 786440 | tf_op jit(solution)/shard_map/ppermute | solution.py:12
  18.5 14.8 %collective-permute-start.15 = (bf16[64,2048]{1,0:T(8,128)(2,1)S(1)}, bf16[64,2048]{1,0:T(8,128)(2,1)S(1)}, u32[]{:S(2)}, u32[]{:S(2)}) collective-permute-start(bf16[64,2048]{1,0:T(8,128)(2,1)S(1)} %slice.112), channel_id=1, source_target_pairs={{0,12},{4,0},{8,4},{12,8},{1,13},{5,1},{9,5},{13,9},{2,14},{6,2},{... | collective-permute-start | bytes 786440 | tf_op jit(solution)/shard_map/ppermute | solution.py:12
  24.2 10.6 %collective-permute-start.4 = (bf16[48,4096]{1,0:T(8,128)(2,1)S(1)}, bf16[48,4096]{1,0:T(8,128)(2,1)S(1)}, u32[]{:S(2)}, u32[]{:S(2)}) collective-permute-start(bf16[48,4096]{1,0:T(8,128)(2,1)S(1)} %collective-permute-done.2), channel_id=1, source_target_pairs={{0,32},{32,64},{64,96},{96,128},{128,160},{160,192},{192,224},{224... | collective-permute-start | bytes 1179656 | tf_op jit(solution)/shard_map/ppermute | solution.py:12
  24.2 10.7 %collective-permute-start.5 = (bf16[48,4096]{1,0:T(8,128)(2,1)S(1)}, bf16[48,4096]{1,0:T(8,128)(2,1)S(1)}, u32[]{:S(2)}, u32[]{:S(2)}) collective-permute-start(bf16[48,4096]{1,0:T(8,128)(2,1)S(1)} %collective-permute-done.3), channel_id=1, source_target_pairs={{0,224},{32,0},{64,32},{96,64},{128,96},{160,128},{192,160},{224,1... | collective-permute-start | bytes 1179656 | tf_op jit(solution)/shard_map/ppermute | solution.py:12
  30.0 12.5 %collective-permute-start.11 = (bf16[128,2048]{1,0:T(8,128)(2,1)S(1)}, bf16[128,2048]{1,0:T(8,128)(2,1)S(1)}, u32[]{:S(2)}, u32[]{:S(2)}) collective-permute-start(bf16[128,2048]{1,0:T(8,128)(2,1)S(1)} %collective-permute-done.10), channel_id=1, source_target_pairs={{0,4},{4,8},{8,12},{12,0},{1,5},{5,9},{9,13},{13,1},{2,6},{6,10},{... | collective-permute-start | bytes 1572872 | tf_op jit(solution)/shard_map/ppermute | solution.py:12
  30.3 12.3 %collective-permute-start.17 = (bf16[128,2048]{1,0:T(8,128)(2,1)S(1)}, bf16[128,2048]{1,0:T(8,128)(2,1)S(1)}, u32[]{:S(2)}, u32[]{:S(2)}) collective-permute-start(bf16[128,2048]{1,0:T(8,128)(2,1)S(1)} %collective-permute-done.10), channel_id=1, source_target_pairs={{0,12},{4,0},{8,4},{12,8},{1,13},{5,1},{9,5},{13,9},{2,14},{6,2},{... | collective-permute-start | bytes 1572872 | tf_op jit(solution)/shard_map/ppermute | solution.py:12
  33.3 12.4 %collective-permute-start.16 = (bf16[128,2048]{1,0:T(8,128)(2,1)S(1)}, bf16[128,2048]{1,0:T(8,128)(2,1)S(1)}, u32[]{:S(2)}, u32[]{:S(2)}) collective-permute-start(bf16[128,2048]{1,0:T(8,128)(2,1)S(1)} %pad_maximum_fusion.1), channel_id=1, source_target_pairs={{0,16},{16,0},{1,17},{17,1},{2,18},{18,2},{3,19},{19,3},{4,20},{20... | collective-permute-start | bytes 1572872 | tf_op jit(solution)/shard_map/ppermute | solution.py:12
  34.7 11.0 %collective-permute-start.6 = (bf16[48,4096]{1,0:T(8,128)(2,1)S(1)}, bf16[48,4096]{1,0:T(8,128)(2,1)S(1)}, u32[]{:S(2)}, u32[]{:S(2)}) collective-permute-start(bf16[48,4096]{1,0:T(8,128)(2,1)S(1)} %collective-permute-done.4), channel_id=1, source_target_pairs={{0,32},{32,64},{64,96},{96,128},{128,160},{160,192},{192,224},{224... | collective-permute-start | bytes 1179656 | tf_op jit(solution)/shard_map/ppermute | solution.py:12
  34.8 11.0 %collective-permute-start.7 = (bf16[48,4096]{1,0:T(8,128)(2,1)S(1)}, bf16[48,4096]{1,0:T(8,128)(2,1)S(1)}, u32[]{:S(2)}, u32[]{:S(2)}) collective-permute-start(bf16[48,4096]{1,0:T(8,128)(2,1)S(1)} %collective-permute-done.5), channel_id=1, source_target_pairs={{0,224},{32,0},{64,32},{96,64},{128,96},{160,128},{192,160},{224,1... | collective-permute-start | bytes 1179656 | tf_op jit(solution)/shard_map/ppermute | solution.py:12
  42.6 17.3 %collective-permute-start.20 = (bf16[512,2048]{1,0:T(8,128)(2,1)S(1)}, bf16[512,2048]{1,0:T(8,128)(2,1)S(1)}, u32[]{:S(2)}, u32[]{:S(2)}) collective-permute-start(bf16[512,2048]{1,0:T(8,128)(2,1)S(1)} %constant_dynamic-update-slice_fusion), channel_id=1, source_target_pairs={{0,1},{1,0},{2,3},{3,2},{4,5},{5,4},{6,7},{7,6},{8,9},{9,8},{10,11... | collective-permute-start | bytes 6291464 | tf_op jit(solution)/shard_map/ppermute | solution.py:12
  42.7 11.9 %collective-permute-start.18 = (bf16[384,2048]{1,0:T(8,128)(2,1)S(1)}, bf16[384,2048]{1,0:T(8,128)(2,1)S(1)}, u32[]{:S(2)}, u32[]{:S(2)}) collective-permute-start(bf16[384,2048]{1,0:T(8,128)(2,1)S(1)} %pad_maximum_fusion), channel_id=1, source_target_pairs={{0,1},{1,0},{2,3},{3,2},{4,5},{5,4},{6,7},{7,6},{8,9},{9,8},{10,11... | collective-permute-start | bytes 4718600 | tf_op jit(solution)/shard_map/ppermute | solution.py:12
  45.7 9.0 %collective-permute-start.19 = (bf16[128,2048]{1,0:T(8,128)(2,1)S(1)}, bf16[128,2048]{1,0:T(8,128)(2,1)S(1)}, u32[]{:S(2)}, u32[]{:S(2)}) collective-permute-start(bf16[128,2048]{1,0:T(8,128)(2,1)S(1)} %collective-permute-done.16), channel_id=1, source_target_pairs={{0,1},{1,0},{2,3},{3,2},{4,5},{5,4},{6,7},{7,6},{8,9},{9,8},{10,11... | collective-permute-start | bytes 1572872 | tf_op jit(solution)/shard_map/ppermute | solution.py:12
  45.7 8.6 %collective-permute-start.8 = (bf16[24,4096]{1,0:T(8,128)(2,1)S(1)}, bf16[24,4096]{1,0:T(8,128)(2,1)S(1)}, u32[]{:S(2)}, u32[]{:S(2)}) collective-permute-start(bf16[24,4096]{1,0:T(8,128)(2,1)S(1)} %slice.108), channel_id=1, source_target_pairs={{0,32},{32,64},{64,96},{96,128},{128,160},{160,192},{192,224},{224... | collective-permute-start | bytes 589832 | tf_op jit(solution)/shard_map/ppermute | solution.py:12
  45.8 8.6 %collective-permute-start.9 = (bf16[24,4096]{1,0:T(8,128)(2,1)S(1)}, bf16[24,4096]{1,0:T(8,128)(2,1)S(1)}, u32[]{:S(2)}, u32[]{:S(2)}) collective-permute-start(bf16[24,4096]{1,0:T(8,128)(2,1)S(1)} %slice.109), channel_id=1, source_target_pairs={{0,224},{32,0},{64,32},{96,64},{128,96},{160,128},{192,160},{224,1... | collective-permute-start | bytes 589832 | tf_op jit(solution)/shard_map/ppermute | solution.py:12
  57.0 12.4 %collective-permute-start.23 = (s16[200,512]{1,0:T(8,128)(2,1)S(1)}, s16[200,512]{1,0:T(8,128)(2,1)S(1)}, u32[]{:S(2)}, u32[]{:S(2)}) collective-permute-start(s16[200,512]{1,0:T(8,128)(2,1)S(1)} %pad_add_fusion), channel_id=1, source_target_pairs={{0,18},{2,16},{16,2},{18,0},{1,19},{3,17},{17,3},{19,1},{4,22},{6,... | collective-permute-start | bytes 614408 | tf_op jit(solution)/shard_map/ppermute | solution.py:108
  57.2 9.2 %collective-permute-start.22 = (s16[200,512]{1,0:T(8,128)(2,1)S(1)}, s16[200,512]{1,0:T(8,128)(2,1)S(1)}, u32[]{:S(2)}, u32[]{:S(2)}) collective-permute-start(s16[200,512]{1,0:T(8,128)(2,1)S(1)} %pad_add_fusion.2), channel_id=1, source_target_pairs={{0,16},{16,0},{1,17},{17,1},{2,18},{18,2},{3,19},{19,3},{4,20},{20... | collective-permute-start | bytes 614408 | tf_op jit(solution)/shard_map/ppermute | solution.py:12
  62.1 8.1 %collective-permute-start.21 = (s16[200,512]{1,0:T(8,128)(2,1)S(1)}, s16[200,512]{1,0:T(8,128)(2,1)S(1)}, u32[]{:S(2)}, u32[]{:S(2)}) collective-permute-start(s16[200,512]{1,0:T(8,128)(2,1)S(1)} %pad_add_fusion.1), channel_id=1, source_target_pairs={{0,2},{2,0},{1,3},{3,1},{4,6},{6,4},{5,7},{7,5},{8,10},{10,8},{9,1... | collective-permute-start | bytes 614408 | tf_op jit(solution)/shard_map/ppermute | solution.py:12
  70.6 7.1 %collective-permute-start.25 = (bf16[2,192,128]{2,1,0:T(8,128)(2,1)S(1)}, bf16[2,192,128]{2,1,0:T(8,128)(2,1)S(1)}, u32[]{:S(2)}, u32[]{:S(2)}) collective-permute-start(bf16[2,192,128]{2,1,0:T(8,128)(2,1)S(1)} %get-tuple-element.21), channel_id=1, source_target_pairs={{0,8},{4,12},{8,0},{12,4},{1,9},{5,13},{9,1},{13,5},{2,10},{6,14},... | collective-permute-start | bytes 294920 | tf_op jit(solution)/shard_map/ppermute | solution.py:12
  (7 other events, 61.8 us)
